TPU v7x, 32 devices: a whole 2x2x4 slice. The times are simulated.
32 devices in a mesh: dp: 4 (over y, x), seq: 8 (over z, core).
Axes of the slice: x: 2, y: 2, z: 4, core: 2. Of those that a mesh axis runs over, the one named last changes fastest.
Arguments:
- resid_in: bfloat16 [12, 2048, 1536], P('dp', 'seq'), may hold values from -6 to 6
- out_grad: bfloat16 [12, 2048, 1536], P('dp', 'seq'), may hold values from -6 to 6
- lengths: int32 [12], P('dp'), may hold values from 512 to 2048, as said below
- norm_gain: float32 [1536], replicated, may hold values from 0.25 to 1.75
- in_proj: bfloat16 [1536, 6400], P(('dp', 'seq')), may hold values from -0.15625 to 0.15625
- dt_proj: bfloat16 [1536, 48], P(('dp', 'seq')), may hold values from -0.15625 to 0.15625
- conv_weight: float32 [4, 3328], replicated, may hold values from -3 to 3
- conv_bias: float32 [3328], replicated, may hold values from -3 to 3
- dt_bias: float32 [48], replicated, may hold values from -13 to -3.6
- a_log: float32 [48], replicated, may hold values from 0 to 2.7
- skip_scale: float32 [48], replicated, may hold values from 0.5 to 1.5
- gate_gain: float32 [3072], replicated, may hold values from 0.25 to 1.75
- out_proj: bfloat16 [3072, 1536], P(('dp', 'seq')), may hold values from -0.109375 to 0.109375
Outputs:
- output: bfloat16 [12, 2048, 1536], P('dp', 'seq')
- input_grad: bfloat16 [12, 2048, 1536], P('dp', 'seq')
- grad_in_proj: float32 [1536, 6400], P(('dp', 'seq'))
- grad_dt_proj: float32 [1536, 48], P(('dp', 'seq'))
- grad_out_proj: float32 [3072, 1536], P(('dp', 'seq'))
- grad_norm_gain: float32 [1536], replicated
- grad_conv_weight: float32 [4, 3328], replicated
- grad_conv_bias: float32 [3328], replicated
- grad_dt_bias: float32 [48], replicated
- grad_a_log: float32 [48], replicated
- grad_skip: float32 [48], replicated
- grad_gate_gain: float32 [3072], replicated
Inputs may be any that keep to these rules, and one draw needn't show every extreme that they name: `lengths`: each of the groups of 3 consecutive sequences starting at a multiple of 3 holds at least one of length 2048.
All inputs are finite; a program needn't handle non-finite values.
Results may differ from a plain program's by a relative error of at most 0.012.
The roundings to bfloat16 on the way count: a program that leaves them out, or rounds other values in their place, can miss the bound.
Values may be sent and summed in bfloat16 or wider, within the bound.
A program may use at most 576 MiB of HBM per device.

v0:
```python
import jax
import jax.numpy as jnp
from jax import lax
from jax.sharding import PartitionSpec as P

MICRO = 3


epsilon = 1e-05
highest = lax.Precision.HIGHEST


def shifted(block, axis, distance):
    devices = range(lax.axis_size(axis))
    route = [(i - distance, i) for i in devices if i - distance in devices]
    return lax.ppermute(block, axis, route)


def entering(value, axis, join, neutral, backward):
    count, mine = (lax.axis_size(axis), lax.axis_index(axis))
    pieces = jax.tree.map(lambda part: lax.all_gather(part, axis), value)
    if backward:
        pieces = jax.tree.map(lambda part: part[::-1], pieces)
        mine = count - 1 - mine
    running = jax.tree.map(
        lambda part, zero: jnp.full_like(part, 0) + jnp.asarray(zero, part.dtype), value, neutral
    )

    def turn(position, running):
        longer = join(running, jax.tree.map(lambda part: part[position], pieces))
        return jax.tree.map(lambda new, old: jnp.where(position < mine, new, old), longer, running)

    return lax.fori_loop(0, count - 1, turn, running)


def rms_input(resid_rows, norm_gain):
    inv_rms = lax.rsqrt(jnp.mean(resid_rows * resid_rows, axis=-1, keepdims=True) + epsilon)
    return resid_rows * inv_rms * norm_gain


def gated_norm(ssd_rows, gate_in, gate_gain):
    gated_rows = ssd_rows * jax.nn.silu(gate_in)
    inv_rms = lax.rsqrt(jnp.mean(gated_rows * gated_rows, axis=-1, keepdims=True) + epsilon)
    return gated_rows * inv_rms * gate_gain


def conv_silu(padded, conv_weight, conv_bias):
    tap_count = conv_weight.shape[0]
    span_len = padded.shape[1] - tap_count + 1
    summed = conv_bias + conv_weight[0] * padded[:, 0:span_len]
    for offset in range(1, tap_count):
        summed = summed + conv_weight[offset] * padded[:, offset : offset + span_len]
    return jax.nn.silu(summed)


def step_sizes(dt_raw, dt_bias, a_log):
    step_size = jax.nn.softplus(dt_raw + dt_bias)
    return (step_size, jnp.cumsum(step_size * -jnp.exp(a_log), axis=1))


def ssd_state(values, dt_raw, dt_bias, a_log, in_keys):
    step_size, log_decay = step_sizes(dt_raw, dt_bias, a_log)
    log_total = log_decay[:, -1]
    weighted = values * (jnp.exp(log_total[:, None, :] - log_decay) * step_size)[..., None]
    local_state = jnp.einsum("bshp,bsn->bhpn", weighted, in_keys, precision=highest)
    return (local_state, jnp.exp(log_total))


def ssd_out(values, dt_raw, dt_bias, a_log, in_keys, out_keys, skip_scale, carried):
    step_size, log_decay = step_sizes(dt_raw, dt_bias, a_log)
    span_len = values.shape[1]
    key_scores = jnp.einsum("btn,bsn->bts", out_keys, in_keys, precision=highest)
    decay_heads = jnp.swapaxes(log_decay, 1, 2)
    causal_mask = lax.iota(jnp.int32, span_len)[:, None] >= lax.iota(jnp.int32, span_len)[None, :]
    log_gaps = jnp.where(
        causal_mask, decay_heads[:, :, :, None] - decay_heads[:, :, None, :], -jnp.inf
    )
    weights = jnp.exp(log_gaps) * jnp.swapaxes(step_size, 1, 2)[:, :, None, :] * key_scores[:, None]
    inside = jnp.einsum("bhts,bshp->bthp", weights, values, precision=highest)
    carried_part = (
        jnp.einsum("btn,bhpn->bthp", out_keys, carried, precision=highest)
        * jnp.exp(log_decay)[..., None]
    )
    return inside + carried_part + skip_scale[:, None] * values


def chain_combine(earlier, later_part):
    decay_one, state_one = earlier
    decay_two, state_two = later_part
    return (decay_one * decay_two, state_two + decay_two[:, :, None, None] * state_one)


def split_conv(conv_rows, inner_width, head_count, state_dim):
    values = conv_rows[..., :inner_width]
    values = values.reshape(values.shape[0], values.shape[1], head_count, inner_width // head_count)
    in_keys = conv_rows[..., inner_width : inner_width + state_dim]
    out_keys = conv_rows[..., inner_width + state_dim :]
    return (values, in_keys, out_keys)


def forward_block(resid_rows, full_in, full_dt, full_out, params):
    norm_gain, conv_weight, conv_bias, dt_bias, a_log, skip_scale, gate_gain = params
    inner_width = gate_gain.shape[0]
    head_count = a_log.shape[0]
    state_dim = (full_in.shape[1] - 2 * inner_width) // 2
    rim_count = conv_weight.shape[0] - 1
    resid_wide = resid_rows.astype(jnp.float32)
    normed = rms_input(resid_wide, norm_gain).astype(jnp.bfloat16)
    projected = jnp.dot(normed, full_in, preferred_element_type=jnp.float32)
    dt_raw = jnp.dot(normed, full_dt, preferred_element_type=jnp.float32)
    gate_in = projected[..., :inner_width]
    conv_in = projected[..., inner_width:]
    rim_rows = shifted(conv_in[:, conv_in.shape[1] - rim_count :], "seq", 1)
    padded = jnp.concatenate([rim_rows, conv_in], axis=1)
    conv_low = conv_silu(padded, conv_weight, conv_bias).astype(jnp.bfloat16)
    conv_rows = lax.optimization_barrier(conv_low).astype(jnp.float32)
    values, in_keys, out_keys = split_conv(conv_rows, inner_width, head_count, state_dim)
    local_state, block_decay = ssd_state(values, dt_raw, dt_bias, a_log, in_keys)
    identity = (jnp.ones_like(block_decay), jnp.zeros_like(local_state))
    _, carried = entering((block_decay, local_state), "seq", chain_combine, identity, False)
    ssd_rows = ssd_out(
        values, dt_raw, dt_bias, a_log, in_keys, out_keys, skip_scale, carried
    ).reshape(gate_in.shape)
    normed_out = gated_norm(ssd_rows, gate_in, gate_gain).astype(jnp.bfloat16)
    mixer_out = jnp.dot(normed_out, full_out, preferred_element_type=jnp.float32)
    kept_rows = (
        resid_wide,
        normed,
        gate_in,
        padded,
        conv_rows,
        dt_raw,
        block_decay,
        carried,
        ssd_rows,
        normed_out,
    )
    return (mixer_out, kept_rows)


def backward_block(kept_rows, mask_rows, grad_rows, full_in, full_dt, full_out, params):
    norm_gain, conv_weight, conv_bias, dt_bias, a_log, skip_scale, gate_gain = params
    inner_width = gate_gain.shape[0]
    head_count = a_log.shape[0]
    state_dim = (full_in.shape[1] - 2 * inner_width) // 2
    (
        resid_wide,
        normed,
        gate_in,
        padded,
        conv_rows,
        dt_raw,
        block_decay,
        carried,
        ssd_rows,
        normed_out,
    ) = kept_rows
    outer_grad = mask_rows[..., None] * grad_rows.astype(jnp.float32)
    mixer_grad = outer_grad.astype(jnp.bfloat16)
    grad_out = jnp.einsum("bsi,bsd->id", normed_out, mixer_grad, preferred_element_type=jnp.float32)
    normed_out_grad = jnp.einsum(
        "bsd,id->bsi", mixer_grad, full_out, preferred_element_type=jnp.float32
    )
    _, norm_pull = jax.vjp(gated_norm, ssd_rows, gate_in, gate_gain)
    ssd_grad, gate_grad, grad_gate = norm_pull(normed_out_grad)
    values, in_keys, out_keys = split_conv(conv_rows, inner_width, head_count, state_dim)
    _, out_pull = jax.vjp(
        ssd_out, values, dt_raw, dt_bias, a_log, in_keys, out_keys, skip_scale, carried
    )
    values_one, dt_one, bias_one, alog_one, keys_one, out_keys_grad, grad_skip, carried_grad = (
        out_pull(ssd_grad.reshape(values.shape))
    )
    identity = (jnp.ones_like(block_decay), jnp.zeros_like(carried_grad))
    _, later_grad = entering((block_decay, carried_grad), "seq", chain_combine, identity, True)
    decay_grad = jnp.sum(later_grad * carried, axis=(2, 3))
    _, state_pull = jax.vjp(ssd_state, values, dt_raw, dt_bias, a_log, in_keys)
    values_two, dt_two, bias_two, alog_two, keys_two = state_pull((later_grad, decay_grad))
    conv_grad = jnp.concatenate(
        [(values_one + values_two).reshape(gate_in.shape), keys_one + keys_two, out_keys_grad],
        axis=-1,
    )
    _, conv_pull = jax.vjp(conv_silu, padded, conv_weight, conv_bias)
    padded_grad, grad_conv_w, grad_conv_b = conv_pull(conv_grad)
    rim_count = padded_grad.shape[1] - gate_in.shape[1]
    from_next = shifted(padded_grad[:, :rim_count].astype(jnp.bfloat16), "seq", -1).astype(
        jnp.float32
    )
    conv_in_grad = padded_grad[:, rim_count:].at[:, gate_in.shape[1] - rim_count :].add(from_next)
    proj_grad = jnp.concatenate([gate_grad, conv_in_grad], axis=-1).astype(jnp.bfloat16)
    step_low = (dt_one + dt_two).astype(jnp.bfloat16)
    grad_in = jnp.einsum("bsd,bse->de", normed, proj_grad, preferred_element_type=jnp.float32)
    grad_dt = jnp.einsum("bsd,bsh->dh", normed, step_low, preferred_element_type=jnp.float32)
    normed_grad = jnp.einsum("bse,de->bsd", proj_grad, full_in, preferred_element_type=jnp.float32)
    normed_grad = normed_grad + jnp.einsum(
        "bsh,dh->bsd", step_low, full_dt, preferred_element_type=jnp.float32
    )
    _, input_pull = jax.vjp(rms_input, resid_wide, norm_gain)
    resid_grad, grad_gain = input_pull(normed_grad)
    input_grad = (outer_grad + resid_grad).astype(jnp.bfloat16)
    small_parts = (
        grad_gain,
        grad_conv_w,
        grad_conv_b,
        bias_one + bias_two,
        alog_one + alog_two,
        grad_skip,
        grad_gate,
    )
    return (input_grad, (grad_in, grad_dt, grad_out), small_parts)


def on_device(
    resid_in,
    out_grad,
    lengths,
    norm_gain,
    in_proj,
    dt_proj,
    conv_weight,
    conv_bias,
    dt_bias,
    a_log,
    skip_scale,
    gate_gain,
    out_proj,
):
    params = (norm_gain, conv_weight, conv_bias, dt_bias, a_log, skip_scale, gate_gain)
    span_len = resid_in.shape[1]
    per_micro = resid_in.shape[0] // MICRO
    positions = lax.axis_index("seq") * span_len + lax.iota(jnp.int32, span_len)
    mask_table = (positions[None, :] < lengths[:, None]).astype(jnp.float32)
    kept_full = (
        lax.all_gather(in_proj, ("dp", "seq"), axis=0, tiled=True),
        lax.all_gather(dt_proj, ("dp", "seq"), axis=0, tiled=True),
        lax.all_gather(out_proj, ("dp", "seq"), axis=0, tiled=True),
    )
    outputs = []
    input_grads = []
    for micro_step in range(MICRO):
        row_range = slice(micro_step * per_micro, (micro_step + 1) * per_micro)
        full_in, full_dt, full_out = kept_full
        resid_rows = resid_in[row_range]
        mask_rows = mask_table[row_range]
        mixer_out, kept_rows = forward_block(resid_rows, full_in, full_dt, full_out, params)
        out_rows = mask_rows[..., None] * (kept_rows[0] + mixer_out)
        outputs.append(out_rows.astype(jnp.bfloat16))
        input_grad, big_grads, small_parts = backward_block(
            kept_rows, mask_rows, out_grad[row_range], full_in, full_dt, full_out, params
        )
        input_grads.append(input_grad)
        if micro_step == 0:
            big_total = big_grads
            small_total = small_parts
        else:
            big_total = jax.tree.map(jnp.add, big_total, big_grads)
            small_total = jax.tree.map(jnp.add, small_total, small_parts)
    total_in, total_dt, total_out = big_total
    big_total = (
        lax.psum_scatter(total_in, ("dp", "seq"), scatter_dimension=0, tiled=True),
        lax.psum_scatter(total_dt, ("dp", "seq"), scatter_dimension=0, tiled=True),
        lax.psum_scatter(total_out, ("dp", "seq"), scatter_dimension=0, tiled=True),
    )
    gain_sum, convw_sum, convb_sum, bias_sum, alog_sum, skip_sum, gate_sum = small_total
    small_total = lax.psum(
        (gain_sum, convw_sum, convb_sum, bias_sum, alog_sum, skip_sum, gate_sum), ("dp", "seq")
    )
    return (
        jnp.concatenate(outputs, axis=0),
        jnp.concatenate(input_grads, axis=0),
        big_total[0],
        big_total[1],
        big_total[2],
        small_total[0],
        small_total[1],
        small_total[2],
        small_total[3],
        small_total[4],
        small_total[5],
        small_total[6],
    )


def solution(mesh):
    placed = (
        P("dp", "seq", None),
        P("dp", "seq", None),
        P("dp"),
        P(),
        P(("dp", "seq"), None),
        P(("dp", "seq"), None),
        P(),
        P(),
        P(),
        P(),
        P(),
        P(),
        P(("dp", "seq"), None),
    )
    return jax.shard_map(
        on_device,
        mesh=mesh,
        in_specs=placed,
        out_specs=(
            P("dp", "seq", None),
            P("dp", "seq", None),
            P(("dp", "seq"), None),
            P(("dp", "seq"), None),
            P(("dp", "seq"), None),
            P(),
            P(),
            P(),
            P(),
            P(),
            P(),
            P(),
        ),
        check_vma=False,
    )
```

profile of v0, /device:TPU:0, one launch (start us, length us, event | category | flops | bytes accessed | tf_op | source)
XLA Modules:
  0.0 2138.6 jit_solution(2969738654552074303)
XLA Ops:
  8.7 46.9 %all_gather.64 = bf16[1536,48]{1,0:T(8,128)(2,1)S(1)} all-gather(bf16[48,48]{1,0:T(8,128)(2,1)} %param.37), channel_id=1, replica_groups=mesh['dp'=4,'seq'=8] {'dp','seq'}, dimensions={0}, use_global_device_ids=true | all-gather | bytes 152064 | tf_op jit(solution)/shard_map/all_gather | solution.py:234
  66.8 77.3 %all-gather.15.cloned.1.call-done = bf16[1536,6400]{1,0:T(8,128)(2,1)} async-done(((bf16[48,6400]{1,0:T(8,128)(2,1)}), bf16[1536,6400]{1,0:T(8,128)(2,1)}) %all-gather.15.cloned.1.call-update) | async-done | bytes 19660816 | tf_op jit(solution)/shard_map/all_gather | solution.py:233
  329.0 15.2 all_gather.74
  396.0 23.3 %while.89 = (s32[]{:T(128)}, f32[1,48,64,128]{3,2,1,0:T(8,128)}, s32[]{:T(128)}, f32[8,1,48,64,128]{4,3,2,1,0:T(8,128)}, f32[8,1,48]{2,1,0:T(1,128)S(1)}, /*index=5*/s32[]{:T(128)}, s32[]{:T(128)}) while((s32[]{:T(128)}, f32[1,48,64,128]{3,2,1,0:T(8,128)}, s32[]{:T(128)}, f32[8,1,48,64,128]{4,3,2,1,0:T(8,128)}, ...), condition=%wide.region_16.17_spmd.clone, body=%wide.region_15.16_spmd.clone.sunk | while | flops 1572868 | bytes 4719281 | solution.py:33
  443.3 18.1 all-gather.19.cloned.1.call-done
  461.4 13.6 while.87
  475.0 102.9 %all-gather.21.cloned.1.call-done = f32[384,64,128]{2,1,0:T(8,128)} async-done(((f32[48,64,128]{2,1,0:T(8,128)}), f32[384,64,128]{2,1,0:T(8,128)}) %all-gather.21.cloned.1.call-update) | async-done | bytes 12582928 | tf_op jit(solution)/shard_map/all_gather | solution.py:21
  782.2 31.5 %fusion.37 = (f32[48,256]{1,0:T(8,128)}, f32[48,256]{1,0:T(8,128)}, f32[48,256]{1,0:T(8,128)}, f32[256,256]{1,0:T(8,128)}, f32[256,256]{1,0:T(8,128)}, /*index=5...) fusion(f32[48,256]{1,0:T(8,128)} %copy.630, ...), kind=kOutput, calls=%fused_computation.63 | convolution fusion | flops 2538295296 | bytes 32260096 | tf_op jit(solution)/shard_map/transpose(jvp(bhts,bshp->bthp))/dot_general | solution.py:79
  886.2 20.3 all-gather.25.cloned.1.call-done
  919.6 27.1 %while.92 = (s32[]{:T(128)}, f32[1,48,64,128]{3,2,1,0:T(8,128)}, s32[]{:T(128)}, f32[8,1,48,64,128]{4,3,2,1,0:T(8,128)}, f32[8,1,48]{2,1,0:T(1,128)}, /*index=5*/s32[]{:T(128)}, s32[]{:T(128)}) while((s32[]{:T(128)}, f32[1,48,64,128]{3,2,1,0:T(8,128)}, s32[]{:T(128)}, f32[8,1,48,64,128]{4,3,2,1,0:T(8,128)}, ...), condition=%wide.region_58.60_spmd.clone, body=%wide.region_57.59_spmd.clone.sunk | while | flops 1572868 | bytes 4719281 | solution.py:33
  949.6 28.4 %while.90 = (s32[]{:T(128)}, f32[1,48,64,128]{3,2,1,0:T(8,128)}, s32[]{:T(128)}, f32[8,1,48,64,128]{4,3,2,1,0:T(8,128)}, f32[8,1,48]{2,1,0:T(1,128)}, /*index=5*/s32[]{:T(128)}, s32[]{:T(128)}) while((s32[]{:T(128)}, f32[1,48,64,128]{3,2,1,0:T(8,128)}, s32[]{:T(128)}, f32[8,1,48,64,128]{4,3,2,1,0:T(8,128)}, ...), condition=%wide.region_22.24_spmd.clone, body=%wide.region_21.23_spmd.clone.sunk | while | flops 1572868 | bytes 4719281 | solution.py:33
  990.8 32.4 %all-gather.27.cloned.1.call-done = f32[384,64,128]{2,1,0:T(8,128)} async-done(((f32[48,64,128]{2,1,0:T(8,128)}), f32[384,64,128]{2,1,0:T(8,128)}) %all-gather.27.cloned.1.call-update) | async-done | bytes 12582928 | tf_op jit(solution)/shard_map/all_gather | solution.py:21
  1035.1 17.0 while.91
  1105.6 13.5 fusion.99
  1122.7 14.5 fusion.101
  1140.8 14.6 fusion.100
  1200.2 15.4 broadcast_multiply_fusion
  1317.8 20.7 add_add_fusion.1
  1338.6 17.9 fusion.123
  1356.5 17.0 fusion.124
  1373.5 40.8 %add_add_fusion = f32[1536,6400]{1,0:T(8,128)} fusion(f32[1536,6400]{1,0:T(8,128)} %fusion.124, f32[1536,6400]{1,0:T(8,128)} %fusion.123, bf16[256,3328]{1,0:T(8,128)(2,1)} %scatter-add.14, bf16[256,3072]{1,0:T(8,128)(2,1)S(1)} %copy-done.78, f32[256]{0:T(256)S(1)} %copy-done.237, f32[1536]{0:T(1024)S(1)} %copy-done.102, bf16[3,256,1536]{2,1,0:T(8,128)(2,1)} %param.32), kind=kOutput, calls=%fused_computation.18 | convolution fusion | flops 5060952064 | bytes 122035200 | tf_op jit(solution)/shard_map/bsd,bse->de/dot_general | solution.py:191
  1441.2 102.1 %reduce-scatter.6.cloned.1.call-done = f32[48,48]{1,0:T(8,128)} async-done(((f32[1536,48]{1,0:T(8,128)}), f32[48,48]{1,0:T(8,128)}) %reduce-scatter.6.cloned.1.call-update) | async-done | bytes 9232 | tf_op jit(solution)/shard_map/reduce_scatter | solution.py:260
  1543.3 212.9 %reduce-scatter.8.cloned.1.call-done = f32[96,1536]{1,0:T(8,128)} async-done(((f32[3072,1536]{1,0:T(8,128)}), f32[96,1536]{1,0:T(8,128)}) %reduce-scatter.8.cloned.1.call-update) | async-done | bytes 589840 | tf_op jit(solution)/shard_map/reduce_scatter | solution.py:261
  1756.2 366.4 %reduce-scatter.4.cloned.1.call-done = f32[48,6400]{1,0:T(8,128)} async-done(((f32[1536,6400]{1,0:T(8,128)}), f32[48,6400]{1,0:T(8,128)}) %reduce-scatter.4.cloned.1.call-update) | async-done | bytes 1228816 | tf_op jit(solution)/shard_map/reduce_scatter | solution.py:259
  (1117 shorter events, 951.3 us)
Async XLA Ops:
  7.2 136.8 %all-gather.15.cloned.1.call-start = ((), (), s32[]{:S(2)}) async-start(), calls=%async_computation.3 | async-start | bytes 20275200 | tf_op jit(solution)/shard_map/all_gather | solution.py:233
  7.9 339.0 %all-gather.17.cloned.1.call-start = ((), (), s32[]{:S(2)}) async-start(), calls=%async_computation.4 | async-start | bytes 9732096 | tf_op jit(solution)/shard_map/all_gather | solution.py:235
  8.7 387.3 %all-gather.23.cloned.1.call-start = ((), (), s32[]{:S(2)}) async-start(), calls=%async_computation.10 | async-start | bytes 14155776 | tf_op jit(solution)/shard_map/all_gather | solution.py:21
  59.0 144.7 %copy-start.234 = (f32[256]{0:T(256)}, f32[256]{0:T(256)S(1)}, u32[]{:S(2)}) copy-start(f32[256]{0:T(256)S(1)} %fusion.358) | copy-start | bytes 3076
  59.1 129.9 %copy-start.214 = (f32[256]{0:T(256)}, f32[256]{0:T(256)S(1)}, u32[]{:S(2)}) copy-start(f32[256]{0:T(256)S(1)} %fusion.360) | copy-start | bytes 3076
  59.6 194.3 %copy-start.96 = (f32[256,48]{1,0:T(8,128)}, f32[256,48]{1,0:T(8,128)S(1)}, u32[]{:S(2)}) copy-start(f32[256,48]{1,0:T(8,128)S(1)} %convolution_add_fusion.6) | copy-start | bytes 147460
  60.0 158.7 %copy-start.99 = (f32[256,48]{1,0:T(8,128)}, f32[256,48]{1,0:T(8,128)S(1)}, u32[]{:S(2)}) copy-start(f32[256,48]{1,0:T(8,128)S(1)} %convolution_add_fusion.7) | copy-start | bytes 147460
  156.5 10.2 collective-permute-start.2
  183.2 278.3 %all-gather.19.cloned.1.call-start = ((), (), s32[]{:S(2)}) async-start(), calls=%async_computation.8 | async-start | bytes 14155776 | tf_op jit(solution)/shard_map/all_gather | solution.py:21
  202.1 26.0 %collective-permute-start.1 = (f32[1,3,3328]{2,1,0:T(4,128)S(1)}, f32[1,3,3328]{2,1,0:T(4,128)S(1)}, u32[]{:S(2)}, u32[]{:S(2)}) collective-permute-start(f32[1,3,3328]{2,1,0:T(4,128)S(1)} %slice.452), channel_id=1, source_target_pairs={{0,1},{1,2},{2,3},{3,4},{4,5},{5,6},{6,7},{8,9},{9,10},{10,11},{11... | collective-permute-start | bytes 119816 | tf_op jit(solution)/shard_map/ppermute | solution.py:16
  216.2 12.6 collective-permute-start
  248.4 329.5 %all-gather.21.cloned.1.call-start = ((), (), s32[]{:S(2)}) async-start(), calls=%async_computation.9 | async-start | bytes 14155776 | tf_op jit(solution)/shard_map/all_gather | solution.py:21
  272.6 601.7 %all-gather.29.cloned.1.call-start = ((), (), s32[]{:S(2)}) async-start(), calls=%async_computation.13 | async-start | bytes 14155776 | tf_op jit(solution)/shard_map/all_gather | solution.py:21
  443.3 212.2 %copy-start.245 = (f32[256]{0:T(256)}, f32[256]{0:T(256)S(1)}, u32[]{:S(2)}) copy-start(f32[256]{0:T(256)S(1)} %fusion.363) | copy-start | bytes 3076
  613.5 244.3 %copy-start.240 = (f32[256]{0:T(256)}, f32[256]{0:T(256)S(1)}, u32[]{:S(2)}) copy-start(f32[256]{0:T(256)S(1)} %fusion.359) | copy-start | bytes 3076
  674.8 231.8 %all-gather.25.cloned.1.call-start = ((), (), s32[]{:S(2)}) async-start(), calls=%async_computation.11 | async-start | bytes 14155776 | tf_op jit(solution)/shard_map/all_gather | solution.py:21
  707.0 316.2 %all-gather.27.cloned.1.call-start = ((), (), s32[]{:S(2)}) async-start(), calls=%async_computation.12 | async-start | bytes 14155776 | tf_op jit(solution)/shard_map/all_gather | solution.py:21
  723.2 718.0 %all-reduce.30.cloned.1.call-start = ((), (), s32[]{:S(2)}) async-start(), calls=%async_computation.14 | async-start | bytes 183296 | tf_op jit(solution)/shard_map/psum | solution.py:264
  1264.4 6.5 collective-permute-start.5
  1265.7 6.1 collective-permute-start.3
  1267.0 8.9 collective-permute-start.4
  1314.6 228.7 %reduce-scatter.6.cloned.1.call-start = ((), (), s32[]{:S(2)}) async-start(), calls=%async_computation.6 | async-start | bytes 811008 | tf_op jit(solution)/shard_map/reduce_scatter | solution.py:260
  1317.7 438.5 %reduce-scatter.8.cloned.1.call-start = ((), (), s32[]{:S(2)}) async-start(), calls=%async_computation.7 | async-start | bytes 19464192 | tf_op jit(solution)/shard_map/reduce_scatter | solution.py:261
  1338.5 784.1 %reduce-scatter.4.cloned.1.call-start = ((), (), s32[]{:S(2)}) async-start(), calls=%async_computation.5 | async-start | bytes 40550400 | tf_op jit(solution)/shard_map/reduce_scatter | solution.py:259
  (303 other events, 4144.8 us)
Sparse Core Ops, SparseCore 0:
  11.1 132.9 all-gather.14
  147.0 80.2 all-gather.16
  229.0 115.9 all-gather.22
  346.5 114.9 all-gather.18
  462.9 114.9 all-gather.20
  674.9 114.9 all-gather.28
  791.6 114.9 all-gather.24
  908.2 114.9 all-gather.26
  1314.7 126.4 all-reduce.29
  1446.7 96.5 reduce-scatter.5
  1550.3 205.8 reduce-scatter.7
  1763.1 359.4 reduce-scatter.3
where the time goes:
time: 2150 us; the launch traced here: 2140 us
  waiting for transfers between devices  938 us (44%)
  matrix products  456 us (21%)
  other arithmetic  320 us (15%)
  local copies, waits for them, and re-layouts  312 us (15%)
  blocking collectives  81.8 us (4%)
    reduce_scatter x1, waiting for transfers between devices, on_device(): lax.psum_scatter(total_in, ('dp', 'seq'), scatter_dimension=0, tiled=True)  366 us
    reduce_scatter x1, waiting for transfers between devices, on_device(): lax.psum_scatter(total_out, ('dp', 'seq'), scatter_dimension=0, tiled=True)  213 us
    all_gather x6, waiting for transfers between devices, entering(): pieces = jax.tree.map(lambda part: lax.all_gather(part, axis), value)  174 us
    dot_general x9, matrix products, ssd_out(): inside = jnp.einsum('bhts,bshp->bthp', weights, values, precision=highest)  119 us
    select_n x42, other arithmetic, turn(): jnp.where(position < mine, new, old)  107 us
    reduce_scatter x1, waiting for transfers between devices, on_device(): lax.psum_scatter(total_dt, ('dp', 'seq'), scatter_dimension=0, tiled=True)  102 us
    all_gather x1, waiting for transfers between devices, on_device(): lax.all_gather(in_proj, ('dp', 'seq'), axis=0, tiled=True)  77.3 us
    dot_general x3, matrix products, backward_block(): jnp.einsum('bsd,bse->de', normed, proj_grad, preferred_element_type=jnp.f...  75.7 us
  transfers between devices with their start and end apart: 18, of which 9 were waited for; matrix products, arithmetic and copies ran while one was open for 32% of the time, Pallas kernels for 0%

commit v1 on v0

v1 whole, which is shorter than its diff:
```python
import functools

import jax
import jax.numpy as jnp
from jax import lax
from jax.experimental import pallas as pl
from jax.experimental.pallas import tpu as pltpu
from jax.sharding import PartitionSpec as P

epsilon = 1e-05
highest = lax.Precision.HIGHEST
HALO = 16
HEADS = 8
LOG2E = 1.4426950408889634
f32 = jnp.float32
bf16 = jnp.bfloat16
MESH = pl.DeviceIdType.MESH


def mm(a, b):
    return lax.dot_general(a, b, (((1,), (0,)), ((), ())), preferred_element_type=f32)


def mm_nt(a, b):
    return lax.dot_general(a, b, (((1,), (1,)), ((), ())), preferred_element_type=f32)


def mm_tn(a, b):
    return lax.dot_general(a, b, (((0,), (0,)), ((), ())), preferred_element_type=f32)


def shifted(block, axis, distance):
    devices = range(lax.axis_size(axis))
    route = [(i - distance, i) for i in devices if i - distance in devices]
    return lax.ppermute(block, axis, route)


def spread(cols, width):
    rows, heads = cols.shape
    low_half = lax.broadcasted_iota(jnp.int32, (rows, 2 * width), 1) < width
    pairs = [
        jnp.where(low_half, cols[:, i : i + 1], cols[:, i + 1 : i + 2]) for i in range(0, heads, 2)
    ]
    return jnp.concatenate(pairs, axis=1)


def gather_heads(x, width):
    rows, total = x.shape
    low_half = lax.broadcasted_iota(jnp.int32, (rows, 2 * width), 1) < width
    head_lane = lax.broadcasted_iota(jnp.int32, (rows, total // width), 1)
    out = jnp.zeros((rows, total // width), f32)
    for i in range(total // (2 * width)):
        pair = x[:, i * 2 * width : (i + 1) * 2 * width]
        one = jnp.sum(jnp.where(low_half, pair, 0.0), axis=1, keepdims=True)
        two = jnp.sum(jnp.where(low_half, 0.0, pair), axis=1, keepdims=True)
        out = jnp.where(head_lane == 2 * i, one, out)
        out = jnp.where(head_lane == 2 * i + 1, two, out)
    return out


def silu_parts(v):
    sg = 1.0 / (1.0 + jnp.exp(-v))
    return v * sg, sg


def conv_pre(a, cw, cb, span):
    first = HALO - (cw.shape[0] - 1)
    out = cb
    for k in range(cw.shape[0]):
        out = out + cw[k : k + 1] * a[first + k : first + k + span]
    return out


def params_of(limit_mb, dims=None):
    return pltpu.CompilerParams(vmem_limit_bytes=limit_mb * 1024 * 1024, dimension_semantics=dims)


def keys_kernel(span, x_ref, w_ref, cw_ref, cb_ref, rows_ref, cin_ref):
    batch = rows_ref.shape[0]
    ext = span + HALO
    acc = mm(x_ref[...], w_ref[...])
    for b in range(batch):
        a = acc[b * ext : (b + 1) * ext]
        row, _ = silu_parts(conv_pre(a, cw_ref[...], cb_ref[...], span))
        rows_ref[b] = row.astype(bf16)
        cin_ref[b] = a.astype(bf16)


def keys_forward(x2, w_conv, col_block, cw, cb, batch, span):
    width = 2 * (cw.shape[1] // 2)
    ext = span + HALO
    return pl.pallas_call(
        functools.partial(keys_kernel, span),
        grid=(1,),
        in_specs=[
            pl.BlockSpec(x2.shape, lambda i: (0, 0)),
            pl.BlockSpec((w_conv.shape[0], width), lambda i: (0, col_block)),
            pl.BlockSpec(cw.shape, lambda i: (0, 0)),
            pl.BlockSpec(cb.shape, lambda i: (0, 0)),
        ],
        out_specs=[
            pl.BlockSpec((batch, span, width), lambda i: (0, 0, 0)),
            pl.BlockSpec((batch, ext, width), lambda i: (0, 0, 0)),
        ],
        out_shape=[
            jax.ShapeDtypeStruct((batch, span, width), bf16),
            jax.ShapeDtypeStruct((batch, ext, width), bf16),
        ],
        compiler_params=params_of(40),
    )(x2, w_conv, cw, cb)


def values_kernel(span, hw, x_ref, w_ref, cw_ref, cb_ref, keys_ref, col_ref, rows_ref, cin_ref, st_ref):
    batch = rows_ref.shape[0]
    n = keys_ref.shape[2] // 2
    ext = span + HALO
    acc = mm(x_ref[...], w_ref[...])
    for b in range(batch):
        a = acc[b * ext : (b + 1) * ext]
        row, _ = silu_parts(conv_pre(a, cw_ref[...], cb_ref[...], span))
        row = row.astype(bf16)
        rows_ref[b] = row
        cin_ref[b] = a.astype(bf16)
        cols = col_ref[0, b]
        c, step = cols[:, :HEADS], cols[:, HEADS:]
        weight = jnp.exp2(c[span - 1 : span] - c) * step
        vw = (row.astype(f32) * spread(weight, hw)).astype(bf16)
        st_ref[b] = mm_tn(keys_ref[b, :, :n], vw)


def values_forward(x2, w_conv, first_block, cw, cb, keys, colpack, hw, span):
    batch = keys.shape[0]
    groups = colpack.shape[0]
    cb_w = HEADS * hw
    ext = span + HALO
    inner = groups * cb_w
    return pl.pallas_call(
        functools.partial(values_kernel, span, hw),
        grid=(groups,),
        in_specs=[
            pl.BlockSpec(x2.shape, lambda i: (0, 0)),
            pl.BlockSpec((w_conv.shape[0], cb_w), lambda i: (0, first_block + i)),
            pl.BlockSpec((cw.shape[0], cb_w), lambda i: (0, i)),
            pl.BlockSpec((1, cb_w), lambda i: (0, i)),
            pl.BlockSpec(keys.shape, lambda i: (0, 0, 0)),
            pl.BlockSpec((1,) + colpack.shape[1:], lambda i: (i, 0, 0, 0)),
        ],
        out_specs=[
            pl.BlockSpec((batch, span, cb_w), lambda i: (0, 0, i)),
            pl.BlockSpec((batch, ext, cb_w), lambda i: (0, 0, i)),
            pl.BlockSpec((batch, keys.shape[2] // 2, cb_w), lambda i: (0, 0, i)),
        ],
        out_shape=[
            jax.ShapeDtypeStruct((batch, span, inner), bf16),
            jax.ShapeDtypeStruct((batch, ext, inner), bf16),
            jax.ShapeDtypeStruct((batch, keys.shape[2] // 2, inner), f32),
        ],
        compiler_params=params_of(50),
    )(x2, w_conv, cw, cb, keys, colpack)


def chain_kernel(backward, size, local_ref, decay_ref, carried_ref, sent, landed, send_sem, recv_sem):
    me = lax.axis_index("seq")
    count = lax.axis_size("seq")
    turn = -1 if backward else 1
    has_prev = me != (count - 1 if backward else 0)
    has_next = me != (0 if backward else count - 1)
    nxt = jnp.clip(me + turn, 0, count - 1)
    prv = jnp.clip(me - turn, 0, count - 1)
    barrier = pltpu.get_barrier_semaphore()

    @pl.when(has_prev)
    def _():
        pl.semaphore_signal(barrier, inc=1, device_id={"seq": prv}, device_id_type=MESH)

    @pl.when(has_next)
    def _():
        pl.semaphore_wait(barrier, 1)

    batch, _, total = local_ref.shape
    per = total // size

    def copy_of(k):
        return pltpu.make_async_remote_copy(
            src_ref=sent.at[k],
            dst_ref=landed.at[k],
            send_sem=send_sem.at[k],
            recv_sem=recv_sem.at[k],
            device_id={"seq": nxt},
            device_id_type=MESH,
        )

    for k in range(batch * per):
        b, part = k % batch, k // batch
        cols = pl.ds(part * size, size)

        @pl.when(has_prev)
        def _():
            copy_of(k).wait_recv()
            carried_ref[b, :, cols] = landed[k].astype(f32)

        @pl.when(jnp.logical_not(has_prev))
        def _():
            carried_ref[b, :, cols] = jnp.zeros_like(carried_ref[b, :, cols])

        @pl.when(has_next)
        def _():
            out = decay_ref[b, :, cols] * carried_ref[b, :, cols] + local_ref[b, :, cols]
            sent[k] = out.astype(bf16)
            copy_of(k).start()

    @pl.when(has_next)
    def _():
        for k in range(batch * per):
            copy_of(k).wait_send()


def chain(local, decay, backward, collective_id):
    size = 512
    count = local.shape[0] * (local.shape[2] // size)
    return pl.pallas_call(
        functools.partial(chain_kernel, backward, size),
        in_specs=[pl.BlockSpec(memory_space=pltpu.VMEM)] * 2,
        out_specs=pl.BlockSpec(memory_space=pltpu.VMEM),
        out_shape=jax.ShapeDtypeStruct(local.shape, f32),
        scratch_shapes=[
            pltpu.VMEM((count, local.shape[1], size), bf16),
            pltpu.VMEM((count, local.shape[1], size), bf16),
            pltpu.SemaphoreType.DMA((count,)),
            pltpu.SemaphoreType.DMA((count,)),
        ],
        compiler_params=pltpu.CompilerParams(
            collective_id=collective_id, has_side_effects=True, vmem_limit_bytes=40 * 1024 * 1024
        ),
    )(local, decay)


def causal(span, transposed):
    one = lax.broadcasted_iota(jnp.int32, (span, span), 0)
    two = lax.broadcasted_iota(jnp.int32, (span, span), 1)
    return (one <= two) if transposed else (one >= two)


def out_kernel(
    span, hw, x_ref, w_ref, v_ref, keys_ref, col_ref, row_ref, h_ref, skip_ref, gain_ref,
    y_ref, gate_ref, no_ref, rg_ref, scores, gated, squares,
):
    g, b = pl.program_id(0), pl.program_id(1)
    groups, batch = pl.num_programs(0), pl.num_programs(1)
    n = keys_ref.shape[2] // 2
    cb_w = HEADS * hw
    k_in, k_out = keys_ref[0, :, :n], keys_ref[0, :, n:]

    @pl.when(g == 0)
    def _():
        scores[b] = jnp.where(causal(span, False), mm_nt(k_out, k_in), 0.0)
        squares[b] = jnp.zeros_like(squares[b])

    cols = col_ref[0, 0]
    c, step = cols[:, :HEADS], cols[:, HEADS:]
    v = v_ref[0].astype(f32)
    vs = (v * spread(step, hw)).astype(bf16)
    s = scores[b]
    low_half = lax.broadcasted_iota(jnp.int32, (span, 2 * hw), 1) < hw
    parts = []
    for i in range(HEADS // 2):
        pair = vs[:, i * 2 * hw : (i + 1) * 2 * hw]
        total = None
        for j in range(2):
            h = 2 * i + j
            gap = jnp.minimum(c[:, h : h + 1] - row_ref[0, 0, h : h + 1, :], 0.0)
            u = (jnp.exp2(gap) * s).astype(bf16)
            half = jnp.where(low_half if j == 0 else jnp.logical_not(low_half), pair, jnp.zeros_like(pair))
            term = mm(u, half)
            total = term if total is None else total + term
        parts.append(total)
    y = jnp.concatenate(parts, axis=1)
    y = y + mm(k_out, h_ref[0].astype(bf16)) * spread(jnp.exp2(c), hw) + skip_ref[...] * v
    y_ref[0] = y
    gate = mm(x_ref[0, HALO:], w_ref[...])
    gate_ref[0] = gate.astype(bf16)
    act, _ = silu_parts(gate)
    gr = y * act
    gated[b, g] = gr
    squares[b] += jnp.broadcast_to(jnp.sum(gr * gr, axis=1, keepdims=True), squares.shape[1:])

    @pl.when(g == groups - 1)
    def _():
        rg = lax.rsqrt(squares[b][:, :1] * (1.0 / (groups * cb_w)) + epsilon)
        rg_ref[b] = jnp.broadcast_to(rg, rg_ref.shape[1:])
        for i in range(no_ref.shape[2] // cb_w):
            part = slice(i * cb_w, (i + 1) * cb_w)
            no_ref[b, :, part] = (gated[b, i] * rg * gain_ref[:, part]).astype(bf16)


def rows_forward(x_ext, w_gate, v, keys, colpack, rowpack, carried, skip, gain, hw, span):
    batch, ext, width = x_ext.shape
    groups = colpack.shape[0]
    cb_w = HEADS * hw
    inner = groups * cb_w
    n = keys.shape[2] // 2
    return pl.pallas_call(
        functools.partial(out_kernel, span, hw),
        grid=(groups, batch),
        in_specs=[
            pl.BlockSpec((1, ext, width), lambda g, b: (b, 0, 0)),
            pl.BlockSpec((width, cb_w), lambda g, b: (0, g)),
            pl.BlockSpec((1, span, cb_w), lambda g, b: (b, 0, g)),
            pl.BlockSpec((1, span, 2 * n), lambda g, b: (b, 0, 0)),
            pl.BlockSpec((1, 1, span, 2 * HEADS), lambda g, b: (g, b, 0, 0)),
            pl.BlockSpec((1, 1, HEADS, span), lambda g, b: (g, b, 0, 0)),
            pl.BlockSpec((1, n, cb_w), lambda g, b: (b, 0, g)),
            pl.BlockSpec((1, cb_w), lambda g, b: (0, g)),
            pl.BlockSpec((1, inner), lambda g, b: (0, 0)),
        ],
        out_specs=[
            pl.BlockSpec((1, span, cb_w), lambda g, b: (b, 0, g)),
            pl.BlockSpec((1, span, cb_w), lambda g, b: (b, 0, g)),
            pl.BlockSpec((batch, span, inner), lambda g, b: (0, 0, 0)),
            pl.BlockSpec((batch, span, 8), lambda g, b: (0, 0, 0)),
        ],
        out_shape=[
            jax.ShapeDtypeStruct((batch, span, inner), f32),
            jax.ShapeDtypeStruct((batch, span, inner), bf16),
            jax.ShapeDtypeStruct((batch, span, inner), bf16),
            jax.ShapeDtypeStruct((batch, span, 8), f32),
        ],
        scratch_shapes=[
            pltpu.VMEM((batch, span, span), f32),
            pltpu.VMEM((batch, groups, span, cb_w), f32),
            pltpu.VMEM((batch, span, 128), f32),
        ],
        compiler_params=params_of(56),
    )(x_ext, w_gate, v, keys, colpack, rowpack, carried, skip, gain)


def gate_back_kernel(
    span, hw, mg_ref, w_ref, y_ref, gate_ref, norm_ref, gain_ref, v_ref, keys_ref, col_ref, row_ref,
    h_ref, skip_ref,
    dgate_ref, dv_ref, dh_ref, cols_ref, dq_ref, dk_ref, dgain_ref, dskip_ref, scores, dscores, dqacc,
):
    g, b = pl.program_id(0), pl.program_id(1)
    groups = pl.num_programs(0)
    n = keys_ref.shape[2] // 2
    k_in, k_out = keys_ref[0, :, :n], keys_ref[0, :, n:]

    @pl.when(g == 0)
    def _():
        scores[b] = jnp.where(causal(span, True), mm_nt(k_in, k_out), 0.0)
        dscores[b] = jnp.zeros_like(dscores[b])
        dqacc[b] = jnp.zeros_like(dqacc[b])

    no_grad = mm_nt(mg_ref[0], w_ref[...])
    gate = gate_ref[0].astype(f32)
    y = y_ref[0]
    rg = norm_ref[0][:, 0:1]
    mean = norm_ref[0][:, 1:2]
    act, sg = silu_parts(gate)
    gn = y * act * rg
    dgain = jnp.sum(no_grad * gn, axis=0, keepdims=True)
    dg = rg * (no_grad * gain_ref[...] - gn * mean)
    dgate_ref[0] = (dg * y * (sg * (1.0 + gate * (1.0 - sg)))).astype(bf16)
    gb = (dg * act).astype(bf16)
    gf = gb.astype(f32)

    cols = col_ref[0, 0]
    c, step = cols[:, :HEADS], cols[:, HEADS:]
    v = v_ref[0].astype(f32)
    step_wide = spread(step, hw)
    vs = (v * step_wide).astype(bf16)
    skip = skip_ref[...]
    dskip = jnp.sum(gf * v, axis=0, keepdims=True)

    @pl.when(b == 0)
    def _():
        dgain_ref[...] = dgain
        dskip_ref[...] = dskip

    @pl.when(b != 0)
    def _():
        dgain_ref[...] += dgain
        dskip_ref[...] += dskip

    s = scores[b]
    low_half = lax.broadcasted_iota(jnp.int32, (span, 2 * hw), 1) < hw
    parts = []
    ds = dscores[b]
    for i in range(HEADS // 2):
        lanes = slice(i * 2 * hw, (i + 1) * 2 * hw)
        total = None
        for j in range(2):
            h = 2 * i + j
            gap = jnp.minimum(row_ref[0, 0, h : h + 1, :] - c[:, h : h + 1], 0.0)
            decay = jnp.exp2(gap)
            u = (decay * s).astype(bf16)
            keep = low_half if j == 0 else jnp.logical_not(low_half)
            half = jnp.where(keep, gb[:, lanes], jnp.zeros_like(gb[:, lanes]))
            term = mm(u, half)
            total = term if total is None else total + term
            ds = ds + decay * mm_nt(vs[:, lanes], half)
        parts.append(total)
    dscores[b] = ds
    u_all = jnp.concatenate(parts, axis=1)
    dv_ref[0] = (u_all * step_wide + skip * gf).astype(bf16)
    rise = gather_heads(gf * (y - skip * v) - vs.astype(f32) * u_all, hw)
    direct = gather_heads(v * u_all, hw)
    cols_ref[0, 0] = jnp.concatenate([rise, direct], axis=1)
    ge = (gf * spread(jnp.exp2(c), hw)).astype(bf16)
    dh_ref[0] = mm_tn(k_out, ge)
    dqacc[b] += mm_nt(ge, h_ref[0].astype(bf16))

    @pl.when(g == groups - 1)
    def _():
        low = jnp.where(causal(span, True), dscores[b], 0.0).astype(bf16)
        dq_ref[b] = dqacc[b] + mm_tn(low, k_in)
        dk_ref[b] = mm(low, k_out)


def gate_backward(mg, w_out, y, gate, norms, gain, v, keys, colpack, rowpack, carried, skip, hw, span):
    batch, _, width = mg.shape
    groups = colpack.shape[0]
    cb_w = HEADS * hw
    inner = groups * cb_w
    n = keys.shape[2] // 2
    block = pl.BlockSpec((1, span, cb_w), lambda g, b: (b, 0, g))
    lanes = pl.BlockSpec((1, cb_w), lambda g, b: (0, g))
    return pl.pallas_call(
        functools.partial(gate_back_kernel, span, hw),
        grid=(groups, batch),
        in_specs=[
            pl.BlockSpec((1, span, width), lambda g, b: (b, 0, 0)),
            pl.BlockSpec((cb_w, width), lambda g, b: (g, 0)),
            block,
            block,
            pl.BlockSpec((1, span, 8), lambda g, b: (b, 0, 0)),
            lanes,
            block,
            pl.BlockSpec((1, span, 2 * n), lambda g, b: (b, 0, 0)),
            pl.BlockSpec((1, 1, span, 2 * HEADS), lambda g, b: (g, b, 0, 0)),
            pl.BlockSpec((1, 1, HEADS, span), lambda g, b: (g, b, 0, 0)),
            pl.BlockSpec((1, n, cb_w), lambda g, b: (b, 0, g)),
            lanes,
        ],
        out_specs=[
            block,
            block,
            pl.BlockSpec((1, n, cb_w), lambda g, b: (b, 0, g)),
            pl.BlockSpec((1, 1, span, 2 * HEADS), lambda g, b: (g, b, 0, 0)),
            pl.BlockSpec((batch, span, n), lambda g, b: (0, 0, 0)),
            pl.BlockSpec((batch, span, n), lambda g, b: (0, 0, 0)),
            lanes,
            lanes,
        ],
        out_shape=[
            jax.ShapeDtypeStruct((batch, span, inner), bf16),
            jax.ShapeDtypeStruct((batch, span, inner), bf16),
            jax.ShapeDtypeStruct((batch, n, inner), f32),
            jax.ShapeDtypeStruct((groups, batch, span, 2 * HEADS), f32),
            jax.ShapeDtypeStruct((batch, span, n), f32),
            jax.ShapeDtypeStruct((batch, span, n), f32),
            jax.ShapeDtypeStruct((1, inner), f32),
            jax.ShapeDtypeStruct((1, inner), f32),
        ],
        scratch_shapes=[
            pltpu.VMEM((batch, span, span), f32),
            pltpu.VMEM((batch, span, span), f32),
            pltpu.VMEM((batch, span, n), f32),
        ],
        compiler_params=params_of(50),
    )(mg, w_out, y, gate, norms, gain, v, keys, colpack, rowpack, carried, skip)


def conv_back(dv, a, cw, cb, span, padded, out_ref, b):
    taps = cw.shape[0]
    first = HALO - (taps - 1)
    pre = conv_pre(a, cw, cb, span)
    _, sg = silu_parts(pre)
    pg = dv * (sg * (1.0 + pre * (1.0 - sg)))
    padded[16 : 16 + span] = pg
    ext = span + HALO
    total = jnp.zeros((ext, cw.shape[1]), f32)
    for k in range(taps):
        total = total + cw[k : k + 1] * padded[taps - 1 - k : taps - 1 - k + ext]
    out_ref[b] = total.astype(bf16)
    dcw = jnp.concatenate(
        [jnp.sum(pg * a[first + k : first + k + span], axis=0, keepdims=True) for k in range(taps)], axis=0
    )
    return dcw, jnp.sum(pg, axis=0, keepdims=True)


def state_back_kernel(
    span, hw, later_ref, h_ref, keys_ref, v_ref, dv_ref, col_ref, cin_ref, cw_ref, cb_ref,
    cig_ref, cols_ref, dk_ref, dcw_ref, dcb_ref, dlast_ref, padded, dkacc,
):
    g, b = pl.program_id(0), pl.program_id(1)
    n = keys_ref.shape[2] // 2
    cols = col_ref[0, 0]
    c, step = cols[:, :HEADS], cols[:, HEADS:]
    later = later_ref[0]
    low = later.astype(bf16)
    left = spread(jnp.exp2(c[span - 1 : span] - c), hw)
    kdh = mm(keys_ref[0, :, :n], low) * left
    v = v_ref[0].astype(f32)
    step_wide = spread(step, hw)
    cols_ref[0, 0] = gather_heads(v * kdh, hw)
    dlast_ref[0] = jnp.broadcast_to(jnp.sum(later * h_ref[0], axis=0, keepdims=True), dlast_ref.shape[1:])
    vw = (v * step_wide * left).astype(bf16)
    part = mm_nt(vw, low)

    @pl.when(g == 0)
    def _():
        dkacc[b] = part

    @pl.when(g != 0)
    def _():
        dkacc[b] += part

    @pl.when(g == pl.num_programs(0) - 1)
    def _():
        dk_ref[b] = dkacc[b]

    padded[0:16] = jnp.zeros((16, padded.shape[1]), f32)
    padded[16 + span :] = jnp.zeros((padded.shape[0] - 16 - span, padded.shape[1]), f32)
    dv = dv_ref[0].astype(f32) + kdh * step_wide
    dcw, dcb = conv_back(dv, cin_ref[0].astype(f32), cw_ref[...], cb_ref[...], span, padded, cig_ref, 0)

    @pl.when(b == 0)
    def _():
        dcw_ref[...] = dcw
        dcb_ref[...] = dcb

    @pl.when(b != 0)
    def _():
        dcw_ref[...] += dcw
        dcb_ref[...] += dcb


def state_backward(later, carried, keys, v, dv, colpack, cin, cw, cb, hw, span):
    batch = v.shape[0]
    groups = colpack.shape[0]
    cb_w = HEADS * hw
    inner = groups * cb_w
    n = keys.shape[2] // 2
    ext = span + HALO
    taps = cw.shape[0]
    block = pl.BlockSpec((1, span, cb_w), lambda g, b: (b, 0, g))
    state = pl.BlockSpec((1, n, cb_w), lambda g, b: (b, 0, g))
    return pl.pallas_call(
        functools.partial(state_back_kernel, span, hw),
        grid=(groups, batch),
        in_specs=[
            state,
            state,
            pl.BlockSpec((1, span, 2 * n), lambda g, b: (b, 0, 0)),
            block,
            block,
            pl.BlockSpec((1, 1, span, 2 * HEADS), lambda g, b: (g, b, 0, 0)),
            pl.BlockSpec((1, ext, cb_w), lambda g, b: (b, 0, g)),
            pl.BlockSpec((taps, cb_w), lambda g, b: (0, g)),
            pl.BlockSpec((1, cb_w), lambda g, b: (0, g)),
        ],
        out_specs=[
            pl.BlockSpec((1, ext, cb_w), lambda g, b: (b, 0, g)),
            pl.BlockSpec((1, 1, span, HEADS), lambda g, b: (g, b, 0, 0)),
            pl.BlockSpec((batch, span, n), lambda g, b: (0, 0, 0)),
            pl.BlockSpec((taps, cb_w), lambda g, b: (0, g)),
            pl.BlockSpec((1, cb_w), lambda g, b: (0, g)),
            pl.BlockSpec((1, 8, cb_w), lambda g, b: (b, 0, g)),
        ],
        out_shape=[
            jax.ShapeDtypeStruct((batch, ext, inner), bf16),
            jax.ShapeDtypeStruct((groups, batch, span, HEADS), f32),
            jax.ShapeDtypeStruct((batch, span, n), f32),
            jax.ShapeDtypeStruct((taps, inner), f32),
            jax.ShapeDtypeStruct((1, inner), f32),
            jax.ShapeDtypeStruct((batch, 8, inner), f32),
        ],
        scratch_shapes=[
            pltpu.VMEM((span + 32, cb_w), f32),
            pltpu.VMEM((batch, span, n), f32),
        ],
        compiler_params=params_of(50),
    )(later, carried, keys, v, dv, colpack, cin, cw, cb)


def keys_back_kernel(span, dk_ref, dk2_ref, dq_ref, cin_ref, cw_ref, cb_ref, cig_ref, dcw_ref, dcb_ref, padded):
    batch = dk_ref.shape[0]
    padded[...] = jnp.zeros_like(padded)
    for b in range(batch):
        dv = jnp.concatenate([dk_ref[b] + dk2_ref[b], dq_ref[b]], axis=1)
        dcw, dcb = conv_back(dv, cin_ref[b].astype(f32), cw_ref[...], cb_ref[...], span, padded, cig_ref, b)
        if b == 0:
            dcw_ref[...] = dcw
            dcb_ref[...] = dcb
        else:
            dcw_ref[...] += dcw
            dcb_ref[...] += dcb


def keys_backward(dk, dk2, dq, cin, cw, cb, span):
    batch, ext, width = cin.shape
    return pl.pallas_call(
        functools.partial(keys_back_kernel, span),
        in_specs=[pl.BlockSpec(memory_space=pltpu.VMEM)] * 6,
        out_specs=[pl.BlockSpec(memory_space=pltpu.VMEM)] * 3,
        out_shape=[
            jax.ShapeDtypeStruct(cin.shape, bf16),
            jax.ShapeDtypeStruct(cw.shape, f32),
            jax.ShapeDtypeStruct(cb.shape, f32),
        ],
        scratch_shapes=[pltpu.VMEM((span + 32, width), f32)],
        compiler_params=params_of(40),
    )(dk, dk2, dq, cin, cw, cb)


def grouped(cols, groups):
    batch, span, heads = cols.shape
    return jnp.transpose(cols.reshape(batch, span, groups, heads // groups), (2, 0, 1, 3))


def ungrouped(cols):
    groups, batch, span, each = cols.shape
    return jnp.transpose(cols, (1, 2, 0, 3)).reshape(batch, span, groups * each)


def on_device(
    resid_in, out_grad, lengths, norm_gain, in_proj, dt_proj, conv_weight, conv_bias, dt_bias, a_log,
    skip_scale, gate_gain, out_proj,
):
    batch, span, width = resid_in.shape
    inner = gate_gain.shape[0]
    heads = a_log.shape[0]
    hw = inner // heads
    n = (in_proj.shape[1] - 2 * inner) // 2
    groups = heads // HEADS
    cb_w = HEADS * hw
    positions = lax.axis_index("seq") * span + lax.iota(jnp.int32, span)
    mask = (positions[None, :] < lengths[:, None]).astype(f32)[..., None]

    halo = shifted(resid_in[:, span - HALO :], "seq", 1)
    resid_ext = jnp.concatenate([halo, resid_in], axis=1).astype(f32)
    rs_ext = lax.rsqrt(jnp.mean(resid_ext * resid_ext, axis=-1, keepdims=True) + epsilon)
    x_ext = (resid_ext * rs_ext * norm_gain).astype(bf16)
    ext = span + HALO
    x2 = x_ext.reshape(batch * ext, width)
    resid_wide = resid_in.astype(f32)
    rs = rs_ext[:, HALO:]

    full_in = lax.all_gather(in_proj, ("dp", "seq"), axis=0, tiled=True)
    full_dt = lax.all_gather(dt_proj, ("dp", "seq"), axis=0, tiled=True)
    full_out = lax.all_gather(out_proj, ("dp", "seq"), axis=0, tiled=True)

    dt_raw = jnp.dot(x_ext[:, HALO:], full_dt, preferred_element_type=f32)
    step = jax.nn.softplus(dt_raw + dt_bias)
    rate = -jnp.exp(a_log)
    tri = causal(span, False).astype(f32)
    log_decay = jnp.einsum("ts,bsh->bth", tri, step * rate, precision=highest)
    scaled = log_decay * LOG2E
    colpack = jnp.concatenate([grouped(scaled, groups), grouped(step, groups)], axis=-1)
    rowpack = jnp.transpose(scaled, (0, 2, 1)).reshape(batch, groups, HEADS, span).transpose(1, 0, 2, 3)
    block_decay = jnp.exp(log_decay[:, span - 1])
    decay_wide = jnp.repeat(block_decay, hw, axis=1)[:, None, :]
    skip_wide = jnp.repeat(skip_scale, hw)[None]
    gain_wide = gate_gain[None]

    cw_keys, cb_keys = conv_weight[:, inner:], conv_bias[None, inner:]
    cw_vals, cb_vals = conv_weight[:, :inner], conv_bias[None, :inner]
    keys, cin_keys = keys_forward(x2, full_in, 2 * inner // (2 * n), cw_keys, cb_keys, batch, span)
    v, cin_vals, local = values_forward(
        x2, full_in, inner // cb_w, cw_vals, cb_vals, keys, colpack, hw, span
    )
    carried = chain(local, decay_wide, False, 1)
    y, gate, normed_out, rg = rows_forward(
        x_ext, full_in, v, keys, colpack, rowpack, carried, skip_wide, gain_wide, hw, span
    )
    mixer_out = jnp.dot(normed_out, full_out, preferred_element_type=f32)
    output = (mask * (resid_wide + mixer_out)).astype(bf16)

    mixer_grad = (mask * out_grad.astype(f32)).astype(bf16)
    mean = jnp.sum(mixer_grad.astype(f32) * mixer_out, axis=-1, keepdims=True) * (1.0 / inner)
    norms = jnp.concatenate([rg[..., :1], mean, jnp.zeros((batch, span, 6), f32)], axis=-1)
    grad_out = jnp.einsum("bsi,bsd->id", normed_out, mixer_grad, preferred_element_type=f32)
    dgate, dv, dh, cols_one, dq, dk, dgain, dskip = gate_backward(
        mixer_grad, full_out, y, gate, norms, gain_wide, v, keys, colpack, rowpack, carried, skip_wide, hw, span
    )
    later = chain(dh, decay_wide, True, 2)
    cig_vals, cols_two, dk2, dcw_vals, dcb_vals, dlast = state_backward(
        later, carried, keys, v, dv, colpack, cin_vals, cw_vals, cb_vals, hw, span
    )
    cig_keys, dcw_keys, dcb_keys = keys_backward(dk, dk2, dq, cin_keys, cw_keys, cb_keys, span)

    rise = ungrouped(cols_one[..., :HEADS])
    direct = ungrouped(cols_one[..., HEADS:])
    ahead = ungrouped(cols_two)
    moved = ahead * step
    last = jnp.sum(moved, axis=1) + dlast[:, 0].reshape(batch, heads, hw).sum(-1) * block_decay
    dlog = rise - moved
    dlog = jnp.einsum("ts,bth->bsh", tri, dlog, precision=highest) + last[:, None, :]
    grad_a = jnp.sum(dlog * step, axis=(0, 1)) * rate
    step_grad = direct + ahead + dlog * rate
    dt_grad = step_grad * jax.nn.sigmoid(dt_raw + dt_bias)
    grad_bias = jnp.sum(dt_grad, axis=(0, 1))
    step_low = dt_grad.astype(bf16)

    x_rows = x_ext[:, HALO:]
    grad_gate = jnp.einsum("bsd,bse->de", x_rows, dgate, preferred_element_type=f32)
    cig = jnp.concatenate([cig_vals, cig_keys], axis=-1)
    grad_conv = jnp.einsum("bsd,bse->de", x_ext, cig, preferred_element_type=f32)
    grad_dt = jnp.einsum("bsd,bsh->dh", x_rows, step_low, preferred_element_type=f32)
    normed_ext = jnp.einsum("bse,de->bsd", cig, full_in[:, inner:], preferred_element_type=f32)
    from_next = shifted(normed_ext[:, :HALO].astype(bf16), "seq", -1).astype(f32)
    normed_grad = normed_ext[:, HALO:]
    normed_grad = jnp.concatenate([normed_grad[:, : span - HALO], normed_grad[:, span - HALO :] + from_next], axis=1)
    normed_grad = normed_grad + jnp.einsum(
        "bse,de->bsd", dgate, full_in[:, :inner], preferred_element_type=f32
    )
    normed_grad = normed_grad + jnp.einsum("bsh,dh->bsd", step_low, full_dt, preferred_element_type=f32)
    nz = resid_wide * rs
    fg = normed_grad * norm_gain
    grad_norm = jnp.sum(normed_grad * nz, axis=(0, 1))
    input_grad = mixer_grad.astype(f32) + rs * (fg - nz * jnp.mean(fg * nz, axis=-1, keepdims=True))

    big = jnp.concatenate([grad_gate, grad_conv, grad_dt], axis=1).astype(bf16)
    sum_in = lax.psum_scatter(big, ("dp", "seq"), scatter_dimension=0, tiled=True).astype(f32)
    sum_out = lax.psum_scatter(grad_out.astype(bf16), ("dp", "seq"), scatter_dimension=0, tiled=True).astype(f32)
    small = lax.psum(
        (
            grad_norm,
            jnp.concatenate([dcw_vals, dcw_keys], axis=1),
            jnp.concatenate([dcb_vals, dcb_keys], axis=1)[0],
            grad_bias,
            grad_a,
            dskip[0].reshape(heads, hw).sum(-1),
            dgain[0],
        ),
        ("dp", "seq"),
    )
    proj = in_proj.shape[1]
    return (
        output,
        input_grad.astype(bf16),
        sum_in[:, :proj],
        sum_in[:, proj:],
        sum_out,
    ) + tuple(small)


def solution(mesh):
    rows = P("dp", "seq", None)
    shard = P(("dp", "seq"), None)
    return jax.shard_map(
        on_device,
        mesh=mesh,
        in_specs=(rows, rows, P("dp"), P(), shard, shard, P(), P(), P(), P(), P(), P(), shard),
        out_specs=(rows, rows, shard, shard, shard, P(), P(), P(), P(), P(), P(), P()),
        check_vma=False,
    )
```

time: 2150 us -> 932 us (0.43)
  waiting for transfers between devices: 938 us -> 369 us
  matrix products: 456 us -> 82.4 us
  Pallas kernels: 0 us -> 301 us
  other arithmetic: 320 us -> 43.5 us
  local copies, waits for them, and re-layouts: 312 us -> 60.8 us
  blocking collectives: 81.8 us -> 46.7 us
    reduce_scatter x3 -> x2, waiting for transfers between devices: 681 us -> 167 us  [the longest x1 167 us: on_device(): lax.psum_scatter(big, ('dp', 'seq'), scatter_dimension=0, tiled=True)]
    dot_general x63 -> x11, matrix products: 456 us -> 82.4 us  [the longest x1 14 us: on_device(): jnp.einsum('bsd,bse->de', x_ext, cig, preferred_element_type=f32)]
    pallas_call x0 -> x8, Pallas kernels: none -> 301 us  [the longest x2 125 us: chain(): pl.pallas_call(functools.partial(chain_kernel, backward, size), in_specs=...]
    all_gather x8 -> x2, waiting for transfers between devices: 251 us -> 75.1 us  [the longest x1 60.3 us: on_device(): full_in = lax.all_gather(in_proj, ('dp', 'seq'), axis=0, tiled=True)]
    psum x1, waiting for transfers between devices: 4 us -> 126 us  [on_device(): lax.psum((grad_norm, jnp.concatenate([dcw_vals, dcw_keys], axis=1), jnp.c...]
    mul x90 -> x2, local copies, waits for them, and re-layouts: 122 us -> 0.26 us  [the longest x1 0.19 us: on_device(): jnp.sum(mixer_grad.astype(f32) * mixer_out, axis=-1, keepdims=True)]
    select_n x42 -> x0, other arithmetic: 107 us -> none  [turn(): jnp.where(position < mine, new, old)]
    reduce_sum x25 -> x4, other arithmetic: 92 us -> 4.36 us  [the longest x1 2.38 us: on_device(): jnp.mean(resid_ext * resid_ext, axis=-1, keepdims=True) + epsilon]
  transfers between devices with their start and end apart: 18 -> 7, of which waited for: 9 -> 4; matrix products, arithmetic and copies ran while one was open for 32% -> 14% of each run, Pallas kernels for 0% -> 33%
where the time goes in v1:
time: 932 us; the launch traced here: 923 us
  waiting for transfers between devices  369 us (40%)
  Pallas kernels  301 us (32%)
  matrix products  82.4 us (9%)
  local copies, waits for them, and re-layouts  60.8 us (7%)
  blocking collectives  46.7 us (5%)
  other arithmetic  43.5 us (5%)
  between operations  14.7 us (2%)
    reduce_scatter x1, waiting for transfers between devices, on_device(): lax.psum_scatter(big, ('dp', 'seq'), scatter_dimension=0, tiled=True)  167 us
    psum x1, waiting for transfers between devices, on_device(): lax.psum((grad_norm, jnp.concatenate([dcw_vals, dcw_keys], axis=1), jnp.c...  126 us
    pallas_call x2, Pallas kernels, chain(): pl.pallas_call(functools.partial(chain_kernel, backward, size), in_specs=...  125 us
    all_gather x1, waiting for transfers between devices, on_device(): full_in = lax.all_gather(in_proj, ('dp', 'seq'), axis=0, tiled=True)  60.3 us
    pallas_call x1, Pallas kernels, gate_backward(): pl.pallas_call(functools.partial(gate_back_kernel, span, hw), grid=(group...  58.4 us
    pallas_call x1, Pallas kernels, state_backward(): pl.pallas_call(functools.partial(state_back_kernel, span, hw), grid=(grou...  51.6 us
    all_gather x1, blocking collectives, on_device(): full_dt = lax.all_gather(dt_proj, ('dp', 'seq'), axis=0, tiled=True)  46.7 us
    pallas_call x1, Pallas kernels, rows_forward(): pl.pallas_call(functools.partial(out_kernel, span, hw), grid=(groups, bat...  37.4 us
  transfers between devices with their start and end apart: 7, of which 4 were waited for; matrix products, arithmetic and copies ran while one was open for 14% of the time, Pallas kernels for 33%

profile of v1, /device:TPU:0, one launch (start us, length us, event | category | flops | bytes accessed | tf_op | source)
XLA Modules:
  0.0 922.5 jit_solution(5917297754411977709)
XLA Ops:
  17.7 46.7 %all_gather.10 = bf16[1536,48]{1,0:T(8,128)(2,1)S(1)} all-gather(bf16[48,48]{1,0:T(8,128)(2,1)} %param.18), channel_id=1, replica_groups=mesh['dp'=4,'seq'=8] {'dp','seq'}, dimensions={0}, use_global_device_ids=true | all-gather | bytes 152064 | tf_op jit(solution)/shard_map/all_gather | solution.py:650
  75.6 3.1 pad_maximum_fusion.1.col_ref
  84.1 60.3 %all-gather.3.cloned.1.call-done.w_ref = bf16[1536,6400]{1,0:T(8,128)(2,1)} async-done(((bf16[48,6400]{1,0:T(8,128)(2,1)}), bf16[1536,6400]{1,0:T(8,128)(2,1)}) %all-gather.3.cloned.1.call-update) | async-done | bytes 19660816 | tf_op jit(solution)/shard_map/all_gather | solution.py:649
  148.6 23.9 %shard_map.221 = (bf16[3,256,3072]{2,1,0:T(8,128)(2,1)}, bf16[3,272,3072]{2,1,0:T(8,128)(2,1)}, f32[3,128,3072]{2,1,0:T(8,128)}) custom-call(bf16[816,1536]{1,0:T(8,128)(2,1)} %fusion.8.x_ref, bf16[1536,6400]{1,0:T(8,128)(2,1)} %all-gather.3.cloned.1.call-done.w_ref, f32[4,3072]{1,0:T(4,128)S(1)} %slice.63.cw_ref, f32[1,3072]{1,0:T(1,128)S(1)} %bitcast.112, ...), custom_call_target="tpu_custom_call" | custom-call | tf_op jit(solution)/shard_map/pallas_call | solution.py:137
  174.9 5.2 shard_map.222.h_ref
  182.3 37.4 %shard_map.223 = (f32[3,256,3072]{2,1,0:T(8,128)}, bf16[3,256,3072]{2,1,0:T(8,128)(2,1)}, bf16[3,256,3072]{2,1,0:T(8,128)(2,1)}, f32[3,256,8]{2,1,0:T(8,128)}) custom-call(bf16[3,272,1536]{2,1,0:T(8,128)(2,1)} %copy-done.24, bf16[1536,6400]{1,0:T(8,128)(2,1)} %all-gather.3.cloned.1.call-done.w_ref, bf16[3,256,3072]{2,1,0:T(8,128)(2,1)} %get-tuple-element.39.v_ref, ...), custom_call_target="tpu_custom_call" | custom-call | tf_op jit(solution)/shard_map/pallas_call | solution.py:302
  219.7 14.7 %all-gather.5.cloned.1.call-done.w_ref = bf16[3072,1536]{1,0:T(8,128)(2,1)} async-done(((bf16[96,1536]{1,0:T(8,128)(2,1)}), bf16[3072,1536]{1,0:T(8,128)(2,1)}) %all-gather.5.cloned.1.call-update) | async-done | bytes 9437200 | tf_op jit(solution)/shard_map/all_gather | solution.py:651
  234.4 13.5 %fusion.15 = (f32[3,256]{1,0:T(4,128)S(1)}, bf16[3,256,1536]{2,1,0:T(8,128)(2,1)S(1)}, bf16[3,256,1536]{2,1,0:T(8,128)(2,1)}) fusion(bf16[3,256,1536]{2,1,0:T(8,128)(2,1)} %param.14, f32[3,256]{1,0:T(4,128)S(1)} %compare_convert_fusion, bf16[3,256,1536]{2,1,0:T(8,128)(2,1)S(1)} %copy-done.20, bf16[3,256,3072]{2,1,0:T(8,128)(2,1)} %get-tuple-element.41, ...), kind=kOutput, calls=%fused_computation.28 | convolution fusion | flops 7259552768 | bytes 23599104 | tf_op jit(solution)/shard_map/dot_general | solution.py:676
  249.3 9.7 %bitcast_convert_fusion.1 = bf16[3072,1536]{1,0:T(8,128)(2,1)} fusion(bf16[3,256,3072]{2,1,0:T(8,128)(2,1)S(1)} %copy-done.38, bf16[3,256,1536]{2,1,0:T(8,128)(2,1)S(1)} %get-tuple-element.76.mg_ref), kind=kOutput, calls=%fused_computation.2 | convolution fusion | flops 7252475904 | bytes 16515072 | tf_op jit(solution)/shard_map/bsi,bsd->id/dot_general | solution.py:682
  260.1 58.4 %shard_map.224 = (bf16[3,256,3072]{2,1,0:T(8,128)(2,1)}, bf16[3,256,3072]{2,1,0:T(8,128)(2,1)}, f32[3,128,3072]{2,1,0:T(8,128)}, f32[6,3,256,16]{3,2,1,0:T(8,128...) custom-call(bf16[3,256,1536]{2,1,0:T(8,128)(2,1)} %copy-done.26, ...), custom_call_target="tpu_custom_call" | custom-call | tf_op jit(solution)/shard_map/pallas_call | solution.py:427
  321.4 120.1 %shard_map.225.later_ref = f32[3,128,3072]{2,1,0:T(8,128)S(1)} custom-call(f32[3,128,3072]{2,1,0:T(8,128)S(1)} %copy-done.6, f32[3,1,3072]{2,1,0:T(1,128)S(1)} %broadcast_in_dim_reshape.6.decay_ref), custom_call_target="tpu_custom_call" | custom-call | tf_op jit(solution)/shard_map/pallas_call | solution.py:221
  443.8 51.6 %shard_map.226 = (bf16[3,272,3072]{2,1,0:T(8,128)(2,1)}, f32[6,3,256,8]{3,2,1,0:T(8,128)S(1)}, f32[3,256,128]{2,1,0:T(8,128)S(1)}, f32[4,3072]{1,0:T(4,128)S(1)}...) custom-call(f32[3,128,3072]{2,1,0:T(8,128)} %copy-done.3, f32[3,128,3072]{2,1,0:T(8,128)} %copy-done, ...), custom_call_target="tpu_custom_call" | custom-call | tf_op jit(solution)/shard_map/pallas_call | solution.py:548
  498.3 3.0 copy.82
  501.2 3.0 slice_bitcast_fusion.5
  517.4 2.9 constant_dynamic-update-slice_fusion.1
  522.8 10.3 %bitcast_convert_fusion.2 = bf16[1536,3072]{1,0:T(8,128)(2,1)S(1)} fusion(bf16[3,256,3072]{2,1,0:T(8,128)(2,1)} %get-tuple-element.54, bf16[3,272,1536]{2,1,0:T(8,128)(2,1)S(1)} %copy-done.25), kind=kOutput, calls=%fused_computation.3 | convolution fusion | flops 7252475904 | bytes 16515072 | tf_op jit(solution)/shard_map/bsd,bse->de/dot_general | solution.py:706
  533.1 14.0 %bitcast_convert_fusion = bf16[1536,3328]{1,0:T(8,128)(2,1)S(1)} fusion(bf16[3,272,1536]{2,1,0:T(8,128)(2,1)S(1)} %copy-done.25, bf16[3,272,3328]{2,1,0:T(8,128)(2,1)} %copy-done.27), kind=kOutput, calls=%fused_computation | convolution fusion | flops 8347582464 | bytes 18161664 | tf_op jit(solution)/shard_map/bsd,bse->de/dot_general | solution.py:708
  547.1 17.7 %pad_maximum_fusion = bf16[1536,6448]{1,0:T(8,128)(2,1)} fusion(bf16[1536,48]{1,0:T(8,128)(2,1)S(1)} %copy.87, bf16[1536,3328]{1,0:T(8,128)(2,1)S(1)} %bitcast_convert_fusion, bf16[1536,3072]{1,0:T(8,128)(2,1)S(1)} %bitcast_convert_fusion.2), kind=kLoop, calls=%fused_computation.1 | loop fusion | flops 59424768 | bytes 39616512 | tf_op jit(solution)/shard_map/concatenate | solution.py:723
  565.0 13.3 %fusion = f32[3,272,1536]{2,1,0:T(8,128)S(1)} fusion(bf16[3,272,3328]{2,1,0:T(8,128)(2,1)} %copy-done.27, bf16[1536,6400]{1,0:T(8,128)(2,1)} %all-gather.3.cloned.1.call-done.w_ref), kind=kOutput, calls=%fused_computation.5 | convolution fusion | flops 8342470656 | bytes 20668416 | tf_op jit(solution)/shard_map/bse,de->bsd/dot_general | solution.py:710
  585.1 12.8 %fusion.1 = f32[3,256,1536]{2,1,0:T(8,128)S(1)} fusion(bf16[3,256,3072]{2,1,0:T(8,128)(2,1)} %get-tuple-element.54, bf16[1536,6400]{1,0:T(8,128)(2,1)} %all-gather.3.cloned.1.call-done.w_ref), kind=kOutput, calls=%fused_computation.7 | convolution fusion | flops 7247757312 | bytes 18874368 | tf_op jit(solution)/shard_map/bse,de->bsd/dot_general | solution.py:714
  598.6 4.5 fusion.12
  603.1 5.5 fusion.16
  610.4 166.9 %reduce-scatter.3.cloned.1.call-done = bf16[48,6448]{1,0:T(8,128)(2,1)} async-done(((bf16[1536,6448]{1,0:T(8,128)(2,1)}), bf16[48,6448]{1,0:T(8,128)(2,1)}) %reduce-scatter.3.cloned.1.call-update) | async-done | bytes 619024 | tf_op jit(solution)/shard_map/reduce_scatter | solution.py:724
  780.8 126.1 %all-reduce.3.cloned.1.call-done = (f32[1536]{0:T(1024)}, f32[4,3328]{1,0:T(4,128)}, f32[3328]{0:T(1024)}, f32[48]{0:T(128)}, f32[48]{0:T(128)}, /*index=5*/f32[48]{0:T(128)}, f32[3072]{0:T(1024)}) async-done(((f32[1536]{0:T(1024)}, f32[4,3328]{1,0:T(4,128)}, f32[3328]{0:T(1024)}, f32[48]{0:T(128)}, f32[48]{0:T(128)}, /*index=5*/f32[48]{0:T(128)}, f32[3072]{0:T(1024)}), (f32[1536]{0:T(1024)}, ...) | async-done | bytes 85584 | tf_op jit(solution)/shard_map/psum | solution.py:726
  (166 shorter events, 83.3 us)
Async XLA Ops:
  7.2 59.8 %copy-start.19 = (bf16[3,256,1536]{2,1,0:T(8,128)(2,1)S(1)}, bf16[3,256,1536]{2,1,0:T(8,128)(2,1)}, u32[]{:S(2)}) copy-start(bf16[3,256,1536]{2,1,0:T(8,128)(2,1)} %param.13) | copy-start | bytes 7077892
  7.2 62.6 %copy-start.39 = (f32[48]{0:T(128)S(1)}, f32[48]{0:T(128)}, u32[]{:S(2)}) copy-start(f32[48]{0:T(128)} %param.21) | copy-start | bytes 580
  7.2 137.2 %all-gather.3.cloned.1.call-start = ((), (), s32[]{:S(2)}) async-start(), calls=%async_computation.2 | async-start | bytes 20275200 | tf_op jit(solution)/shard_map/all_gather | solution.py:649
  7.9 226.5 %all-gather.5.cloned.1.call-start = ((), (), s32[]{:S(2)}) async-start(), calls=%async_computation.3 | async-start | bytes 9732096 | tf_op jit(solution)/shard_map/all_gather | solution.py:651
  8.7 599.8 %reduce-scatter.5.cloned.1.call-start = ((), (), s32[]{:S(2)}) async-start(), calls=%async_computation.5 | async-start | bytes 9732096 | tf_op jit(solution)/shard_map/reduce_scatter | solution.py:725
  9.7 54.8 %collective-permute-start = (bf16[3,16,1536]{2,1,0:T(8,128)(2,1)S(1)}, bf16[3,16,1536]{2,1,0:T(8,128)(2,1)S(1)}, u32[]{:S(2)}, u32[]{:S(2)}) collective-permute-start(bf16[3,16,1536]{2,1,0:T(8,128)(2,1)S(1)} %slice.62), channel_id=1, source_target_pairs={{0,1},{1,2},{2,3},{3,4},{4,5},{5,6},{6,7},{8,9},{9,10},{10,11},{11... | collective-permute-start | bytes 442376 | tf_op jit(solution)/shard_map/ppermute | solution.py:35
  78.7 70.0 %copy-start.1 = (f32[6,3,256,16]{3,2,1,0:T(8,128)}, f32[6,3,256,16]{3,2,1,0:T(8,128)S(1)}, u32[]{:S(2)}) copy-start(f32[6,3,256,16]{3,2,1,0:T(8,128)S(1)} %pad_maximum_fusion.1.col_ref) | copy-start | bytes 884740
  148.6 23.9 %copy-start.4 = (bf16[3,256,256]{2,1,0:T(8,128)(2,1)}, bf16[3,256,256]{2,1,0:T(8,128)(2,1)S(1)}, u32[]{:S(2)}) copy-start(bf16[3,256,256]{2,1,0:T(8,128)(2,1)S(1)} %get-tuple-element.38.keys_ref) | copy-start | bytes 1179652
  182.3 52.1 %copy-start.20 = (bf16[3,256,1536]{2,1,0:T(8,128)(2,1)S(1)}, bf16[3,256,1536]{2,1,0:T(8,128)(2,1)}, u32[]{:S(2)}) copy-start(bf16[3,256,1536]{2,1,0:T(8,128)(2,1)} %param.13) | copy-start | bytes 7077892
  234.4 14.8 %copy-start.38 = (bf16[3,256,3072]{2,1,0:T(8,128)(2,1)S(1)}, bf16[3,256,3072]{2,1,0:T(8,128)(2,1)}, u32[]{:S(2)}) copy-start(bf16[3,256,3072]{2,1,0:T(8,128)(2,1)} %get-tuple-element.41) | copy-start | bytes 14155780
  259.0 518.3 %reduce-scatter.3.cloned.1.call-start = ((), (), s32[]{:S(2)}) async-start(), calls=%async_computation.4 | async-start | bytes 20680704 | tf_op jit(solution)/shard_map/reduce_scatter | solution.py:724
  318.5 123.0 %copy-start.10 = (f32[3,256,128]{2,1,0:T(8,128)}, f32[3,256,128]{2,1,0:T(8,128)S(1)}, u32[]{:S(2)}) copy-start(f32[3,256,128]{2,1,0:T(8,128)S(1)} %get-tuple-element.51.dq_ref) | copy-start | bytes 1179652
  318.5 123.0 %copy-start.12 = (f32[3,256,128]{2,1,0:T(8,128)}, f32[3,256,128]{2,1,0:T(8,128)S(1)}, u32[]{:S(2)}) copy-start(f32[3,256,128]{2,1,0:T(8,128)S(1)} %get-tuple-element.49.dk_ref) | copy-start | bytes 1179652
  506.6 8.7 copy-start.11
  506.6 8.7 copy-start.13
  506.6 8.7 copy-start.15
  564.8 342.0 %all-reduce.3.cloned.1.call-start = ((), (), s32[]{:S(2)}) async-start(), calls=%async_computation.6 | async-start | bytes 183296 | tf_op jit(solution)/shard_map/psum | solution.py:726
  580.6 17.9 %collective-permute-start.1 = (bf16[3,16,1536]{2,1,0:T(8,128)(2,1)S(1)}, bf16[3,16,1536]{2,1,0:T(8,128)(2,1)S(1)}, u32[]{:S(2)}, u32[]{:S(2)}) collective-permute-start(bf16[3,16,1536]{2,1,0:T(8,128)(2,1)S(1)} %slice.114), channel_id=1, source_target_pairs={{1,0},{2,1},{3,2},{4,3},{5,4},{6,5},{7,6},{9,8},{10,9},{11,10},{12... | collective-permute-start | bytes 442376 | tf_op jit(solution)/shard_map/ppermute | solution.py:35
  585.1 12.9 %copy-start.40 = (f32[48]{0:T(128)S(1)}, f32[48]{0:T(128)}, u32[]{:S(2)}) copy-start(f32[48]{0:T(128)} %param.22) | copy-start | bytes 580
  585.1 13.4 %copy-start.23 = (f32[3,272,1536]{2,1,0:T(8,128)S(1)}, f32[3,272,1536]{2,1,0:T(8,128)}, u32[]{:S(2)}) copy-start(f32[3,272,1536]{2,1,0:T(8,128)} %copy-done.22) | copy-start | bytes 15040516
  585.1 13.5 %copy-start.21 = (bf16[3,256,1536]{2,1,0:T(8,128)(2,1)S(1)}, bf16[3,256,1536]{2,1,0:T(8,128)(2,1)}, u32[]{:S(2)}) copy-start(bf16[3,256,1536]{2,1,0:T(8,128)(2,1)} %param.13) | copy-start | bytes 7077892
  585.1 13.5 %slice-start = ((f32[3,272,1536]{2,1,0:T(8,128)}), f32[3,240,1536]{2,1,0:T(8,128)S(1)}, s32[]{:S(2)}) async-start(f32[3,272,1536]{2,1,0:T(8,128)} %copy-done.22), calls=%async_computation.7 | async-start | bytes 8847360 | tf_op jit(solution)/shard_map/slice | solution.py:713
  585.1 13.5 %copy-start.29 = (bf16[1536,48]{1,0:T(8,128)(2,1)S(1)}, bf16[1536,48]{1,0:T(8,128)(2,1)}, u32[]{:S(2)}) copy-start(bf16[1536,48]{1,0:T(8,128)(2,1)} %copy-done.28) | copy-start | bytes 442372
  585.1 13.5 %copy-start.37 = (f32[1536]{0:T(1024)S(1)}, f32[1536]{0:T(1024)}, u32[]{:S(2)}) copy-start(f32[1536]{0:T(1024)} %param.16) | copy-start | bytes 18436
  (25 other events, 72.7 us)
Sparse Core Ops, SparseCore 0:
  11.1 133.3 all-gather.2
  147.4 86.9 all-gather.4
  259.1 196.0 reduce-scatter.4
  565.0 212.2 reduce-scatter.2
  784.7 122.1 all-reduce.2

commit v2 on v1

--- a/solution.py
+++ b/solution.py
@@ -613,6 +613,521 @@
     )(dk, dk2, dq, cin, cw, cb)
 
 
+class Place:
+    def __init__(self):
+        self.dp = lax.axis_index("dp")
+        self.seq = lax.axis_index("seq")
+        y, x = self.dp // 2, self.dp % 2
+        self.z, self.core = self.seq // 2, self.seq % 2
+        self.dx = 2 * y + (1 - x)
+        self.dy = 2 * (1 - y) + x
+        self.dxy = 2 * (1 - y) + (1 - x)
+        self.to_x = (self.dx, self.seq)
+        self.to_y = (self.dy, self.seq)
+        self.to_core = (self.dp, 2 * self.z + 1 - self.core)
+        self.to_up = (self.dp, 2 * jnp.minimum(self.z + 1, 3) + self.core)
+        self.to_down = (self.dp, 2 * jnp.maximum(self.z - 1, 0) + self.core)
+        self.to_across = (self.dp, 2 * jnp.where(self.z < 2, self.z + 2, self.z - 2) + self.core)
+        self.has_up = self.z < 3
+        self.has_down = self.z > 0
+
+    def near(self, k):
+        z = self.z
+        return (z, z + 1 - 2 * (z % 2), jnp.where(z < 2, 2, 1), jnp.where(z < 2, 3, 0))[k]
+
+    def greet(self, others=()):
+        barrier = pltpu.get_barrier_semaphore()
+        for device in (self.to_x, self.to_y, self.to_core) + tuple(others):
+            pl.semaphore_signal(barrier, inc=1, device_id=device, device_id_type=MESH)
+
+        @pl.when(self.has_up)
+        def _():
+            pl.semaphore_signal(barrier, inc=1, device_id=self.to_up, device_id_type=MESH)
+
+        @pl.when(self.has_down)
+        def _():
+            pl.semaphore_signal(barrier, inc=1, device_id=self.to_down, device_id_type=MESH)
+
+        ends = self.has_up.astype(jnp.int32) + self.has_down.astype(jnp.int32)
+        pl.semaphore_wait(barrier, 3 + len(others) + ends)
+
+
+GATHER_KINDS = 11
+
+
+def gather_steps(place, shard, full, split, own_sem, send, recv):
+    rows, width = shard.shape
+    z, core = place.z, place.core
+    every, left, right = pl.ds(0, width), pl.ds(0, split), pl.ds(split, width - split)
+
+    def view(d, zz, cc, cols):
+        start = pl.multiple_of((d * 8 + zz * 2 + cc) * rows, 16)
+        return full.at[pl.ds(start, rows), cols]
+
+    def copy(kind, slot, device, d, zz, cc, cols, src=None):
+        dst = view(d, zz, cc, cols)
+        return pltpu.make_async_remote_copy(
+            src_ref=dst if src is None else src,
+            dst_ref=dst,
+            send_sem=send.at[kind, slot],
+            recv_sem=recv.at[kind, slot],
+            device_id=device,
+            device_id_type=MESH,
+        )
+
+    def pieces(k):
+        zk = place.near(k)
+        src = shard if k == 0 else None
+        dp = place.dp
+        return dict(
+            x=copy(2, k, place.to_x, dp, zk, core, every, src),
+            y=copy(3, k, place.to_y, dp, zk, core, every, src),
+            own=copy(6, k, place.to_core, dp, zk, core, every, src),
+        )
+
+    def along(k, up):
+        zk = place.near(k)
+        src = shard if k == 0 else None
+        device = place.to_up if up else place.to_down
+        dst = view(place.dp, zk, core, every)
+        return pltpu.make_async_remote_copy(
+            src_ref=dst if src is None else src,
+            dst_ref=dst,
+            send_sem=send.at[0 if up else 1, k],
+            recv_sem=recv.at[0, zk],
+            device_id=device,
+            device_id_type=MESH,
+        )
+
+    def arrive(k):
+        zk = place.near(k)
+        if k > 0:
+            along(k, True).wait_recv()
+
+        @pl.when(jnp.logical_and(zk <= z, place.has_up))
+        def _():
+            along(k, True).start()
+
+        @pl.when(jnp.logical_and(zk >= z, place.has_down))
+        def _():
+            along(k, False).start()
+
+        made = pieces(k)
+        made["x"].start()
+        made["y"].start()
+        made["own"].start()
+
+    def cross(k):
+        zk = place.near(k)
+        return (
+            copy(2, k, place.to_x, place.dx, zk, core, every),
+            copy(3, k, place.to_y, place.dy, zk, core, every),
+            copy(4, k, place.to_y, place.dx, zk, core, left),
+            copy(5, k, place.to_x, place.dy, zk, core, right),
+            copy(7, k, place.to_core, place.dx, zk, core, every),
+            copy(8, k, place.to_core, place.dy, zk, core, every),
+        )
+
+    def forward(k):
+        from_x, from_y, left_on, right_on, core_x, core_y = cross(k)
+        from_x.wait_recv()
+        left_on.start()
+        core_x.start()
+        from_y.wait_recv()
+        right_on.start()
+        core_y.start()
+
+    def corner(k):
+        zk = place.near(k)
+        return (
+            copy(4, k, place.to_y, place.dxy, zk, core, left),
+            copy(5, k, place.to_x, place.dxy, zk, core, right),
+            copy(9, k, place.to_core, place.dxy, zk, core, left),
+            copy(10, k, place.to_core, place.dxy, zk, core, right),
+        )
+
+    def last(k):
+        from_y, from_x, core_left, core_right = corner(k)
+        from_y.wait_recv()
+        core_left.start()
+        from_x.wait_recv()
+        core_right.start()
+
+    def mine():
+        return pltpu.make_async_copy(shard, view(place.dp, z, core, every), own_sem)
+
+    def begin():
+        mine().start()
+        arrive(0)
+
+    def finish():
+        mine().wait()
+        other = 1 - core
+        for k in range(4):
+            zk = place.near(k)
+            for kind, d, cols in (
+                (6, place.dp, every), (7, place.dx, every), (8, place.dy, every),
+                (9, place.dxy, left), (10, place.dxy, right),
+            ):
+                copy(kind, k, place.to_core, d, zk, other, cols).wait_recv()
+        for k in range(4):
+            zk = place.near(k)
+
+            @pl.when(jnp.logical_and(zk <= z, place.has_up))
+            def _():
+                along(k, True).wait_send()
+
+            @pl.when(jnp.logical_and(zk >= z, place.has_down))
+            def _():
+                along(k, False).wait_send()
+
+            made = pieces(k)
+            made["x"].wait_send()
+            made["y"].wait_send()
+            made["own"].wait_send()
+            for one in cross(k)[2:]:
+                one.wait_send()
+            for one in corner(k)[2:]:
+                one.wait_send()
+
+    return [
+        begin,
+        lambda: arrive(1),
+        lambda: forward(0),
+        lambda: arrive(2),
+        lambda: forward(1),
+        lambda: arrive(3),
+        lambda: forward(2),
+        lambda: last(0),
+        lambda: forward(3),
+        lambda: last(1),
+        lambda: last(2),
+        lambda: last(3),
+        finish,
+    ]
+
+
+def gather_scratch():
+    return [
+        pltpu.SemaphoreType.DMA,
+        pltpu.SemaphoreType.DMA((GATHER_KINDS, 4)),
+        pltpu.SemaphoreType.DMA((GATHER_KINDS, 4)),
+    ]
+
+
+def gather_kernel(splits, *refs):
+    count = len(splits)
+    shards, fulls, sems = refs[:count], refs[count : 2 * count], refs[2 * count :]
+    place = Place()
+    place.greet()
+    plans = [
+        gather_steps(place, shards[i], fulls[i], splits[i], *sems[3 * i : 3 * i + 3]) for i in range(count)
+    ]
+    for step in zip(*plans):
+        for one in step:
+            one()
+
+
+def gather(shards, splits, collective_id):
+    count = len(shards)
+    spec = pl.BlockSpec(memory_space=pl.ANY)
+    return pl.pallas_call(
+        functools.partial(gather_kernel, splits),
+        in_specs=[spec] * count,
+        out_specs=[spec] * count,
+        out_shape=[jax.ShapeDtypeStruct((s.shape[0] * 32, s.shape[1]), s.dtype) for s in shards],
+        scratch_shapes=gather_scratch() * count,
+        compiler_params=pltpu.CompilerParams(collective_id=collective_id, has_side_effects=True),
+    )(*shards)
+
+
+class Scatter:
+    def __init__(self, place, big, out, own, land_core, land_xy, land_z, local, send, recv, split):
+        self.place, self.big, self.out = place, big, out
+        self.own, self.land_core, self.land_xy, self.land_z = own, land_core, land_xy, land_z
+        self.local, self.send, self.recv = local, send, recv
+        self.rows, self.width = out.shape
+        self.split = split
+        self.left, self.right = slice(0, split), slice(split, self.width)
+
+    def groups(self):
+        p = self.place
+        return (p.dxy, p.dx, p.dy, p.dp)
+
+    def far(self, k):
+        return self.place.near(3 - k)
+
+    def source(self, d, zz, cc):
+        start = pl.multiple_of((d * 8 + zz * 2 + cc) * self.rows, 16)
+        return self.big.at[pl.ds(start, self.rows)]
+
+    def remote(self, src, dst, kind, slot, device):
+        return pltpu.make_async_remote_copy(
+            src_ref=src, dst_ref=dst, send_sem=self.send.at[kind, slot], recv_sem=self.recv.at[kind, slot],
+            device_id=device, device_id_type=MESH,
+        )
+
+    def to_other(self, i, k):
+        p = self.place
+        src = self.source(self.groups()[i], self.far(k), 1 - p.core)
+        return self.remote(src, self.land_core.at[i, k], i, k, p.to_core)
+
+    def load(self, i, k):
+        p = self.place
+        return pltpu.make_async_copy(
+            self.source(self.groups()[i], self.far(k), p.core), self.own.at[i, k], self.local.at[i, k]
+        )
+
+    def start_group(self, i):
+        for k in range(4):
+            self.to_other(i, k).start()
+            self.load(i, k).start()
+
+    def join(self, i, k):
+        self.load(i, k).wait()
+        self.to_other(i, k).wait_recv()
+        self.own[i, k] = self.own[i, k] + self.land_core[i, k]
+
+    def side(self, kind, k):
+        p = self.place
+        left, right = pl.ds(0, self.split), pl.ds(self.split, self.width - self.split)
+        group, cols, device = (
+            (0, left, p.to_y),
+            (0, right, p.to_x),
+            (2, left, p.to_y),
+            (1, right, p.to_x),
+            (2, right, p.to_y),
+            (1, left, p.to_x),
+        )[kind]
+        size = self.split if cols is left else self.width - self.split
+        return self.remote(
+            self.own.at[group, k, :, cols], self.land_xy.at[kind, k, :, pl.ds(0, size)], 4 + kind, k, device
+        )
+
+    def take(self, kind, group, cols, k):
+        self.side(kind, k).wait_recv()
+        size = cols.stop - cols.start
+        self.own[group, k, :, cols] = self.own[group, k, :, cols] + self.land_xy[kind, k, :, 0:size]
+
+    def corner(self, k):
+        self.join(0, k)
+        self.side(0, k).start()
+        self.side(1, k).start()
+
+    def sides(self, k):
+        self.join(1, k)
+        self.side(3, k).start()
+        self.join(2, k)
+        self.side(2, k).start()
+        self.take(0, 1, self.left, k)
+        self.side(5, k).start()
+        self.take(1, 2, self.right, k)
+        self.side(4, k).start()
+
+    def along(self, k, up):
+        p = self.place
+        zk = self.far(k)
+        return pltpu.make_async_remote_copy(
+            src_ref=self.own.at[3, k],
+            dst_ref=self.land_z.at[0 if up else 1, zk],
+            send_sem=self.send.at[10, k],
+            recv_sem=self.recv.at[10 if up else 11, zk],
+            device_id=p.to_up if up else p.to_down,
+            device_id_type=MESH,
+        )
+
+    def mine(self, k):
+        p = self.place
+        self.join(3, k)
+        self.take(2, 3, self.left, k)
+        self.take(3, 3, self.right, k)
+        self.take(5, 3, self.left, k)
+        self.take(4, 3, self.right, k)
+        if k == 3:
+            return
+        zk = self.far(k)
+        rising = zk > p.z
+        behind = jnp.logical_or(
+            jnp.logical_and(rising, p.has_down), jnp.logical_and(jnp.logical_not(rising), p.has_up)
+        )
+
+        @pl.when(jnp.logical_and(behind, rising))
+        def _():
+            self.along(k, True).wait_recv()
+            self.own[3, k] = self.own[3, k] + self.land_z[0, zk]
+
+        @pl.when(jnp.logical_and(behind, jnp.logical_not(rising)))
+        def _():
+            self.along(k, False).wait_recv()
+            self.own[3, k] = self.own[3, k] + self.land_z[1, zk]
+
+        @pl.when(rising)
+        def _():
+            self.along(k, True).start()
+
+        @pl.when(jnp.logical_not(rising))
+        def _():
+            self.along(k, False).start()
+
+    def result(self):
+        p = self.place
+        self.out[...] = self.own[3, 3].astype(f32)
+
+        @pl.when(p.has_down)
+        def _():
+            self.along(3, True).wait_recv()
+            self.out[...] += self.land_z[0, p.z].astype(f32)
+
+        @pl.when(p.has_up)
+        def _():
+            self.along(3, False).wait_recv()
+            self.out[...] += self.land_z[1, p.z].astype(f32)
+
+    def drain(self):
+        for k in range(4):
+            for i in range(4):
+                self.to_other(i, k).wait_send()
+            for kind in range(6):
+                self.side(kind, k).wait_send()
+            if k < 3:
+                self.along(k, True).wait_send()
+
+    @staticmethod
+    def scratch(rows, width, split):
+        half = max(split, width - split)
+        return [
+            pltpu.VMEM((4, 4, rows, width), bf16),
+            pltpu.VMEM((4, 4, rows, width), bf16),
+            pltpu.VMEM((6, 4, rows, half), bf16),
+            pltpu.VMEM((2, 4, rows, width), bf16),
+            pltpu.SemaphoreType.DMA((4, 4)),
+            pltpu.SemaphoreType.DMA((11, 4)),
+            pltpu.SemaphoreType.DMA((12, 4)),
+        ]
+
+
+class Small:
+    def __init__(self, place, value, out, sent, landed, send, recv):
+        p = place
+        self.value, self.out, self.sent, self.landed, self.send, self.recv = value, out, sent, landed, send, recv
+        pair = 2 * (p.z + 1 - 2 * (p.z % 2)) + p.core
+        self.devices = (p.to_core, p.to_x, p.to_y, (p.dp, pair), p.to_across)
+
+    def copy(self, i):
+        return pltpu.make_async_remote_copy(
+            src_ref=self.sent.at[i], dst_ref=self.landed.at[i], send_sem=self.send.at[i],
+            recv_sem=self.recv.at[i], device_id=self.devices[i], device_id_type=MESH,
+        )
+
+    def go(self, i):
+        if i == 0:
+            self.sent[0] = self.value[...]
+            self.copy(0).start()
+            return
+        self.copy(i - 1).wait_recv()
+        total = self.sent[i - 1] + self.landed[i - 1]
+        if i < 5:
+            self.sent[i] = total
+            self.copy(i).start()
+        else:
+            self.out[...] = total
+            for k in range(5):
+                self.copy(k).wait_send()
+
+    @staticmethod
+    def scratch(shape):
+        return [
+            pltpu.VMEM((5,) + shape, f32),
+            pltpu.VMEM((5,) + shape, f32),
+            pltpu.SemaphoreType.DMA((5,)),
+            pltpu.SemaphoreType.DMA((5,)),
+        ]
+
+
+def scatter_kernel(splits, with_small, *refs):
+    count = len(splits)
+    ins = count + (1 if with_small else 0)
+    bigs, outs = refs[:count], refs[ins : ins + count]
+    scratch = refs[2 * ins :]
+    place = Place()
+    place.greet((place.to_across,) if with_small else ())
+    plans = [
+        Scatter(place, bigs[i], outs[i], *scratch[7 * i : 7 * i + 7], splits[i]) for i in range(count)
+    ]
+    small = None
+    if with_small:
+        small = Small(place, refs[count], refs[ins + count], *scratch[7 * count :])
+    for i in range(4):
+        for plan in plans:
+            plan.start_group(i)
+    if small:
+        small.go(0)
+    for k in range(4):
+        for plan in plans:
+            plan.corner(k)
+    if small:
+        small.go(1)
+    for k in range(4):
+        for plan in plans:
+            plan.sides(k)
+        if small and k % 2 == 1:
+            small.go(2 + k // 2)
+    for k in range(4):
+        for plan in plans:
+            plan.mine(k)
+    if small:
+        small.go(4)
+    for plan in plans:
+        plan.result()
+    if small:
+        small.go(5)
+    for plan in plans:
+        plan.drain()
+
+
+def scatter(bigs, splits, small, collective_id):
+    count = len(bigs)
+    spec = pl.BlockSpec(memory_space=pl.ANY)
+    vmem = pl.BlockSpec(memory_space=pltpu.VMEM)
+    shapes = [(b.shape[0] // 32, b.shape[1]) for b in bigs]
+    extra = [] if small is None else [small]
+    scratch = sum([Scatter.scratch(s[0], s[1], sp) for s, sp in zip(shapes, splits)], [])
+    if small is not None:
+        scratch = scratch + Small.scratch(small.shape)
+    return pl.pallas_call(
+        functools.partial(scatter_kernel, splits, small is not None),
+        in_specs=[spec] * count + [vmem] * len(extra),
+        out_specs=[vmem] * (count + len(extra)),
+        out_shape=[jax.ShapeDtypeStruct(s, f32) for s in shapes]
+        + [jax.ShapeDtypeStruct(e.shape, f32) for e in extra],
+        scratch_shapes=scratch,
+        compiler_params=pltpu.CompilerParams(
+            collective_id=collective_id, has_side_effects=True, vmem_limit_bytes=60 * 1024 * 1024
+        ),
+    )(*bigs, *extra)
+
+
+def own_kernels():
+    return lax.axis_size("dp") == 4 and lax.axis_size("seq") == 8
+
+
+def gather_rows(shards, splits, collective_id):
+    if own_kernels():
+        return gather(shards, splits, collective_id)
+    return [lax.all_gather(s, ("dp", "seq"), axis=0, tiled=True) for s in shards]
+
+
+def scatter_rows(bigs, splits, small, collective_id):
+    if own_kernels():
+        return scatter(bigs, splits, small, collective_id)
+    outs = [lax.psum_scatter(b, ("dp", "seq"), scatter_dimension=0, tiled=True).astype(f32) for b in bigs]
+    return outs + ([] if small is None else [lax.psum(small, ("dp", "seq"))])
+
+
+def half_of(width):
+    return (width // 2 + 127) // 128 * 128
+
+
 def grouped(cols, groups):
     batch, span, heads = cols.shape
     return jnp.transpose(cols.reshape(batch, span, groups, heads // groups), (2, 0, 1, 3))
@@ -646,9 +1161,17 @@
     resid_wide = resid_in.astype(f32)
     rs = rs_ext[:, HALO:]
 
-    full_in = lax.all_gather(in_proj, ("dp", "seq"), axis=0, tiled=True)
-    full_dt = lax.all_gather(dt_proj, ("dp", "seq"), axis=0, tiled=True)
-    full_out = lax.all_gather(out_proj, ("dp", "seq"), axis=0, tiled=True)
+    conv_cols = in_proj.shape[1] - inner
+    dt_pad = (-(conv_cols + heads)) % 128
+    conv_shard = jnp.concatenate(
+        [in_proj[:, inner:], dt_proj, jnp.zeros((in_proj.shape[0], dt_pad), bf16)], axis=1
+    )
+    conv_all = conv_cols + heads + dt_pad
+    (full_conv,) = gather_rows([conv_shard], [half_of(conv_all)], 3)
+    full_gate, full_out = gather_rows(
+        [in_proj[:, :inner], out_proj], [half_of(inner), half_of(width)], 4
+    )
+    full_dt = full_conv[:, conv_cols : conv_cols + heads]
 
     dt_raw = jnp.dot(x_ext[:, HALO:], full_dt, preferred_element_type=f32)
     step = jax.nn.softplus(dt_raw + dt_bias)
@@ -665,13 +1188,13 @@
 
     cw_keys, cb_keys = conv_weight[:, inner:], conv_bias[None, inner:]
     cw_vals, cb_vals = conv_weight[:, :inner], conv_bias[None, :inner]
-    keys, cin_keys = keys_forward(x2, full_in, 2 * inner // (2 * n), cw_keys, cb_keys, batch, span)
+    keys, cin_keys = keys_forward(x2, full_conv, inner // (2 * n), cw_keys, cb_keys, batch, span)
     v, cin_vals, local = values_forward(
-        x2, full_in, inner // cb_w, cw_vals, cb_vals, keys, colpack, hw, span
+        x2, full_conv, 0, cw_vals, cb_vals, keys, colpack, hw, span
     )
     carried = chain(local, decay_wide, False, 1)
     y, gate, normed_out, rg = rows_forward(
-        x_ext, full_in, v, keys, colpack, rowpack, carried, skip_wide, gain_wide, hw, span
+        x_ext, full_gate, v, keys, colpack, rowpack, carried, skip_wide, gain_wide, hw, span
     )
     mixer_out = jnp.dot(normed_out, full_out, preferred_element_type=f32)
     output = (mask * (resid_wide + mixer_out)).astype(bf16)
@@ -707,12 +1230,12 @@
     cig = jnp.concatenate([cig_vals, cig_keys], axis=-1)
     grad_conv = jnp.einsum("bsd,bse->de", x_ext, cig, preferred_element_type=f32)
     grad_dt = jnp.einsum("bsd,bsh->dh", x_rows, step_low, preferred_element_type=f32)
-    normed_ext = jnp.einsum("bse,de->bsd", cig, full_in[:, inner:], preferred_element_type=f32)
+    normed_ext = jnp.einsum("bse,de->bsd", cig, full_conv[:, :conv_cols], preferred_element_type=f32)
     from_next = shifted(normed_ext[:, :HALO].astype(bf16), "seq", -1).astype(f32)
     normed_grad = normed_ext[:, HALO:]
     normed_grad = jnp.concatenate([normed_grad[:, : span - HALO], normed_grad[:, span - HALO :] + from_next], axis=1)
     normed_grad = normed_grad + jnp.einsum(
-        "bse,de->bsd", dgate, full_in[:, :inner], preferred_element_type=f32
+        "bse,de->bsd", dgate, full_gate, preferred_element_type=f32
     )
     normed_grad = normed_grad + jnp.einsum("bsh,dh->bsd", step_low, full_dt, preferred_element_type=f32)
     nz = resid_wide * rs
@@ -720,29 +1243,41 @@
     grad_norm = jnp.sum(normed_grad * nz, axis=(0, 1))
     input_grad = mixer_grad.astype(f32) + rs * (fg - nz * jnp.mean(fg * nz, axis=-1, keepdims=True))
 
-    big = jnp.concatenate([grad_gate, grad_conv, grad_dt], axis=1).astype(bf16)
-    sum_in = lax.psum_scatter(big, ("dp", "seq"), scatter_dimension=0, tiled=True).astype(f32)
-    sum_out = lax.psum_scatter(grad_out.astype(bf16), ("dp", "seq"), scatter_dimension=0, tiled=True).astype(f32)
-    small = lax.psum(
-        (
-            grad_norm,
-            jnp.concatenate([dcw_vals, dcw_keys], axis=1),
-            jnp.concatenate([dcb_vals, dcb_keys], axis=1)[0],
-            grad_bias,
-            grad_a,
-            dskip[0].reshape(heads, hw).sum(-1),
-            dgain[0],
-        ),
-        ("dp", "seq"),
+    grad_conv = jnp.concatenate([grad_conv, grad_dt, jnp.zeros((width, dt_pad), f32)], axis=1)
+    pieces = (
+        grad_norm,
+        jnp.concatenate([dcw_vals, dcw_keys], axis=1),
+        jnp.concatenate([dcb_vals, dcb_keys], axis=1)[0],
+        dgain[0],
+        grad_bias,
+        grad_a,
+        dskip[0].reshape(heads, hw).sum(-1),
     )
-    proj = in_proj.shape[1]
+    flat = jnp.concatenate([p.reshape(-1) for p in pieces])
+    small = jnp.pad(flat, (0, (-flat.size) % 1024)).reshape(-1, 128)
+    sum_gate, sum_out = scatter_rows(
+        [grad_gate.astype(bf16), grad_out.astype(bf16)], [half_of(inner), half_of(width)], None, 5
+    )
+    sum_conv, small = scatter_rows([grad_conv.astype(bf16)], [half_of(conv_all)], small, 6)
+    flat, sums, at = small.reshape(-1), [], 0
+    for p in pieces:
+        sums.append(flat[at : at + p.size].reshape(p.shape))
+        at += p.size
+    sum_norm, sum_cw, sum_cb, sum_gain, sum_bias, sum_a, sum_skip = sums
     return (
         output,
         input_grad.astype(bf16),
-        sum_in[:, :proj],
-        sum_in[:, proj:],
+        jnp.concatenate([sum_gate, sum_conv[:, :conv_cols]], axis=1),
+        sum_conv[:, conv_cols : conv_cols + heads],
         sum_out,
-    ) + tuple(small)
+        sum_norm,
+        sum_cw,
+        sum_cb,
+        sum_bias,
+        sum_a,
+        sum_skip,
+        sum_gain,
+    )
 
 
 def solution(mesh):

time: 932 us -> 743 us (0.80)
  waiting for transfers between devices: 369 us -> 0.01 us
  Pallas kernels: 301 us -> 548 us
  blocking collectives: 46.7 us -> 0 us
  other arithmetic: 43.5 us -> 17.4 us
  local copies, waits for them, and re-layouts: 60.8 us -> 83 us
  between operations: 14.7 us -> 1.8 us
    pallas_call x0 -> x4, Pallas kernels: none -> 292 us  [the longest x2 155 us: scatter(): pl.pallas_call(functools.partial(scatter_kernel, splits, small is not Non...]
    reduce_scatter x2 -> x0, waiting for transfers between devices: 167 us -> none  [the longest x1 167 us: on_device(): lax.psum_scatter(big, ('dp', 'seq'), scatter_dimension=0, tiled=True)]
    psum x1 -> x0, waiting for transfers between devices: 126 us -> none  [on_device(): lax.psum((grad_norm, jnp.concatenate([dcw_vals, dcw_keys], axis=1), jnp.c...]
    all_gather x2 -> x0, waiting for transfers between devices: 75.1 us -> none  [the longest x1 60.3 us: on_device(): full_in = lax.all_gather(in_proj, ('dp', 'seq'), axis=0, tiled=True)]
    all_gather x1 -> x0, blocking collectives: 46.7 us -> none  [on_device(): full_dt = lax.all_gather(dt_proj, ('dp', 'seq'), axis=0, tiled=True)]
    pallas_call x2, Pallas kernels: 125 us -> 81.5 us  [chain(): pl.pallas_call(functools.partial(chain_kernel, backward, size), in_specs=...]
    concatenate x0 -> x3, local copies, waits for them, and re-layouts: none -> 17.6 us  [the longest x1 16 us: on_device(): jnp.concatenate([grad_conv, grad_dt, jnp.zeros((width, dt_pad), f32)], ax...]
    concatenate x1, other arithmetic: 17.7 us -> 1.11 us  [on_device(): jnp.concatenate([sum_gate, sum_conv[:, :conv_cols]], axis=1)]
  transfers between devices with their start and end apart: 7 -> 2, of which waited for: 4 -> 0; matrix products, arithmetic and copies ran while one was open for 14% -> 4% of each run, Pallas kernels for 33% -> 30%
where the time goes in v2:
time: 743 us; the launch traced here: 734 us
  Pallas kernels  548 us (74%)
  local copies, waits for them, and re-layouts  83 us (11%)
  matrix products  79.8 us (11%)
  other arithmetic  17.4 us (2%)
    pallas_call x2, Pallas kernels, scatter(): pl.pallas_call(functools.partial(scatter_kernel, splits, small is not Non...  155 us
    pallas_call x2, Pallas kernels, gather(): pl.pallas_call(functools.partial(gather_kernel, splits), in_specs=[spec]...  137 us
    pallas_call x2, Pallas kernels, chain(): pl.pallas_call(functools.partial(chain_kernel, backward, size), in_specs=...  81.5 us
    pallas_call x1, Pallas kernels, gate_backward(): pl.pallas_call(functools.partial(gate_back_kernel, span, hw), grid=(group...  58.1 us
    pallas_call x1, Pallas kernels, state_backward(): pl.pallas_call(functools.partial(state_back_kernel, span, hw), grid=(grou...  51.7 us
    pallas_call x1, Pallas kernels, rows_forward(): pl.pallas_call(functools.partial(out_kernel, span, hw), grid=(groups, bat...  37.5 us
    unnamed x102, local copies, waits for them, and re-layouts  26.2 us
    pallas_call x1, Pallas kernels, values_forward(): pl.pallas_call(functools.partial(values_kernel, span, hw), grid=(groups,)...  23.8 us
  transfers between devices with their start and end apart: 2, of which 0 were waited for; matrix products, arithmetic and copies ran while one was open for 4% of the time, Pallas kernels for 30%

profile of v2, /device:TPU:0, one launch (start us, length us, event | category | flops | bytes accessed | tf_op | source)
XLA Modules:
  0.0 733.5 jit_solution(5708696981712172701)
XLA Ops:
  11.1 54.3 %shard_map.221.w_ref = bf16[1536,3456]{1,0:T(8,128)(2,1)} custom-call(bf16[48,3456]{1,0:T(8,128)(2,1)} %concatenate.35.refs_0_), custom_call_target="tpu_custom_call" | custom-call | tf_op jit(solution)/shard_map/pallas_call | solution.py:834
  66.3 82.4 %shard_map.220 = (bf16[1536,3072]{1,0:T(8,128)(2,1)}, bf16[3072,1536]{1,0:T(8,128)(2,1)}) custom-call(bf16[48,3072]{1,0:T(8,128)(2,1)} %slice.100.refs_0_, bf16[96,1536]{1,0:T(8,128)(2,1)} %refs_1_.1), custom_call_target="tpu_custom_call" | custom-call | tf_op jit(solution)/shard_map/pallas_call | solution.py:834
  162.8 4.5 pad_maximum_fusion.col_ref
  170.7 23.8 %shard_map.223 = (bf16[3,256,3072]{2,1,0:T(8,128)(2,1)}, bf16[3,272,3072]{2,1,0:T(8,128)(2,1)}, f32[3,128,3072]{2,1,0:T(8,128)}) custom-call(bf16[816,1536]{1,0:T(8,128)(2,1)} %copy-done.2, bf16[1536,3456]{1,0:T(8,128)(2,1)} %shard_map.221.w_ref, f32[4,3072]{1,0:T(4,128)S(1)} %slice.102.cw_ref, f32[1,3072]{1,0:T(1,128)S(1)} %bitcast.125, ...), custom_call_target="tpu_custom_call" | custom-call | tf_op jit(solution)/shard_map/pallas_call | solution.py:137
  196.9 5.3 shard_map.224.h_ref
  204.4 37.5 %shard_map.225 = (f32[3,256,3072]{2,1,0:T(8,128)}, bf16[3,256,3072]{2,1,0:T(8,128)(2,1)}, bf16[3,256,3072]{2,1,0:T(8,128)(2,1)}, f32[3,256,8]{2,1,0:T(8,128)}) custom-call(bf16[3,272,1536]{2,1,0:T(8,128)(2,1)} %copy-done.22, bf16[1536,3072]{1,0:T(8,128)(2,1)} %get-tuple-element.44.w_ref, bf16[3,256,3072]{2,1,0:T(8,128)(2,1)} %get-tuple-element.46.v_ref, ...), custom_call_target="tpu_custom_call" | custom-call | tf_op jit(solution)/shard_map/pallas_call | solution.py:302
  241.9 13.4 %fusion.18 = (f32[3,256]{1,0:T(4,128)S(1)}, bf16[3,256,1536]{2,1,0:T(8,128)(2,1)}, bf16[3,256,1536]{2,1,0:T(8,128)(2,1)}) fusion(bf16[3,256,1536]{2,1,0:T(8,128)(2,1)S(1)} %copy-done.33, f32[3,256]{1,0:T(4,128)S(1)} %compare_convert_fusion, bf16[3,256,1536]{2,1,0:T(8,128)(2,1)S(1)} %copy-done.20, bf16[3,256,3072]{2,1,0:T(8,128)(2,1)} %get-tuple-element.48, ...), kind=kOutput, calls=%fused_computation.28 | convolution fusion | flops 7259552768 | bytes 23599104 | tf_op jit(solution)/shard_map/dot_general | solution.py:1199
  256.8 58.1 %shard_map.226 = (bf16[3,256,3072]{2,1,0:T(8,128)(2,1)}, bf16[3,256,3072]{2,1,0:T(8,128)(2,1)}, f32[3,128,3072]{2,1,0:T(8,128)}, f32[6,3,256,16]{3,2,1,0:T(8,128...) custom-call(bf16[3,256,1536]{2,1,0:T(8,128)(2,1)} %get-tuple-element, ...), custom_call_target="tpu_custom_call" | custom-call | tf_op jit(solution)/shard_map/pallas_call | solution.py:427
  316.3 3.2 copy-done.8
  319.5 76.2 %shard_map.227.later_ref = f32[3,128,3072]{2,1,0:T(8,128)S(1)} custom-call(f32[3,128,3072]{2,1,0:T(8,128)S(1)} %copy-done.8, f32[3,1,3072]{2,1,0:T(1,128)S(1)} %broadcast_in_dim_reshape.6.decay_ref), custom_call_target="tpu_custom_call" | custom-call | tf_op jit(solution)/shard_map/pallas_call | solution.py:221
  398.0 51.7 %shard_map.228 = (bf16[3,272,3072]{2,1,0:T(8,128)(2,1)}, f32[6,3,256,8]{3,2,1,0:T(8,128)S(1)}, f32[3,256,128]{2,1,0:T(8,128)S(1)}, f32[4,3072]{1,0:T(4,128)S(1)}...) custom-call(f32[3,128,3072]{2,1,0:T(8,128)} %copy-done.3, f32[3,128,3072]{2,1,0:T(8,128)} %copy-done, ...), custom_call_target="tpu_custom_call" | custom-call | tf_op jit(solution)/shard_map/pallas_call | solution.py:548
  449.8 6.0 constant_dynamic-update-slice_fusion.1
  458.6 10.6 %fusion = f32[3,272,1536]{2,1,0:T(8,128)S(1)} fusion(bf16[3,272,3328]{2,1,0:T(8,128)(2,1)} %constant_dynamic-update-slice_fusion, bf16[1536,3456]{1,0:T(8,128)(2,1)S(1)} %bitcast.123), kind=kOutput, calls=%fused_computation.3 | convolution fusion | flops 8342470656 | bytes 20668416 | tf_op jit(solution)/shard_map/bse,de->bsd/dot_general | solution.py:1233
  474.5 16.6 %bitcast_convert_fusion = bf16[1536,3328]{1,0:T(8,128)(2,1)} fusion(bf16[3,272,1536]{2,1,0:T(8,128)(2,1)S(1)} %copy-done.23, bf16[3,272,3328]{2,1,0:T(8,128)(2,1)} %constant_dynamic-update-slice_fusion), kind=kOutput, calls=%fused_computation | convolution fusion | flops 8347582464 | bytes 18161664 | tf_op jit(solution)/shard_map/bsd,bse->de/dot_general | solution.py:1231
  491.1 9.2 %fusion.3 = f32[3,256,1536]{2,1,0:T(8,128)} fusion(bf16[3,256,3072]{2,1,0:T(8,128)(2,1)S(1)} %bitcast.145, bf16[1536,3072]{1,0:T(8,128)(2,1)S(1)} %bitcast.135), kind=kOutput, calls=%fused_computation.6 | convolution fusion | flops 7247757312 | bytes 18874368 | tf_op jit(solution)/shard_map/bse,de->bsd/dot_general | solution.py:1237
  500.3 9.6 %bitcast_convert_fusion.2.refs_0_ = bf16[1536,3072]{1,0:T(8,128)(2,1)} fusion(bf16[3,256,3072]{2,1,0:T(8,128)(2,1)S(1)} %bitcast.145, bf16[3,272,1536]{2,1,0:T(8,128)(2,1)S(1)} %copy-done.23), kind=kOutput, calls=%fused_computation.2 | convolution fusion | flops 7252475904 | bytes 16515072 | tf_op jit(solution)/shard_map/bsd,bse->de/dot_general | solution.py:1229
  509.9 9.8 %bitcast_convert_fusion.1.refs_1_ = bf16[3072,1536]{1,0:T(8,128)(2,1)} fusion(bf16[3,256,3072]{2,1,0:T(8,128)(2,1)S(1)} %bitcast.143, bf16[3,256,1536]{2,1,0:T(8,128)(2,1)S(1)} %copy-done.25), kind=kOutput, calls=%fused_computation.1 | convolution fusion | flops 7252475904 | bytes 16515072 | tf_op jit(solution)/shard_map/bsi,bsd->id/dot_general | solution.py:1205
  522.3 3.1 slice_bitcast_fusion.1
  525.4 3.1 copy.83
  537.3 85.5 %shard_map.230 = (f32[48,3072]{1,0:T(8,128)}, f32[96,1536]{1,0:T(8,128)}) custom-call(bf16[1536,3072]{1,0:T(8,128)(2,1)} %bitcast_convert_fusion.2.refs_0_, bf16[3072,1536]{1,0:T(8,128)(2,1)} %bitcast_convert_fusion.1.refs_1_), custom_call_target="tpu_custom_call" | custom-call | tf_op jit(solution)/shard_map/pallas_call | solution.py:1097
  622.9 16.0 %concatenate.40.refs_0_ = bf16[1536,3456]{1,0:T(8,128)(2,1)} concatenate(bf16[1536,3328]{1,0:T(8,128)(2,1)} %bitcast_convert_fusion, bf16[1536,48]{1,0:T(8,128)(2,1)} %copy.91, bf16[1536,80]{1,0:T(8,128)(2,1)S(1)} %broadcast_in_dim.44), dimensions={1} | concatenate | bytes 21233664 | tf_op jit(solution)/shard_map/concatenate | solution.py:1246
  640.0 6.5 fusion.15
  647.1 69.8 %shard_map.231 = (f32[48,3456]{1,0:T(8,128)}, f32[168,128]{1,0:T(8,128)}) custom-call(bf16[1536,3456]{1,0:T(8,128)(2,1)} %concatenate.40.refs_0_, f32[168,128]{1,0:T(8,128)} %pad_bitcast_fusion.refs_1_), custom_call_target="tpu_custom_call" | custom-call | tf_op jit(solution)/shard_map/pallas_call | solution.py:1097
  726.2 4.9 fusion.19
  (184 shorter events, 70.6 us)
Async XLA Ops:
  1.6 147.2 %collective-permute-start = (bf16[3,16,1536]{2,1,0:T(8,128)(2,1)S(1)}, bf16[3,16,1536]{2,1,0:T(8,128)(2,1)S(1)}, u32[]{:S(2)}, u32[]{:S(2)}) collective-permute-start(bf16[3,16,1536]{2,1,0:T(8,128)(2,1)S(1)} %slice.99), channel_id=1, source_target_pairs={{0,1},{1,2},{2,3},{3,4},{4,5},{5,6},{6,7},{8,9},{9,10},{10,11},{11... | collective-permute-start | bytes 442376 | tf_op jit(solution)/shard_map/ppermute | solution.py:35
  11.1 54.4 %copy-start.31 = (f32[48]{0:T(128)S(1)}, f32[48]{0:T(128)}, u32[]{:S(2)}) copy-start(f32[48]{0:T(128)} %param.23) | copy-start | bytes 580
  11.1 55.1 %copy-start.32 = (s32[3]{0:T(128)S(1)}, s32[3]{0:T(128)}, u32[]{:S(2)}) copy-start(s32[3]{0:T(128)} %param.15) | copy-start | bytes 40
  11.1 137.7 %copy-start.35 = (f32[48]{0:T(128)S(1)}, f32[48]{0:T(128)}, u32[]{:S(2)}) copy-start(f32[48]{0:T(128)} %param.22) | copy-start | bytes 580
  11.1 137.7 %copy-start.20 = (bf16[3,256,1536]{2,1,0:T(8,128)(2,1)S(1)}, bf16[3,256,1536]{2,1,0:T(8,128)(2,1)}, u32[]{:S(2)}) copy-start(bf16[3,256,1536]{2,1,0:T(8,128)(2,1)} %param.13) | copy-start | bytes 7077892
  11.1 138.4 %copy-start.30 = (f32[1536]{0:T(1024)S(1)}, f32[1536]{0:T(1024)}, u32[]{:S(2)}) copy-start(f32[1536]{0:T(1024)} %param.16) | copy-start | bytes 18436
  65.4 86.3 %copy-start.34 = (f32[48]{0:T(128)S(1)}, f32[48]{0:T(128)}, u32[]{:S(2)}) copy-start(f32[48]{0:T(128)} %param.21) | copy-start | bytes 580
  168.8 25.8 %copy-start.6 = (bf16[3,256,256]{2,1,0:T(8,128)(2,1)}, bf16[3,256,256]{2,1,0:T(8,128)(2,1)S(1)}, u32[]{:S(2)}) copy-start(bf16[3,256,256]{2,1,0:T(8,128)(2,1)S(1)} %get-tuple-element.45.keys_ref) | copy-start | bytes 1179652
  168.8 25.8 %copy-start.12 = (bf16[3,272,256]{2,1,0:T(8,128)(2,1)}, bf16[3,272,256]{2,1,0:T(8,128)(2,1)S(1)}, u32[]{:S(2)}) copy-start(bf16[3,272,256]{2,1,0:T(8,128)(2,1)S(1)} %get-tuple-element.60.cin_ref) | copy-start | bytes 1253380
  204.4 37.5 %copy-start.33 = (bf16[3,256,1536]{2,1,0:T(8,128)(2,1)S(1)}, bf16[3,256,1536]{2,1,0:T(8,128)(2,1)}, u32[]{:S(2)}) copy-start(bf16[3,256,1536]{2,1,0:T(8,128)(2,1)} %param.14) | copy-start | bytes 7077892
  316.3 79.4 %copy-start.4 = (f32[6,3,256,16]{3,2,1,0:T(8,128)}, f32[6,3,256,16]{3,2,1,0:T(8,128)S(1)}, u32[]{:S(2)}) copy-start(f32[6,3,256,16]{3,2,1,0:T(8,128)S(1)} %get-tuple-element.63) | copy-start | bytes 884740
  319.5 139.1 %slice-start.3 = ((s8[10616832]{0:T(1024)(128)(4,1)}), s8[4194304]{0:T(1024)(128)(4,1)S(1)}, s32[]{:S(2)}) async-start(s8[10616832]{0:T(1024)(128)(4,1)} %bitcast.122), calls=%async_computation.3 | async-start | bytes 8388608
  398.0 60.6 %slice-start.4 = ((s8[10616832]{0:T(1024)(128)(4,1)}), s8[4194304]{0:T(1024)(128)(4,1)S(1)}, s32[]{:S(2)}) async-start(s8[10616832]{0:T(1024)(128)(4,1)} %bitcast.122), calls=%async_computation.4 | async-start | bytes 8388608
  398.0 60.6 %slice-start.5 = ((s8[10616832]{0:T(1024)(128)(4,1)}), s8[2228224]{0:T(1024)(128)(4,1)S(1)}, s32[]{:S(2)}) async-start(s8[10616832]{0:T(1024)(128)(4,1)} %bitcast.122), calls=%async_computation.5 | async-start | bytes 4456448
  471.9 19.2 %slice-start.6 = ((s8[9437184]{0:T(1024)(128)(4,1)}), s8[4194304]{0:T(1024)(128)(4,1)S(1)}, s32[]{:S(2)}) async-start(s8[9437184]{0:T(1024)(128)(4,1)} %bitcast.134), calls=%async_computation.6 | async-start | bytes 8388608
  471.9 19.2 %slice-start.11 = ((s8[4718592]{0:T(1024)(128)(4,1)}), s8[4194304]{0:T(1024)(128)(4,1)S(1)}, s32[]{:S(2)}) async-start(s8[4718592]{0:T(1024)(128)(4,1)} %bitcast.144), calls=%async_computation.11 | async-start | bytes 8388608
  474.4 16.6 %slice-start.7 = ((s8[9437184]{0:T(1024)(128)(4,1)}), s8[4194304]{0:T(1024)(128)(4,1)S(1)}, s32[]{:S(2)}) async-start(s8[9437184]{0:T(1024)(128)(4,1)} %bitcast.134), calls=%async_computation.7 | async-start | bytes 8388608
  474.5 16.6 %slice-start.8 = ((s8[9437184]{0:T(1024)(128)(4,1)}), s8[1048576]{0:T(1024)(128)(4,1)S(1)}, s32[]{:S(2)}) async-start(s8[9437184]{0:T(1024)(128)(4,1)} %bitcast.134), calls=%async_computation.8 | async-start | bytes 2097152
  474.5 16.6 %slice-start.12 = ((s8[4718592]{0:T(1024)(128)(4,1)}), s8[524288]{0:T(1024)(128)(4,1)S(1)}, s32[]{:S(2)}) async-start(s8[4718592]{0:T(1024)(128)(4,1)} %bitcast.144), calls=%async_computation.12 | async-start | bytes 1048576
  474.5 35.5 %slice-start.9 = ((s8[4718592]{0:T(1024)(128)(4,1)}), s8[4194304]{0:T(1024)(128)(4,1)S(1)}, s32[]{:S(2)}) async-start(s8[4718592]{0:T(1024)(128)(4,1)} %bitcast.142), calls=%async_computation.9 | async-start | bytes 8388608
  491.1 18.8 %slice-start.10 = ((s8[4718592]{0:T(1024)(128)(4,1)}), s8[524288]{0:T(1024)(128)(4,1)S(1)}, s32[]{:S(2)}) async-start(s8[4718592]{0:T(1024)(128)(4,1)} %bitcast.142), calls=%async_computation.10 | async-start | bytes 1048576
  531.5 107.4 %collective-permute-start.1 = (bf16[3,16,1536]{2,1,0:T(8,128)(2,1)}, bf16[3,16,1536]{2,1,0:T(8,128)(2,1)}, u32[]{:S(2)}, u32[]{:S(2)}) collective-permute-start(bf16[3,16,1536]{2,1,0:T(8,128)(2,1)} %slice.173), channel_id=1, source_target_pairs={{1,0},{2,1},{3,2},{4,3},{5,4},{6,5},{7,6},{9,8},{10,9},{11,10},{12... | collective-permute-start | bytes 442376 | tf_op jit(solution)/shard_map/ppermute | solution.py:35
  622.9 16.0 %copy-start.36 = (f32[48]{0:T(128)S(1)}, f32[48]{0:T(128)}, u32[]{:S(2)}) copy-start(f32[48]{0:T(128)} %param.22) | copy-start | bytes 580
  622.9 17.1 %copy-start.21 = (bf16[3,256,1536]{2,1,0:T(8,128)(2,1)S(1)}, bf16[3,256,1536]{2,1,0:T(8,128)(2,1)}, u32[]{:S(2)}) copy-start(bf16[3,256,1536]{2,1,0:T(8,128)(2,1)} %param.13) | copy-start | bytes 7077892
  (28 other events, 173.4 us)

commit v3 on v2

v3 whole, which is shorter than its diff:
```python
import functools

import jax
import jax.numpy as jnp
from jax import lax
from jax.experimental import pallas as pl
from jax.experimental.pallas import tpu as pltpu
from jax.sharding import PartitionSpec as P

epsilon = 1e-05
highest = lax.Precision.HIGHEST
HALO = 16
HEADS = 8
LOG2E = 1.4426950408889634
f32 = jnp.float32
bf16 = jnp.bfloat16
MESH = pl.DeviceIdType.MESH


def mm(a, b):
    return lax.dot_general(a, b, (((1,), (0,)), ((), ())), preferred_element_type=f32)


def mm_nt(a, b):
    return lax.dot_general(a, b, (((1,), (1,)), ((), ())), preferred_element_type=f32)


def mm_tn(a, b):
    return lax.dot_general(a, b, (((0,), (0,)), ((), ())), preferred_element_type=f32)


def shifted(block, axis, distance):
    devices = range(lax.axis_size(axis))
    route = [(i - distance, i) for i in devices if i - distance in devices]
    return lax.ppermute(block, axis, route)


def spread(cols, width):
    rows, heads = cols.shape
    low_half = lax.broadcasted_iota(jnp.int32, (rows, 2 * width), 1) < width
    pairs = [
        jnp.where(low_half, cols[:, i : i + 1], cols[:, i + 1 : i + 2]) for i in range(0, heads, 2)
    ]
    return jnp.concatenate(pairs, axis=1)


def gather_heads(x, width):
    rows, total = x.shape
    low_half = lax.broadcasted_iota(jnp.int32, (rows, 2 * width), 1) < width
    head_lane = lax.broadcasted_iota(jnp.int32, (rows, total // width), 1)
    out = jnp.zeros((rows, total // width), f32)
    for i in range(total // (2 * width)):
        pair = x[:, i * 2 * width : (i + 1) * 2 * width]
        one = jnp.sum(jnp.where(low_half, pair, 0.0), axis=1, keepdims=True)
        two = jnp.sum(jnp.where(low_half, 0.0, pair), axis=1, keepdims=True)
        out = jnp.where(head_lane == 2 * i, one, out)
        out = jnp.where(head_lane == 2 * i + 1, two, out)
    return out


def silu_parts(v):
    sg = 1.0 / (1.0 + jnp.exp(-v))
    return v * sg, sg


def conv_pre(a, cw, cb, span):
    first = HALO - (cw.shape[0] - 1)
    out = cb
    for k in range(cw.shape[0]):
        out = out + cw[k : k + 1] * a[first + k : first + k + span]
    return out


def params_of(limit_mb, dims=None):
    return pltpu.CompilerParams(vmem_limit_bytes=limit_mb * 1024 * 1024, dimension_semantics=dims)


def causal(span, transposed):
    one = lax.broadcasted_iota(jnp.int32, (span, span), 0)
    two = lax.broadcasted_iota(jnp.int32, (span, span), 1)
    return (one <= two) if transposed else (one >= two)


class Place:
    def __init__(self):
        self.dp = lax.axis_index("dp")
        self.seq = lax.axis_index("seq")
        y, x = self.dp // 2, self.dp % 2
        self.z, self.core = self.seq // 2, self.seq % 2
        self.dx = 2 * y + (1 - x)
        self.dy = 2 * (1 - y) + x
        self.dxy = 2 * (1 - y) + (1 - x)
        self.to_x = (self.dx, self.seq)
        self.to_y = (self.dy, self.seq)
        self.to_core = (self.dp, 2 * self.z + 1 - self.core)
        self.to_up = (self.dp, 2 * jnp.minimum(self.z + 1, 3) + self.core)
        self.to_down = (self.dp, 2 * jnp.maximum(self.z - 1, 0) + self.core)
        self.to_across = (self.dp, 2 * jnp.where(self.z < 2, self.z + 2, self.z - 2) + self.core)
        self.has_up = self.z < 3
        self.has_down = self.z > 0

    def near(self, k):
        z = self.z
        return (z, z + 1 - 2 * (z % 2), jnp.where(z < 2, 2, 1), jnp.where(z < 2, 3, 0))[k]

    def greet(self, others=()):
        barrier = pltpu.get_barrier_semaphore()
        for device in (self.to_x, self.to_y, self.to_core) + tuple(others):
            pl.semaphore_signal(barrier, inc=1, device_id=device, device_id_type=MESH)

        @pl.when(self.has_up)
        def _():
            pl.semaphore_signal(barrier, inc=1, device_id=self.to_up, device_id_type=MESH)

        @pl.when(self.has_down)
        def _():
            pl.semaphore_signal(barrier, inc=1, device_id=self.to_down, device_id_type=MESH)

        ends = self.has_up.astype(jnp.int32) + self.has_down.astype(jnp.int32)
        pl.semaphore_wait(barrier, 3 + len(others) + ends)


GATHER_KINDS = 11


def gather_steps(place, shard, full, split, own_sem, send, recv):
    rows, width = full.shape[0] // 32, full.shape[1]
    z, core = place.z, place.core
    every, left, right = pl.ds(0, width), pl.ds(0, split), pl.ds(split, width - split)
    two = split < width

    def view(d, zz, cc, cols):
        start = pl.multiple_of((d * 8 + zz * 2 + cc) * rows, 16)
        return full.at[pl.ds(start, rows), cols]

    def copy(kind, slot, device, d, zz, cc, cols, src=None):
        dst = view(d, zz, cc, cols)
        return pltpu.make_async_remote_copy(
            src_ref=dst if src is None else src,
            dst_ref=dst,
            send_sem=send.at[kind, slot],
            recv_sem=recv.at[kind, slot],
            device_id=device,
            device_id_type=MESH,
        )

    def pieces(k):
        zk = place.near(k)
        src = shard if k == 0 else None
        dp = place.dp
        return dict(
            x=copy(2, k, place.to_x, dp, zk, core, every, src),
            y=copy(3, k, place.to_y, dp, zk, core, every, src),
            own=copy(6, k, place.to_core, dp, zk, core, every, src),
        )

    def along(k, up):
        zk = place.near(k)
        src = shard if k == 0 else None
        device = place.to_up if up else place.to_down
        dst = view(place.dp, zk, core, every)
        return pltpu.make_async_remote_copy(
            src_ref=dst if src is None else src,
            dst_ref=dst,
            send_sem=send.at[0 if up else 1, k],
            recv_sem=recv.at[0, zk],
            device_id=device,
            device_id_type=MESH,
        )

    def arrive(k):
        zk = place.near(k)
        if k > 0:
            along(k, True).wait_recv()

        @pl.when(jnp.logical_and(zk <= z, place.has_up))
        def _():
            along(k, True).start()

        @pl.when(jnp.logical_and(zk >= z, place.has_down))
        def _():
            along(k, False).start()

        made = pieces(k)
        made["x"].start()
        made["y"].start()
        made["own"].start()

    def cross(k):
        zk = place.near(k)
        return (
            copy(2, k, place.to_x, place.dx, zk, core, every),
            copy(3, k, place.to_y, place.dy, zk, core, every),
            copy(4, k, place.to_y, place.dx, zk, core, left),
            copy(5, k, place.to_x, place.dy, zk, core, right) if two else None,
            copy(7, k, place.to_core, place.dx, zk, core, every),
            copy(8, k, place.to_core, place.dy, zk, core, every),
        )

    def forward(k):
        from_x, from_y, left_on, right_on, core_x, core_y = cross(k)
        from_x.wait_recv()
        left_on.start()
        core_x.start()
        from_y.wait_recv()
        if two:
            right_on.start()
        core_y.start()

    def corner(k):
        zk = place.near(k)
        return (
            copy(4, k, place.to_y, place.dxy, zk, core, left),
            copy(5, k, place.to_x, place.dxy, zk, core, right) if two else None,
            copy(9, k, place.to_core, place.dxy, zk, core, left),
            copy(10, k, place.to_core, place.dxy, zk, core, right) if two else None,
        )

    def last(k):
        from_y, from_x, core_left, core_right = corner(k)
        from_y.wait_recv()
        core_left.start()
        if two:
            from_x.wait_recv()
            core_right.start()

    def mine():
        return pltpu.make_async_copy(shard, view(place.dp, z, core, every), own_sem)

    def begin():
        mine().start()
        arrive(0)

    def finish():
        mine().wait()
        other = 1 - core
        for k in range(4):
            zk = place.near(k)
            for kind, d, cols in (
                (6, place.dp, every), (7, place.dx, every), (8, place.dy, every),
                (9, place.dxy, left), (10, place.dxy, right),
            ):
                if kind == 10 and not two:
                    continue
                copy(kind, k, place.to_core, d, zk, other, cols).wait_recv()
        for k in range(4):
            zk = place.near(k)

            @pl.when(jnp.logical_and(zk <= z, place.has_up))
            def _():
                along(k, True).wait_send()

            @pl.when(jnp.logical_and(zk >= z, place.has_down))
            def _():
                along(k, False).wait_send()

            made = pieces(k)
            made["x"].wait_send()
            made["y"].wait_send()
            made["own"].wait_send()
            for one in cross(k)[2:] + corner(k)[2:]:
                if one is not None:
                    one.wait_send()

    return [
        begin,
        lambda: arrive(1),
        lambda: forward(0),
        lambda: arrive(2),
        lambda: forward(1),
        lambda: arrive(3),
        lambda: forward(2),
        lambda: last(0),
        lambda: forward(3),
        lambda: last(1),
        lambda: last(2),
        lambda: last(3),
        finish,
    ]


def gather_scratch():
    return [
        pltpu.SemaphoreType.DMA,
        pltpu.SemaphoreType.DMA((GATHER_KINDS, 4)),
        pltpu.SemaphoreType.DMA((GATHER_KINDS, 4)),
    ]


def part_of(ref, part):
    return ref.at[:, pl.ds(part[0], part[1])]


def gather_kernel(splits, parts, *refs):
    count = len(splits)
    shards, fulls, sems = refs[:count], refs[count : 2 * count], refs[2 * count :]
    place = Place()
    place.greet()
    plans = [
        gather_steps(place, part_of(shards[i], parts[i]), fulls[i], splits[i], *sems[3 * i : 3 * i + 3])
        for i in range(count)
    ]
    for step in zip(*plans):
        for one in step:
            one()


def gather(shards, parts, splits, collective_id):
    count = len(shards)
    spec = pl.BlockSpec(memory_space=pl.ANY)
    return pl.pallas_call(
        functools.partial(gather_kernel, splits, parts),
        in_specs=[spec] * count,
        out_specs=[spec] * count,
        out_shape=[jax.ShapeDtypeStruct((s.shape[0] * 32, p[1]), s.dtype) for s, p in zip(shards, parts)],
        scratch_shapes=gather_scratch() * count,
        compiler_params=pltpu.CompilerParams(collective_id=collective_id, has_side_effects=True),
    )(*shards)


class Scatter:
    def __init__(self, place, big, out, own, land_core, land_xy, land_z, local, send, recv, split):
        self.place, self.big, self.out = place, big, out
        self.own, self.land_core, self.land_xy, self.land_z = own, land_core, land_xy, land_z
        self.local, self.send, self.recv = local, send, recv
        self.rows, self.width = out.shape
        self.split = split
        self.left, self.right = slice(0, split), slice(split, self.width)

    def groups(self):
        p = self.place
        return (p.dxy, p.dx, p.dy, p.dp)

    def far(self, k):
        return self.place.near(3 - k)

    def source(self, d, zz, cc):
        start = pl.multiple_of((d * 8 + zz * 2 + cc) * self.rows, 16)
        return self.big.at[pl.ds(start, self.rows)]

    def remote(self, src, dst, kind, slot, device):
        return pltpu.make_async_remote_copy(
            src_ref=src, dst_ref=dst, send_sem=self.send.at[kind, slot], recv_sem=self.recv.at[kind, slot],
            device_id=device, device_id_type=MESH,
        )

    def to_other(self, i, k):
        p = self.place
        src = self.source(self.groups()[i], self.far(k), 1 - p.core)
        return self.remote(src, self.land_core.at[i, k], i, k, p.to_core)

    def load(self, i, k):
        p = self.place
        return pltpu.make_async_copy(
            self.source(self.groups()[i], self.far(k), p.core), self.own.at[i, k], self.local.at[i, k]
        )

    def start(self, k):
        for i in range(4):
            self.to_other(i, k).start()
            self.load(i, k).start()

    def join(self, i, k):
        self.load(i, k).wait()
        self.to_other(i, k).wait_recv()
        self.own[i, k] = self.own[i, k] + self.land_core[i, k]

    def side(self, kind, k):
        p = self.place
        left, right = pl.ds(0, self.split), pl.ds(self.split, self.width - self.split)
        group, cols, device = (
            (0, left, p.to_y),
            (0, right, p.to_x),
            (2, left, p.to_y),
            (1, right, p.to_x),
            (2, right, p.to_y),
            (1, left, p.to_x),
        )[kind]
        size = self.split if cols is left else self.width - self.split
        return self.remote(
            self.own.at[group, k, :, cols], self.land_xy.at[kind, k, :, pl.ds(0, size)], 4 + kind, k, device
        )

    def take(self, kind, group, cols, k):
        self.side(kind, k).wait_recv()
        size = cols.stop - cols.start
        self.own[group, k, :, cols] = self.own[group, k, :, cols] + self.land_xy[kind, k, :, 0:size]

    def corner(self, k):
        self.join(0, k)
        self.side(0, k).start()
        self.side(1, k).start()

    def sides(self, k):
        self.join(1, k)
        self.side(3, k).start()
        self.join(2, k)
        self.side(2, k).start()

    def turns(self, k):
        self.take(0, 1, self.left, k)
        self.side(5, k).start()
        self.take(1, 2, self.right, k)
        self.side(4, k).start()

    def along(self, k, up):
        p = self.place
        zk = self.far(k)
        return pltpu.make_async_remote_copy(
            src_ref=self.own.at[3, k],
            dst_ref=self.land_z.at[0 if up else 1, zk],
            send_sem=self.send.at[10, k],
            recv_sem=self.recv.at[10 if up else 11, zk],
            device_id=p.to_up if up else p.to_down,
            device_id_type=MESH,
        )

    def rising(self, k):
        return self.far(k) > self.place.z

    def behind(self, k):
        p = self.place
        rising = self.rising(k)
        return jnp.logical_or(
            jnp.logical_and(rising, p.has_down), jnp.logical_and(jnp.logical_not(rising), p.has_up)
        )

    def send_along(self, k):
        @pl.when(self.rising(k))
        def _():
            self.along(k, True).start()

        @pl.when(jnp.logical_not(self.rising(k)))
        def _():
            self.along(k, False).start()

    def mine(self, k):
        self.join(3, k)
        self.take(2, 3, self.left, k)
        self.take(3, 3, self.right, k)
        self.take(5, 3, self.left, k)
        self.take(4, 3, self.right, k)
        if k < 3:

            @pl.when(jnp.logical_not(self.behind(k)))
            def _():
                self.send_along(k)

    def line(self, k):
        zk = self.far(k)

        @pl.when(jnp.logical_and(self.behind(k), self.rising(k)))
        def _():
            self.along(k, True).wait_recv()
            self.own[3, k] = self.own[3, k] + self.land_z[0, zk]

        @pl.when(jnp.logical_and(self.behind(k), jnp.logical_not(self.rising(k))))
        def _():
            self.along(k, False).wait_recv()
            self.own[3, k] = self.own[3, k] + self.land_z[1, zk]

        @pl.when(self.behind(k))
        def _():
            self.send_along(k)

    def result(self):
        p = self.place
        self.out[...] = self.own[3, 3].astype(f32)

        @pl.when(p.has_down)
        def _():
            self.along(3, True).wait_recv()
            self.out[...] += self.land_z[0, p.z].astype(f32)

        @pl.when(p.has_up)
        def _():
            self.along(3, False).wait_recv()
            self.out[...] += self.land_z[1, p.z].astype(f32)

    def drain(self):
        for k in range(4):
            for i in range(4):
                self.to_other(i, k).wait_send()
            for kind in range(6):
                self.side(kind, k).wait_send()
            if k < 3:
                self.along(k, True).wait_send()

    def steps(self):
        start, corner, sides, turns, mine, line = (
            self.start, self.corner, self.sides, self.turns, self.mine, self.line
        )
        return [
            (0, lambda: start(0)),
            (2, lambda: start(1)),
            (3, lambda: corner(0)),
            (4, lambda: sides(0)),
            (6, lambda: start(2)),
            (8, lambda: turns(0)),
            (9, lambda: corner(1)),
            (10, lambda: sides(1)),
            (12, lambda: start(3)),
            (14, lambda: mine(0)),
            (17, lambda: turns(1)),
            (18, lambda: corner(2)),
            (19, lambda: sides(2)),
            (22, lambda: line(0)),
            (23, lambda: mine(1)),
            (26, lambda: turns(2)),
            (27, lambda: corner(3)),
            (28, lambda: sides(3)),
            (31, lambda: line(1)),
            (32, lambda: mine(2)),
            (35, lambda: turns(3)),
            (40, lambda: line(2)),
            (42, lambda: mine(3)),
            (47, self.result),
            (50, self.drain),
        ]

    @staticmethod
    def scratch(rows, width, split):
        half = max(split, width - split)
        return [
            pltpu.VMEM((4, 4, rows, width), bf16),
            pltpu.VMEM((4, 4, rows, width), bf16),
            pltpu.VMEM((6, 4, rows, half), bf16),
            pltpu.VMEM((2, 4, rows, width), bf16),
            pltpu.SemaphoreType.DMA((4, 4)),
            pltpu.SemaphoreType.DMA((11, 4)),
            pltpu.SemaphoreType.DMA((12, 4)),
        ]


class Small:
    def __init__(self, place, value, out, sent, landed, send, recv):
        p = place
        self.value, self.out, self.sent, self.landed, self.send, self.recv = value, out, sent, landed, send, recv
        pair = 2 * (p.z + 1 - 2 * (p.z % 2)) + p.core
        self.devices = (p.to_core, p.to_x, p.to_y, (p.dp, pair), p.to_across)

    def copy(self, i):
        return pltpu.make_async_remote_copy(
            src_ref=self.sent.at[i], dst_ref=self.landed.at[i], send_sem=self.send.at[i],
            recv_sem=self.recv.at[i], device_id=self.devices[i], device_id_type=MESH,
        )

    def go(self, i):
        if i == 0:
            self.sent[0] = self.value[...]
            self.copy(0).start()
            return
        self.copy(i - 1).wait_recv()
        total = self.sent[i - 1] + self.landed[i - 1]
        if i < 5:
            self.sent[i] = total
            self.copy(i).start()
        else:
            self.out[...] = total
            for k in range(5):
                self.copy(k).wait_send()

    @staticmethod
    def scratch(shape):
        return [
            pltpu.VMEM((5,) + shape, f32),
            pltpu.VMEM((5,) + shape, f32),
            pltpu.SemaphoreType.DMA((5,)),
            pltpu.SemaphoreType.DMA((5,)),
        ]


def scatter_kernel(splits, with_small, *refs):
    count = len(splits)
    ins = count + (1 if with_small else 0)
    bigs, outs = refs[:count], refs[ins : ins + count]
    scratch = refs[2 * ins :]
    place = Place()
    place.greet((place.to_across,) if with_small else ())
    plans = [
        Scatter(place, bigs[i], outs[i], *scratch[7 * i : 7 * i + 7], splits[i]) for i in range(count)
    ]
    small = None
    if with_small:
        small = Small(place, refs[count], refs[ins + count], *scratch[7 * count :])
    small_at = {0: 0, 5: 1, 9: 2, 13: 3, 17: 4, 21: 5}
    for i, steps in enumerate(zip(*[plan.steps() for plan in plans])):
        for _, step in steps:
            step()
        if small and i in small_at:
            small.go(small_at[i])


def scatter(bigs, splits, small, collective_id):
    count = len(bigs)
    spec = pl.BlockSpec(memory_space=pl.ANY)
    vmem = pl.BlockSpec(memory_space=pltpu.VMEM)
    shapes = [(b.shape[0] // 32, b.shape[1]) for b in bigs]
    extra = [] if small is None else [small]
    scratch = sum([Scatter.scratch(s[0], s[1], sp) for s, sp in zip(shapes, splits)], [])
    if small is not None:
        scratch = scratch + Small.scratch(small.shape)
    return pl.pallas_call(
        functools.partial(scatter_kernel, splits, small is not None),
        in_specs=[spec] * count + [vmem] * len(extra),
        out_specs=[vmem] * (count + len(extra)),
        out_shape=[jax.ShapeDtypeStruct(s, f32) for s in shapes]
        + [jax.ShapeDtypeStruct(e.shape, f32) for e in extra],
        scratch_shapes=scratch,
        compiler_params=pltpu.CompilerParams(
            collective_id=collective_id, has_side_effects=True, vmem_limit_bytes=60 * 1024 * 1024
        ),
    )(*bigs, *extra)


def prep_kernel(span, heads, x_ref, wk_ref, wd_ref, cw_ref, cb_ref, bias_ref, rate_ref,
                rows_ref, cin_ref, col_ref, row_ref, raw_ref, step_ref):
    batch = rows_ref.shape[0]
    ext = span + HALO
    acc = mm(x_ref[...], wk_ref[...])
    raw_all = mm(x_ref[...], wd_ref[...])
    tri = causal(span, False).astype(f32)
    for b in range(batch):
        a = acc[b * ext : (b + 1) * ext]
        row, _ = silu_parts(conv_pre(a, cw_ref[...], cb_ref[...], span))
        rows_ref[b] = row.astype(bf16)
        cin_ref[b] = a.astype(bf16)
        raw = raw_all[b * ext + HALO : (b + 1) * ext] + bias_ref[...]
        step = jnp.maximum(raw, 0.0) + jnp.log1p(jnp.exp(-jnp.abs(raw)))
        scaled = lax.dot_general(
            tri, step * rate_ref[...], (((1,), (0,)), ((), ())), precision=highest, preferred_element_type=f32
        ) * LOG2E
        raw_ref[b] = raw
        step_ref[b] = step
        turned = jnp.transpose(scaled)
        for g in range(heads // HEADS):
            some = slice(g * HEADS, (g + 1) * HEADS)
            col_ref[g, b] = jnp.concatenate([scaled[:, some], step[:, some]], axis=1)
            row_ref[g, b] = turned[some]


def prepare(x2, w_conv, key_block, w_dt, cw, cb, bias, rate, batch, span, heads):
    width = cw.shape[1]
    ext = span + HALO
    groups = heads // HEADS
    lanes = bias.shape[1]
    whole = lambda shape: pl.BlockSpec(shape, lambda i: (0,) * len(shape))
    shapes = [
        ((batch, span, width), bf16),
        ((batch, ext, width), bf16),
        ((groups, batch, span, 2 * HEADS), f32),
        ((groups, batch, HEADS, span), f32),
        ((batch, span, lanes), f32),
        ((batch, span, lanes), f32),
    ]
    return pl.pallas_call(
        functools.partial(prep_kernel, span, heads),
        grid=(1,),
        in_specs=[
            whole(x2.shape),
            pl.BlockSpec((w_conv.shape[0], width), lambda i: (0, key_block)),
            whole(w_dt.shape),
            whole(cw.shape), whole(cb.shape), whole(bias.shape), whole(rate.shape),
        ],
        out_specs=[whole(s) for s, _ in shapes],
        out_shape=[jax.ShapeDtypeStruct(s, d) for s, d in shapes],
        compiler_params=params_of(50),
    )(x2, w_conv, w_dt, cw, cb, bias, rate)


class Chain:
    def __init__(self, backward, sent, landed, send, recv):
        self.sent, self.landed, self.send, self.recv = sent, landed, send, recv
        me, count = lax.axis_index("seq"), lax.axis_size("seq")
        turn = -1 if backward else 1
        self.place = count - 1 - me if backward else me
        self.has_prev = self.place > 0
        self.has_next = self.place < count - 1
        self.next = (lax.axis_index("dp"), jnp.clip(me + turn, 0, count - 1))
        self.prev = (lax.axis_index("dp"), jnp.clip(me - turn, 0, count - 1))

    def copy(self, k):
        return pltpu.make_async_remote_copy(
            src_ref=self.sent.at[k], dst_ref=self.landed.at[k], send_sem=self.send.at[k],
            recv_sem=self.recv.at[k], device_id=self.next, device_id_type=MESH,
        )

    def pass_on(self, k, decay, local):
        @pl.when(self.has_prev)
        def _():
            self.copy(k).wait_recv()

        @pl.when(jnp.logical_not(self.has_prev))
        def _():
            self.landed[k] = jnp.zeros_like(self.landed[k])

        @pl.when(self.has_next)
        def _():
            self.sent[k] = (decay() * self.landed[k].astype(f32) + local()).astype(bf16)
            self.copy(k).start()

    def drain(self):
        @pl.when(self.has_next)
        def _():
            for k in range(self.sent.shape[0]):
                self.copy(k).wait_send()

    @staticmethod
    def scratch(count, n, size):
        return [
            pltpu.VMEM((count, n, size), bf16),
            pltpu.VMEM((count, n, size), bf16),
            pltpu.SemaphoreType.DMA((count,)),
            pltpu.SemaphoreType.DMA((count,)),
        ]


def greet_all(place, chain):
    barrier = pltpu.get_barrier_semaphore()
    flags = [chain.has_prev, chain.has_next]
    devices = [chain.prev, chain.next]
    total = chain.has_prev.astype(jnp.int32) + chain.has_next.astype(jnp.int32)
    if place is not None:
        flags += [place.has_up, place.has_down]
        devices += [place.to_up, place.to_down]
        total = total + place.has_up.astype(jnp.int32) + place.has_down.astype(jnp.int32) + 3
        for device in (place.to_x, place.to_y, place.to_core):
            pl.semaphore_signal(barrier, inc=1, device_id=device, device_id_type=MESH)
    for flag, device in zip(flags, devices):

        @pl.when(flag)
        def _(device=device):
            pl.semaphore_signal(barrier, inc=1, device_id=device, device_id_type=MESH)

    pl.semaphore_wait(barrier, total)


def front_kernel(span, hw, groups, splits, parts, hooks, *refs):
    count = len(splits)
    (x_ref, w_ref, cw_ref, cb_ref, keys_ref, col_ref, row_ref, skip_ref) = refs[:8]
    shards = refs[8 : 8 + count]
    rows_ref, cin_ref, y_ref, carried_ref = refs[8 + count : 12 + count]
    fulls = refs[12 + count : 12 + 2 * count]
    rest = refs[12 + 2 * count :]
    values, local, scores = rest[:3]
    chain = Chain(False, *rest[3:7])
    batch = rows_ref.shape[0]
    n = keys_ref.shape[2] // 2
    ext = span + HALO
    i = pl.program_id(0)
    last_decay = rest[-1]
    place = Place() if count else None
    plans = [
        gather_steps(place, part_of(shards[j], parts[j]), fulls[j], splits[j], *rest[7 + 3 * j : 10 + 3 * j])
        for j in range(count)
    ]
    low_half = lax.broadcasted_iota(jnp.int32, (span, 2 * hw), 1) < hw

    @pl.when(i == 0)
    def _():
        greet_all(place, chain)

    def hook(b):
        for slot, plan in zip(hooks, zip(*plans)):
            if slot % batch == b:

                @pl.when(i == slot // batch)
                def _(plan=plan):
                    for one in plan:
                        one()

    def ready(j):
        for b in range(batch):
            k = j * batch + b
            chain.pass_on(k, lambda: last_decay[k], lambda: local[k])

    def values_part(b, acc):
        a = acc[b * ext : (b + 1) * ext]
        row, _ = silu_parts(conv_pre(a, cw_ref[...], cb_ref[...], span))
        row = row.astype(bf16)
        rows_ref[b] = row
        values[i * batch + b] = row
        cin_ref[b] = a.astype(bf16)
        cols = col_ref[0, b]
        c, step = cols[:, :HEADS], cols[:, HEADS:]
        weight = jnp.exp2(c[span - 1 : span] - c) * step
        vw = (row.astype(f32) * spread(weight, hw)).astype(bf16)
        local[i * batch + b] = mm_tn(keys_ref[b, :, :n], vw)
        last_decay[i * batch + b] = spread(jnp.exp2(c[span - 1 : span]), hw)

    def rows_part(b):
        g = i - groups
        at = g * batch + b
        k_in, k_out = keys_ref[b, :, :n], keys_ref[b, :, n:]

        @pl.when(g == 0)
        def _():
            scores[b] = jnp.where(causal(span, False), mm_nt(k_out, k_in), 0.0)

        cols = col_ref[0, b]
        c, step = cols[:, :HEADS], cols[:, HEADS:]
        v = values[at].astype(f32)
        vs = (v * spread(step, hw)).astype(bf16)
        s = scores[b]
        rows = row_ref[0, b]
        parts_y = []
        for p in range(HEADS // 2):
            pair = vs[:, p * 2 * hw : (p + 1) * 2 * hw]
            total = None
            for q in range(2):
                h = 2 * p + q
                gap = jnp.minimum(c[:, h : h + 1] - rows[h : h + 1, :], 0.0)
                u = (jnp.exp2(gap) * s).astype(bf16)
                keep = low_half if q == 0 else jnp.logical_not(low_half)
                term = mm(u, jnp.where(keep, pair, jnp.zeros_like(pair)))
                total = term if total is None else total + term
            parts_y.append(total)
        inside = jnp.concatenate(parts_y, axis=1)
        came = chain.landed[at]
        carried_ref[b] = came
        y_ref[b] = inside + mm(k_out, came) * spread(jnp.exp2(c), hw) + skip_ref[...] * v

    @pl.when(i < groups)
    def _():
        acc = mm(x_ref[...], w_ref[...])
        for b in range(batch):
            hook(b)
            values_part(b, acc)

    @pl.when(i >= groups)
    def _():
        for b in range(batch):
            hook(b)
            rows_part(b)

    early = i - chain.place

    @pl.when(jnp.logical_and(jnp.logical_and(early >= 0, early < groups), i <= groups - 1 + early))
    def _():
        ready(early)

    late = i - (groups - 1)

    @pl.when(jnp.logical_and(jnp.logical_and(late >= 0, late < groups), chain.place > groups - 1))
    def _():
        ready(late)

    @pl.when(i == 2 * groups - 1)
    def _():
        chain.drain()


def front(x2, w_conv, cw, cb, keys, colpack, rowpack, skip, shards, parts, splits, hooks, hw, span, collective_id):
    batch = keys.shape[0]
    groups = colpack.shape[0]
    cb_w = HEADS * hw
    ext = span + HALO
    inner = groups * cb_w
    n = keys.shape[2] // 2
    first = lambda i: jnp.minimum(i, groups - 1)
    then = lambda i: jnp.maximum(i - groups, 0)
    group = lambda i: i % groups
    hbm = pl.BlockSpec(memory_space=pl.ANY)
    count = len(shards)
    return pl.pallas_call(
        functools.partial(front_kernel, span, hw, groups, splits, parts, hooks),
        grid=(2 * groups,),
        in_specs=[
            pl.BlockSpec(x2.shape, lambda i: (0, 0)),
            pl.BlockSpec((w_conv.shape[0], cb_w), lambda i: (0, first(i))),
            pl.BlockSpec((cw.shape[0], cb_w), lambda i: (0, first(i))),
            pl.BlockSpec((1, cb_w), lambda i: (0, first(i))),
            pl.BlockSpec(keys.shape, lambda i: (0, 0, 0)),
            pl.BlockSpec((1,) + colpack.shape[1:], lambda i: (group(i), 0, 0, 0)),
            pl.BlockSpec((1,) + rowpack.shape[1:], lambda i: (group(i), 0, 0, 0)),
            pl.BlockSpec((1, cb_w), lambda i: (0, then(i))),
        ]
        + [hbm] * count,
        out_specs=[
            pl.BlockSpec((batch, span, cb_w), lambda i: (0, 0, first(i))),
            pl.BlockSpec((batch, ext, cb_w), lambda i: (0, 0, first(i))),
            pl.BlockSpec((batch, span, cb_w), lambda i: (0, 0, then(i))),
            pl.BlockSpec((batch, n, cb_w), lambda i: (0, 0, then(i))),
        ]
        + [hbm] * count,
        out_shape=[
            jax.ShapeDtypeStruct((batch, span, inner), bf16),
            jax.ShapeDtypeStruct((batch, ext, inner), bf16),
            jax.ShapeDtypeStruct((batch, span, inner), f32),
            jax.ShapeDtypeStruct((batch, n, inner), bf16),
        ]
        + [jax.ShapeDtypeStruct((s.shape[0] * 32, p[1]), s.dtype) for s, p in zip(shards, parts)],
        scratch_shapes=[
            pltpu.VMEM((groups * batch, span, cb_w), bf16),
            pltpu.VMEM((groups * batch, n, cb_w), f32),
            pltpu.VMEM((batch, span, span), f32),
        ]
        + Chain.scratch(groups * batch, n, cb_w)
        + gather_scratch() * count
        + [pltpu.VMEM((groups * batch, 1, cb_w), f32)],
        compiler_params=pltpu.CompilerParams(
            collective_id=collective_id, has_side_effects=True, vmem_limit_bytes=58 * 1024 * 1024
        ),
    )(x2, w_conv, cw, cb, keys, colpack, rowpack, skip, *shards)


def norm_kernel(span, x_ref, w_ref, y_ref, gain_ref, gate_ref, no_ref, rg_ref, gated, squares):
    g = pl.program_id(0)
    groups = pl.num_programs(0)
    batch = x_ref.shape[0]
    cb_w = w_ref.shape[1]

    @pl.when(g == 0)
    def _():
        squares[...] = jnp.zeros_like(squares)

    for b in range(batch):
        gate = mm(x_ref[b, HALO:], w_ref[...])
        gate_ref[b] = gate.astype(bf16)
        act, _ = silu_parts(gate)
        gr = y_ref[b] * act
        gated[g, b] = gr
        squares[b] += sum([gr[:, i * 128 : (i + 1) * 128] * gr[:, i * 128 : (i + 1) * 128] for i in range(cb_w // 128)])

    @pl.when(g == groups - 1)
    def _():
        for b in range(batch):
            total = jnp.sum(squares[b], axis=1, keepdims=True)
            rg = lax.rsqrt(total * (1.0 / (no_ref.shape[2])) + epsilon)
            rg_ref[b] = jnp.broadcast_to(rg, rg_ref.shape[1:])
            for i in range(no_ref.shape[2] // cb_w):
                part = slice(i * cb_w, (i + 1) * cb_w)
                no_ref[b, :, part] = (gated[i, b] * rg * gain_ref[:, part]).astype(bf16)


def gated_norm(x_ext, w_gate, y, gain, span, cb_w):
    batch, ext, width = x_ext.shape
    inner = y.shape[2]
    groups = inner // cb_w
    block = pl.BlockSpec((batch, span, cb_w), lambda g: (0, 0, g))
    return pl.pallas_call(
        functools.partial(norm_kernel, span),
        grid=(groups,),
        in_specs=[
            pl.BlockSpec((batch, ext, width), lambda g: (0, 0, 0)),
            pl.BlockSpec((width, cb_w), lambda g: (0, g)),
            block,
            pl.BlockSpec((1, inner), lambda g: (0, 0)),
        ],
        out_specs=[
            block,
            pl.BlockSpec((batch, span, inner), lambda g: (0, 0, 0)),
            pl.BlockSpec((batch, span, 8), lambda g: (0, 0, 0)),
        ],
        out_shape=[
            jax.ShapeDtypeStruct((batch, span, inner), bf16),
            jax.ShapeDtypeStruct((batch, span, inner), bf16),
            jax.ShapeDtypeStruct((batch, span, 8), f32),
        ],
        scratch_shapes=[
            pltpu.VMEM((groups, batch, span, cb_w), f32),
            pltpu.VMEM((batch, span, 128), f32),
        ],
        compiler_params=params_of(56),
    )(x_ext, w_gate, y, gain)


def scatter_beside(i, batch, slots, starts, splits, bigs, outs, scratch):
    if not splits:
        return lambda b: None
    place = Place()
    plans = [
        Scatter(place, bigs[j], outs[j], *scratch[7 * j : 7 * j + 7], splits[j]).steps()
        for j in range(len(splits))
    ]
    at = {}
    for steps in zip(*plans):
        for time, step in steps:
            slot = min([k for k in range(slots) if starts(k) >= time] + [slots - 1])
            at.setdefault(slot, []).append(step)

    def run(b):
        for slot, steps in at.items():
            if slot % batch == b:

                @pl.when(i == slot // batch)
                def _(steps=steps):
                    for step in steps:
                        step()

    return run


def gate_back_kernel(span, hw, groups, splits, *refs):
    count = len(splits)
    (mg_ref, w_ref, y_ref, gate_ref, norm_ref, gain_ref, v_ref, keys_ref, col_ref, row_ref) = refs[:10]
    h_ref, skip_ref = refs[10:12]
    bigs = refs[12 : 12 + count]
    (dgate_ref, dv_ref, later_ref, cols_ref, dq_ref, dk_ref, dgain_ref, dskip_ref) = refs[12 + count : 20 + count]
    outs = refs[20 + count : 20 + 2 * count]
    rest = refs[20 + 2 * count :]
    scores, dscores, dqacc, gbs, rises, local, decays = rest[:7]
    chain = Chain(True, *rest[7:11])
    batch = mg_ref.shape[0]
    blocks = groups * batch
    i = pl.program_id(0)
    g = i % groups
    n = keys_ref.shape[2] // 2
    skip = skip_ref[...]
    low_half = lax.broadcasted_iota(jnp.int32, (span, 2 * hw), 1) < hw

    @pl.when(i == 0)
    def _():
        greet_all(Place() if count else None, chain)

    hook = scatter_beside(i, batch, 2 * blocks, lambda k: gate_start(k, blocks), splits, bigs, outs, rest[11:])

    def gate_part(b):
        at = g * batch + b
        cols = col_ref[0, b]
        c = cols[:, :HEADS]
        no_grad = mm_nt(mg_ref[b], w_ref[...])
        gate = gate_ref[b].astype(f32)
        y = y_ref[b]
        rg = norm_ref[b][:, 0:1]
        mean = norm_ref[b][:, 1:2]
        act, sg = silu_parts(gate)
        gn = y * act * rg
        dgain = jnp.sum(no_grad * gn, axis=0, keepdims=True)
        dg = rg * (no_grad * gain_ref[...] - gn * mean)
        dgate_ref[b] = (dg * y * (sg * (1.0 + gate * (1.0 - sg)))).astype(bf16)
        gb = (dg * act).astype(bf16)
        gbs[at] = gb
        gf = gb.astype(f32)
        v = v_ref[b].astype(f32)
        dskip = jnp.sum(gf * v, axis=0, keepdims=True)
        rises[at] = gather_heads(gf * (y - skip * v), hw)
        ge = (gf * spread(jnp.exp2(c), hw)).astype(bf16)
        local[at] = mm_tn(keys_ref[b, :, n:], ge)
        decays[at] = spread(jnp.exp2(c[span - 1 : span]), hw)
        part = mm_nt(ge, h_ref[b])

        @pl.when(g == 0)
        def _():
            dqacc[b] = part

        @pl.when(g != 0)
        def _():
            dqacc[b] += part

        if b == 0:
            dgain_ref[...] = dgain
            dskip_ref[...] = dskip
        else:
            dgain_ref[...] += dgain
            dskip_ref[...] += dskip

    def block_part(b):
        at = g * batch + b
        cols = col_ref[0, b]
        c, step = cols[:, :HEADS], cols[:, HEADS:]
        k_in, k_out = keys_ref[b, :, :n], keys_ref[b, :, n:]

        @pl.when(g == 0)
        def _():
            scores[b] = jnp.where(causal(span, True), mm_nt(k_in, k_out), 0.0)
            dscores[b] = jnp.zeros_like(dscores[b])

        later_ref[b] = chain.landed[at]
        gb = gbs[at]
        gf = gb.astype(f32)
        v = v_ref[b].astype(f32)
        step_wide = spread(step, hw)
        vs = (v * step_wide).astype(bf16)
        rows = row_ref[0, b]
        s = scores[b]
        parts = []
        ds = dscores[b]
        for p in range(HEADS // 2):
            lanes = slice(p * 2 * hw, (p + 1) * 2 * hw)
            total = None
            for q in range(2):
                h = 2 * p + q
                gap = jnp.minimum(rows[h : h + 1, :] - c[:, h : h + 1], 0.0)
                decay = jnp.exp2(gap)
                u = (decay * s).astype(bf16)
                keep = low_half if q == 0 else jnp.logical_not(low_half)
                half = jnp.where(keep, gb[:, lanes], jnp.zeros_like(gb[:, lanes]))
                term = mm(u, half)
                total = term if total is None else total + term
                ds = ds + decay * mm_nt(vs[:, lanes], half)
            parts.append(total)
        dscores[b] = ds
        u_all = jnp.concatenate(parts, axis=1)
        dv_ref[b] = (u_all * step_wide + skip * gf).astype(bf16)
        fall = gather_heads(vs.astype(f32) * u_all, hw)
        direct = gather_heads(v * u_all, hw)
        cols_ref[0, b] = jnp.concatenate([rises[at] - fall, direct], axis=1)

        @pl.when(g == groups - 1)
        def _():
            low = jnp.where(causal(span, True), dscores[b], 0.0).astype(bf16)
            dq_ref[b] = dqacc[b] + mm_tn(low, k_in)
            dk_ref[b] = mm(low, k_out)

    lag = jnp.minimum(3 * chain.place, blocks - 1)
    for b in range(batch):
        hook(b)

        @pl.when(i < groups)
        def _():
            gate_part(b)

        @pl.when(i >= groups)
        def _():
            block_part(b)

        k = i * batch + b - lag

        @pl.when(jnp.logical_and(k >= 0, k < blocks))
        def _():
            chain.pass_on(k, lambda: decays[k], lambda: local[k])

    @pl.when(i == 2 * groups - 1)
    def _():
        chain.drain()


def gate_backward(
    mg, w_out, y, gate, norms, gain, v, keys, colpack, rowpack, carried, skip, bigs, splits, hw, span,
    collective_id,
):
    hbm = pl.BlockSpec(memory_space=pl.ANY)
    shapes = [(x.shape[0] // 32, x.shape[1]) for x in bigs]
    batch, _, width = mg.shape
    groups = colpack.shape[0]
    cb_w = HEADS * hw
    inner = groups * cb_w
    n = keys.shape[2] // 2
    blocks = groups * batch
    first = lambda i: jnp.minimum(i, groups - 1)
    then = lambda i: jnp.maximum(i - groups, 0)
    both = lambda i: i % groups
    block = lambda f, rows: pl.BlockSpec((batch, rows, cb_w), lambda i: (0, 0, f(i)))
    lanes = lambda f: pl.BlockSpec((1, cb_w), lambda i: (0, f(i)))
    whole = lambda shape: pl.BlockSpec(shape, lambda i: (0,) * len(shape))
    return pl.pallas_call(
        functools.partial(gate_back_kernel, span, hw, groups, splits),
        grid=(2 * groups,),
        in_specs=[
            whole(mg.shape),
            pl.BlockSpec((cb_w, width), lambda i: (first(i), 0)),
            block(first, span),
            block(first, span),
            whole(norms.shape),
            lanes(first),
            block(both, span),
            whole(keys.shape),
            pl.BlockSpec((1,) + colpack.shape[1:], lambda i: (both(i), 0, 0, 0)),
            pl.BlockSpec((1,) + rowpack.shape[1:], lambda i: (then(i), 0, 0, 0)),
            block(first, n),
            lanes(both),
        ]
        + [hbm] * len(bigs),
        out_specs=[
            block(first, span),
            block(then, span),
            block(then, n),
            pl.BlockSpec((1, batch, span, 2 * HEADS), lambda i: (then(i), 0, 0, 0)),
            whole((batch, span, n)),
            whole((batch, span, n)),
            lanes(first),
            lanes(first),
        ]
        + [whole(s) for s in shapes],
        out_shape=[
            jax.ShapeDtypeStruct((batch, span, inner), bf16),
            jax.ShapeDtypeStruct((batch, span, inner), bf16),
            jax.ShapeDtypeStruct((batch, n, inner), bf16),
            jax.ShapeDtypeStruct((groups, batch, span, 2 * HEADS), f32),
            jax.ShapeDtypeStruct((batch, span, n), f32),
            jax.ShapeDtypeStruct((batch, span, n), f32),
            jax.ShapeDtypeStruct((1, inner), f32),
            jax.ShapeDtypeStruct((1, inner), f32),
        ]
        + [jax.ShapeDtypeStruct(s, f32) for s in shapes],
        scratch_shapes=[
            pltpu.VMEM((batch, span, span), f32),
            pltpu.VMEM((batch, span, span), f32),
            pltpu.VMEM((batch, span, n), f32),
            pltpu.VMEM((blocks, span, cb_w), bf16),
            pltpu.VMEM((blocks, span, HEADS), f32),
            pltpu.VMEM((blocks, n, cb_w), f32),
            pltpu.VMEM((blocks, 1, cb_w), f32),
        ]
        + Chain.scratch(blocks, n, cb_w)
        + sum([Scatter.scratch(s[0], s[1], sp) for s, sp in zip(shapes, splits)], []),
        compiler_params=pltpu.CompilerParams(
            collective_id=collective_id, has_side_effects=True, vmem_limit_bytes=60 * 1024 * 1024
        ),
    )(mg, w_out, y, gate, norms, gain, v, keys, colpack, rowpack, carried, skip, *bigs)


def conv_back(dv, a, cw, cb, span, padded, out_ref, b):
    taps = cw.shape[0]
    first = HALO - (taps - 1)
    pre = conv_pre(a, cw, cb, span)
    _, sg = silu_parts(pre)
    pg = dv * (sg * (1.0 + pre * (1.0 - sg)))
    padded[16 : 16 + span] = pg
    ext = span + HALO
    total = jnp.zeros((ext, cw.shape[1]), f32)
    for k in range(taps):
        total = total + cw[k : k + 1] * padded[taps - 1 - k : taps - 1 - k + ext]
    out_ref[b] = total.astype(bf16)
    dcw = jnp.concatenate(
        [jnp.sum(pg * a[first + k : first + k + span], axis=0, keepdims=True) for k in range(taps)], axis=0
    )
    return dcw, jnp.sum(pg, axis=0, keepdims=True)


def back_kernel(span, hw, groups, splits, *refs):
    count = len(splits)
    (later_ref, h_ref, keys_ref, v_ref, dv_ref, col_ref, cin_ref, cw_ref, cb_ref) = refs[:9]
    bigs = refs[9 : 9 + count]
    cig_ref, cols_ref, dk_ref, dcw_ref, dcb_ref, dlast_ref = refs[9 + count : 15 + count]
    outs = refs[15 + count : 15 + 2 * count]
    rest = refs[15 + 2 * count :]
    padded, dkacc = rest[:2]
    i = pl.program_id(0)
    batch = dk_ref.shape[0]
    n = keys_ref.shape[2] // 2

    @pl.when(i == 0)
    def _():
        if count:
            Place().greet()
        padded[0:16] = jnp.zeros((16, padded.shape[1]), f32)
        padded[16 + span :] = jnp.zeros((padded.shape[0] - 16 - span, padded.shape[1]), f32)

    hook = scatter_beside(i, batch, groups * batch, back_start, splits, bigs, outs, rest[2:])
    for b in range(batch):
        hook(b)
        cols = col_ref[0, b]
        c, step = cols[:, :HEADS], cols[:, HEADS:]
        low = later_ref[b]
        left = spread(jnp.exp2(c[span - 1 : span] - c), hw)
        kdh = mm(keys_ref[b, :, :n], low) * left
        v = v_ref[b].astype(f32)
        step_wide = spread(step, hw)
        cols_ref[0, b] = gather_heads(v * kdh, hw)
        dlast_ref[b] = jnp.broadcast_to(
            jnp.sum(low.astype(f32) * h_ref[b].astype(f32), axis=0, keepdims=True), dlast_ref.shape[1:]
        )
        vw = (v * step_wide * left).astype(bf16)
        part = mm_nt(vw, low)

        @pl.when(i == 0)
        def _():
            dkacc[b] = part

        @pl.when(i != 0)
        def _():
            dkacc[b] += part

        @pl.when(i == groups - 1)
        def _():
            dk_ref[b] = dkacc[b]

        dv = dv_ref[b].astype(f32) + kdh * step_wide
        dcw, dcb = conv_back(dv, cin_ref[b].astype(f32), cw_ref[...], cb_ref[...], span, padded, cig_ref, b)
        if b == 0:
            dcw_ref[...] = dcw
            dcb_ref[...] = dcb
        else:
            dcw_ref[...] += dcw
            dcb_ref[...] += dcb


def back(later, carried, keys, v, dv, colpack, cin, cw, cb, bigs, splits, hw, span, collective_id):
    batch = v.shape[0]
    groups = colpack.shape[0]
    cb_w = HEADS * hw
    inner = groups * cb_w
    n = keys.shape[2] // 2
    ext = span + HALO
    taps = cw.shape[0]
    block = lambda rows: pl.BlockSpec((batch, rows, cb_w), lambda i: (0, 0, i))
    lanes = lambda rows: pl.BlockSpec((rows, cb_w), lambda i: (0, i))
    hbm = pl.BlockSpec(memory_space=pl.ANY)
    shapes = [(x.shape[0] // 32, x.shape[1]) for x in bigs]
    return pl.pallas_call(
        functools.partial(back_kernel, span, hw, groups, splits),
        grid=(groups,),
        in_specs=[
            block(n),
            block(n),
            pl.BlockSpec(keys.shape, lambda i: (0, 0, 0)),
            block(span),
            block(span),
            pl.BlockSpec((1,) + colpack.shape[1:], lambda i: (i, 0, 0, 0)),
            block(ext),
            lanes(taps),
            lanes(1),
        ]
        + [hbm] * len(bigs),
        out_specs=[
            block(ext),
            pl.BlockSpec((1, batch, span, HEADS), lambda i: (i, 0, 0, 0)),
            pl.BlockSpec((batch, span, n), lambda i: (0, 0, 0)),
            lanes(taps),
            lanes(1),
            block(8),
        ]
        + [pl.BlockSpec(s, lambda i: (0, 0)) for s in shapes],
        out_shape=[
            jax.ShapeDtypeStruct((batch, ext, inner), bf16),
            jax.ShapeDtypeStruct((groups, batch, span, HEADS), f32),
            jax.ShapeDtypeStruct((batch, span, n), f32),
            jax.ShapeDtypeStruct((taps, inner), f32),
            jax.ShapeDtypeStruct((1, inner), f32),
            jax.ShapeDtypeStruct((batch, 8, inner), f32),
        ]
        + [jax.ShapeDtypeStruct(s, f32) for s in shapes],
        scratch_shapes=[
            pltpu.VMEM((span + 32, cb_w), f32),
            pltpu.VMEM((batch, span, n), f32),
        ]
        + sum([Scatter.scratch(s[0], s[1], sp) for s, sp in zip(shapes, splits)], []),
        compiler_params=pltpu.CompilerParams(
            collective_id=collective_id if bigs else None,
            has_side_effects=bool(bigs),
            vmem_limit_bytes=58 * 1024 * 1024,
        ),
    )(later, carried, keys, v, dv, colpack, cin, cw, cb, *bigs)


def keys_back_kernel(span, dk_ref, dk2_ref, dq_ref, cin_ref, cw_ref, cb_ref, cig_ref, dcw_ref, dcb_ref, padded):
    batch = dk_ref.shape[0]
    padded[...] = jnp.zeros_like(padded)
    for b in range(batch):
        dv = jnp.concatenate([dk_ref[b] + dk2_ref[b], dq_ref[b]], axis=1)
        dcw, dcb = conv_back(dv, cin_ref[b].astype(f32), cw_ref[...], cb_ref[...], span, padded, cig_ref, b)
        if b == 0:
            dcw_ref[...] = dcw
            dcb_ref[...] = dcb
        else:
            dcw_ref[...] += dcw
            dcb_ref[...] += dcb


def keys_backward(dk, dk2, dq, cin, cw, cb, span):
    batch, ext, width = cin.shape
    return pl.pallas_call(
        functools.partial(keys_back_kernel, span),
        in_specs=[pl.BlockSpec(memory_space=pltpu.VMEM)] * 6,
        out_specs=[pl.BlockSpec(memory_space=pltpu.VMEM)] * 3,
        out_shape=[
            jax.ShapeDtypeStruct(cin.shape, bf16),
            jax.ShapeDtypeStruct(cw.shape, f32),
            jax.ShapeDtypeStruct(cb.shape, f32),
        ],
        scratch_shapes=[pltpu.VMEM((span + 32, width), f32)],
        compiler_params=params_of(40),
    )(dk, dk2, dq, cin, cw, cb)


def own_kernels():
    return lax.axis_size("dp") == 4 and lax.axis_size("seq") == 8


def gather_rows(shards, parts, splits, collective_id):
    if own_kernels():
        return gather(shards, parts, splits, collective_id)
    return [
        lax.all_gather(s[:, p[0] : p[0] + p[1]], ("dp", "seq"), axis=0, tiled=True)
        for s, p in zip(shards, parts)
    ]


def scatter_rows(bigs, splits, small, collective_id):
    if own_kernels():
        return scatter(bigs, splits, small, collective_id)
    outs = [lax.psum_scatter(b, ("dp", "seq"), scatter_dimension=0, tiled=True).astype(f32) for b in bigs]
    return outs + ([] if small is None else [lax.psum(small, ("dp", "seq"))])


def half_of(width):
    return (width // 2 + 127) // 128 * 128


def ungrouped(cols):
    groups, batch, span, each = cols.shape
    return jnp.transpose(cols, (1, 2, 0, 3)).reshape(batch, span, groups * each)


FRONT_HOOKS = (0, 6, 7, 13, 14, 20, 22, 24, 31, 33, 35, 35, 35)


def gate_start(k, blocks):
    return 1.0 * k if k < blocks else 1.0 * blocks + 1.6 * (k - blocks)


def back_start(k):
    return 2.9 * k


def on_device(
    resid_in, out_grad, lengths, norm_gain, in_proj, dt_proj, conv_weight, conv_bias, dt_bias, a_log,
    skip_scale, gate_gain, out_proj,
):
    batch, span, width = resid_in.shape
    inner = gate_gain.shape[0]
    heads = a_log.shape[0]
    hw = inner // heads
    n = (in_proj.shape[1] - 2 * inner) // 2
    cb_w = HEADS * hw
    positions = lax.axis_index("seq") * span + lax.iota(jnp.int32, span)
    mask = (positions[None, :] < lengths[:, None]).astype(f32)[..., None]

    conv_cols = in_proj.shape[1] - inner
    dt_pad = (-(conv_cols + heads)) % 128
    conv_all = conv_cols + heads + dt_pad
    dt_shard = jnp.pad(dt_proj, ((0, 0), (0, dt_pad)))
    later_shards, later_parts = [in_proj, out_proj], [(0, inner), (0, width)]
    later_splits = [half_of(inner), half_of(width)]
    full_conv, full_dt = gather_rows(
        [in_proj, dt_shard], [(inner, conv_cols), (0, heads + dt_pad)], [half_of(conv_cols), heads + dt_pad], 3
    )

    halo = shifted(resid_in[:, span - HALO :], "seq", 1)
    resid_ext = jnp.concatenate([halo, resid_in], axis=1).astype(f32)
    rs_ext = lax.rsqrt(jnp.mean(resid_ext * resid_ext, axis=-1, keepdims=True) + epsilon)
    x_ext = (resid_ext * rs_ext * norm_gain).astype(bf16)
    ext = span + HALO
    x2 = x_ext.reshape(batch * ext, width)
    resid_wide = resid_in.astype(f32)
    rs = rs_ext[:, HALO:]

    rate = -jnp.exp(a_log)
    lane_pad = (0, (-heads) % 128)
    skip_wide = jnp.repeat(skip_scale, hw)[None]
    gain_wide = gate_gain[None]
    cw_keys, cb_keys = conv_weight[:, inner:], conv_bias[None, inner:]
    cw_vals, cb_vals = conv_weight[:, :inner], conv_bias[None, :inner]
    keys, cin_keys, colpack, rowpack, raw, step = prepare(
        x2, full_conv, inner // (2 * n), full_dt, cw_keys, cb_keys,
        jnp.pad(dt_bias, lane_pad)[None], jnp.pad(rate, lane_pad)[None], batch, span, heads,
    )
    inside = own_kernels()
    made = front(
        x2, full_conv, cw_vals, cb_vals, keys, colpack, rowpack, skip_wide,
        later_shards if inside else [], later_parts, later_splits if inside else [], FRONT_HOOKS, hw, span, 1,
    )
    v, cin_vals, y, carried = made[:4]
    full_gate, full_out = made[4:] if inside else gather_rows(later_shards, later_parts, later_splits, 4)
    gate, normed_out, rg = gated_norm(x_ext, full_gate, y, gain_wide, span, cb_w)
    mixer_out = jnp.dot(normed_out, full_out, preferred_element_type=f32)
    output = (mask * (resid_wide + mixer_out)).astype(bf16)

    mixer_grad = (mask * out_grad.astype(f32)).astype(bf16)
    mean = jnp.sum(mixer_grad.astype(f32) * mixer_out, axis=-1, keepdims=True) * (1.0 / inner)
    norms = jnp.concatenate([rg[..., :1], mean, jnp.zeros((batch, span, 6), f32)], axis=-1)
    grad_out = jnp.einsum("bsi,bsd->id", normed_out, mixer_grad, preferred_element_type=f32).astype(bf16)
    made = gate_backward(
        mixer_grad, full_out, y, gate, norms, gain_wide, v, keys, colpack, rowpack, carried, skip_wide,
        [grad_out] if inside else [], later_splits[1:] if inside else [], hw, span, 7,
    )
    dgate, dv, later, cols_one, dq, dk, dgain, dskip = made[:8]
    (sum_out,) = made[8:] if inside else scatter_rows([grad_out], later_splits[1:], None, 5)
    x_rows = x_ext[:, HALO:]
    grad_gate = jnp.einsum("bsd,bse->de", x_rows, dgate, preferred_element_type=f32).astype(bf16)
    made = back(
        later, carried, keys, v, dv, colpack, cin_vals, cw_vals, cb_vals,
        [grad_gate] if inside else [], later_splits[:1] if inside else [], hw, span, 2,
    )
    cig_vals, cols_two, dk2, dcw_vals, dcb_vals, dlast = made[:6]
    (sum_gate,) = made[6:] if inside else scatter_rows([grad_gate], later_splits[:1], None, 5)
    cig_keys, dcw_keys, dcb_keys = keys_backward(dk, dk2, dq, cin_keys, cw_keys, cb_keys, span)

    raw, step = raw[..., :heads], step[..., :heads]
    rise = ungrouped(cols_one[..., :HEADS])
    direct = ungrouped(cols_one[..., HEADS:])
    ahead = ungrouped(cols_two)
    moved = ahead * step
    tri = causal(span, False).astype(f32)
    block_decay = jnp.exp2(colpack[:, :, span - 1, :HEADS]).transpose(1, 0, 2).reshape(batch, heads)
    last = jnp.sum(moved, axis=1) + dlast[:, 0].reshape(batch, heads, hw).sum(-1) * block_decay
    dlog = rise - moved
    dlog = jnp.einsum("ts,bth->bsh", tri, dlog, precision=highest) + last[:, None, :]
    grad_a = jnp.sum(dlog * step, axis=(0, 1)) * rate
    step_grad = direct + ahead + dlog * rate
    dt_grad = step_grad * jax.nn.sigmoid(raw)
    grad_bias = jnp.sum(dt_grad, axis=(0, 1))
    step_low = jnp.pad(dt_grad.astype(bf16), ((0, 0), (HALO, 0), (0, dt_pad)))

    cig = jnp.concatenate([cig_vals, cig_keys, step_low], axis=-1)
    grad_conv = jnp.einsum("bsd,bse->de", x_ext, cig, preferred_element_type=f32).astype(bf16)
    normed_ext = jnp.einsum("bse,de->bsd", cig[..., :conv_cols], full_conv, preferred_element_type=f32)
    normed_ext = normed_ext + jnp.einsum("bse,de->bsd", step_low, full_dt, preferred_element_type=f32)
    from_next = shifted(normed_ext[:, :HALO].astype(bf16), "seq", -1).astype(f32)
    normed_grad = normed_ext[:, HALO:]
    normed_grad = jnp.concatenate([normed_grad[:, : span - HALO], normed_grad[:, span - HALO :] + from_next], axis=1)
    normed_grad = normed_grad + jnp.einsum("bse,de->bsd", dgate, full_gate, preferred_element_type=f32)
    nz = resid_wide * rs
    fg = normed_grad * norm_gain
    grad_norm = jnp.sum(normed_grad * nz, axis=(0, 1))
    input_grad = mixer_grad.astype(f32) + rs * (fg - nz * jnp.mean(fg * nz, axis=-1, keepdims=True))

    pieces = (
        grad_norm,
        jnp.concatenate([dcw_vals, dcw_keys], axis=1),
        jnp.concatenate([dcb_vals, dcb_keys], axis=1)[0],
        dgain[0],
        grad_bias,
        grad_a,
        dskip[0].reshape(heads, hw).sum(-1),
    )
    flat = jnp.concatenate([p.reshape(-1) for p in pieces])
    small = jnp.pad(flat, (0, (-flat.size) % 1024)).reshape(-1, 128)
    sum_conv, small = scatter_rows([grad_conv], [half_of(conv_all)], small, 6)
    flat, sums, at = small.reshape(-1), [], 0
    for p in pieces:
        sums.append(flat[at : at + p.size].reshape(p.shape))
        at += p.size
    sum_norm, sum_cw, sum_cb, sum_gain, sum_bias, sum_a, sum_skip = sums
    return (
        output,
        input_grad.astype(bf16),
        jnp.concatenate([sum_gate, sum_conv[:, :conv_cols]], axis=1),
        sum_conv[:, conv_cols : conv_cols + heads],
        sum_out,
        sum_norm,
        sum_cw,
        sum_cb,
        sum_bias,
        sum_a,
        sum_skip,
        sum_gain,
    )


def solution(mesh):
    rows = P("dp", "seq", None)
    shard = P(("dp", "seq"), None)
    return jax.shard_map(
        on_device,
        mesh=mesh,
        in_specs=(rows, rows, P("dp"), P(), shard, shard, P(), P(), P(), P(), P(), P(), shard),
        out_specs=(rows, rows, shard, shard, shard, P(), P(), P(), P(), P(), P(), P()),
        check_vma=False,
    )
```

time: 743 us -> 533 us (0.72)
  Pallas kernels: 548 us -> 374 us
  local copies, waits for them, and re-layouts: 83 us -> 38.9 us
    pallas_call x2 -> x1, Pallas kernels: 155 us -> 59.3 us  [scatter(): pl.pallas_call(functools.partial(scatter_kernel, splits, small is not Non...]
    pallas_call x9 -> x6, Pallas kernels: 391 us -> 313 us  [the longest x1 91.4 us: front(): pl.pallas_call(functools.partial(front_kernel, span, hw, groups, splits,...]
    unnamed x102 -> x50, local copies, waits for them, and re-layouts: 26.2 us -> 3.74 us
    concatenate x3 -> x0, local copies, waits for them, and re-layouts: 18.4 us -> none  [the longest x1 16 us: on_device(): jnp.concatenate([grad_conv, grad_dt, jnp.zeros((width, dt_pad), f32)], ax...]
    dot_general x5 -> x2, matrix products: 19.7 us -> 17.9 us  [the longest x1 14.4 us: on_device(): jnp.einsum('bse,de->bsd', cig[..., :conv_cols], full_conv, preferred_elem...]
  transfers between devices with their start and end apart: 2 -> 2, of which waited for: 0 -> 0; matrix products, arithmetic and copies ran while one was open for 4% -> 5% of each run, Pallas kernels for 30% -> 10%
where the time goes in v3:
time: 533 us; the launch traced here: 527 us
  Pallas kernels  374 us (70%)
  matrix products  86.9 us (16%)
  local copies, waits for them, and re-layouts  38.9 us (7%)
  other arithmetic  21.4 us (4%)
    pallas_call x1, Pallas kernels, front(): pl.pallas_call(functools.partial(front_kernel, span, hw, groups, splits,...  91.4 us
    pallas_call x1, Pallas kernels, gate_backward(): pl.pallas_call(functools.partial(gate_back_kernel, span, hw, groups, spli...  81.1 us
    pallas_call x1, Pallas kernels, back(): pl.pallas_call(functools.partial(back_kernel, span, hw, groups, splits),...  61.7 us
    pallas_call x1, Pallas kernels, scatter(): pl.pallas_call(functools.partial(scatter_kernel, splits, small is not Non...  59.3 us
    pallas_call x1, Pallas kernels, gather(): pl.pallas_call(functools.partial(gather_kernel, splits, parts), in_specs=...  54.9 us
    pallas_call x1, Pallas kernels, gated_norm(): pl.pallas_call(functools.partial(norm_kernel, span), grid=(groups,), in_s...  17.1 us
    dot_general x1, matrix products, on_device(): jnp.einsum('bse,de->bsd', dgate, full_gate, preferred_element_type=f32)  14.6 us
    dot_general x1, matrix products, on_device(): jnp.einsum('bsd,bse->de', x_ext, cig, preferred_element_type=f32)  14.5 us
  transfers between devices with their start and end apart: 2, of which 0 were waited for; matrix products, arithmetic and copies ran while one was open for 5% of the time, Pallas kernels for 10%

profile of v3, /device:TPU:0, one launch (start us, length us, event | category | flops | bytes accessed | tf_op | source)
XLA Modules:
  0.0 526.8 jit_solution(14161401155622933193)
XLA Ops:
  1.6 2.4 collective-permute-start
  12.2 54.9 %shard_map.220 = (bf16[1536,3328]{1,0:T(8,128)(2,1)}, bf16[1536,128]{1,0:T(8,128)(2,1)}) custom-call(bf16[48,6400]{1,0:T(8,128)(2,1)} %refs_8_.1, bf16[48,128]{1,0:T(8,128)(2,1)} %pad.19.refs_1_), custom_call_target="tpu_custom_call" | custom-call | tf_op jit(solution)/shard_map/pallas_call | solution.py:311
  67.8 2.2 multiply_reduce_fusion
  70.1 2.3 maximum_convert_fusion
  74.5 6.6 %shard_map.221 = (bf16[3,256,256]{2,1,0:T(8,128)(2,1)S(1)}, bf16[3,272,256]{2,1,0:T(8,128)(2,1)S(1)}, f32[6,3,256,16]{3,2,1,0:T(8,128)}, f32[6,3,8,256]{3,2,1,0:...) custom-call(bf16[816,1536]{1,0:T(8,128)(2,1)} %fusion.18.x_ref.refs_0_, ...), custom_call_target="tpu_custom_call" | custom-call | tf_op jit(solution)/shard_map/pallas_call | solution.py:656
  83.4 91.4 %shard_map.222 = (bf16[3,256,3072]{2,1,0:T(8,128)(2,1)}, bf16[3,272,3072]{2,1,0:T(8,128)(2,1)}, f32[3,256,3072]{2,1,0:T(8,128)}, bf16[3,128,3072]{2,1,0:T(8,128)...) custom-call(bf16[816,1536]{1,0:T(8,128)(2,1)} %fusion.18.x_ref.refs_0_, ...), custom_call_target="tpu_custom_call" | custom-call | tf_op jit(solution)/shard_map/pallas_call | solution.py:865
  174.9 2.1 multiply_convert_fusion.x_ref
  177.0 17.1 %shard_map.223 = (bf16[3,256,3072]{2,1,0:T(8,128)(2,1)}, bf16[3,256,3072]{2,1,0:T(8,128)(2,1)}, f32[3,256,8]{2,1,0:T(8,128)}) custom-call(bf16[3,272,1536]{2,1,0:T(8,128)(2,1)} %multiply_convert_fusion.x_ref, bf16[1536,3072]{1,0:T(8,128)(2,1)} %get-tuple-element.55.w_ref, f32[3,256,3072]{2,1,0:T(8,128)} %get-tuple-element.56.y_ref.refs_2_, f32[1,3072]{1,0:T(1,128)} %bitcast.89), custom_call_target="tpu_custom_call" | custom-call | tf_op jit(solution)/shard_map/pallas_call | solution.py:941
  194.1 13.9 %fusion.25 = (f32[3,256]{1,0:T(4,128)S(1)}, bf16[3,256,1536]{2,1,0:T(8,128)(2,1)}, bf16[3,256,1536]{2,1,0:T(8,128)(2,1)}) fusion(bf16[3,256,1536]{2,1,0:T(8,128)(2,1)} %param.14, f32[3,256]{1,0:T(4,128)S(1)} %compare_convert_fusion, bf16[3,256,1536]{2,1,0:T(8,128)(2,1)S(1)} %copy-done.6, bf16[3,256,3072]{2,1,0:T(8,128)(2,1)} %get-tuple-element.57, ...), kind=kOutput, calls=%fused_computation.35 | convolution fusion | flops 7259552768 | bytes 23599104 | tf_op jit(solution)/shard_map/dot_general | solution.py:1458
  208.2 12.5 %bitcast_convert_fusion.2.refs_12_ = bf16[3072,1536]{1,0:T(8,128)(2,1)} fusion(bf16[3,256,3072]{2,1,0:T(8,128)(2,1)} %get-tuple-element.57, bf16[3,256,1536]{2,1,0:T(8,128)(2,1)} %get-tuple-element.93.refs_0_), kind=kOutput, calls=%fused_computation.2 | convolution fusion | flops 7252475904 | bytes 16515072 | tf_op jit(solution)/shard_map/bsi,bsd->id/dot_general | solution.py:1464
  221.6 81.1 %shard_map.224 = (bf16[3,256,3072]{2,1,0:T(8,128)(2,1)}, bf16[3,256,3072]{2,1,0:T(8,128)(2,1)}, bf16[3,128,3072]{2,1,0:T(8,128)(2,1)}, f32[6,3,256,16]{3,2,1,0:T...) custom-call(bf16[3,256,1536]{2,1,0:T(8,128)(2,1)} %get-tuple-element, ...), custom_call_target="tpu_custom_call" | custom-call | tf_op jit(solution)/shard_map/pallas_call | solution.py:1147
  302.7 12.9 %bitcast_convert_fusion.1.refs_9_ = bf16[1536,3072]{1,0:T(8,128)(2,1)} fusion(bf16[3,256,3072]{2,1,0:T(8,128)(2,1)} %get-tuple-element.66, bf16[3,272,1536]{2,1,0:T(8,128)(2,1)} %multiply_convert_fusion.x_ref), kind=kOutput, calls=%fused_computation.1 | convolution fusion | flops 7252475904 | bytes 16515072 | tf_op jit(solution)/shard_map/bsd,bse->de/dot_general | solution.py:1472
  315.7 3.0 slice_bitcast_fusion
  318.7 2.3 copy.75
  321.0 61.7 %shard_map.225 = (bf16[3,272,3072]{2,1,0:T(8,128)(2,1)}, f32[6,3,256,8]{3,2,1,0:T(8,128)}, f32[3,256,128]{2,1,0:T(8,128)}, f32[4,3072]{1,0:T(4,128)}, f32[1,3072...) custom-call(bf16[3,128,3072]{2,1,0:T(8,128)(2,1)} %get-tuple-element.63.refs_0_, ...), custom_call_target="tpu_custom_call" | custom-call | tf_op jit(solution)/shard_map/pallas_call | solution.py:1292
  382.7 2.4 copy.76
  387.6 2.3 copy.77
  392.9 14.4 %fusion = f32[3,272,1536]{2,1,0:T(8,128)} fusion(bf16[1536,3328]{1,0:T(8,128)(2,1)} %get-tuple-element.50.wk_ref.refs_1_, bf16[3,272,256]{2,1,0:T(8,128)(2,1)S(1)} %get-tuple-element.72, bf16[3,272,3072]{2,1,0:T(8,128)(2,1)} %get-tuple-element.67), kind=kOutput, calls=%fused_computation.3 | convolution fusion | flops 8353333248 | bytes 20668416 | tf_op jit(solution)/shard_map/bse,de->bsd/dot_general | solution.py:1499
  408.0 3.6 convolution_add_fusion
  411.6 2.4 slice.125
  417.0 14.5 %bitcast_convert_fusion.refs_0_ = bf16[1536,3456]{1,0:T(8,128)(2,1)} fusion(bf16[3,272,1536]{2,1,0:T(8,128)(2,1)S(1)} %copy-done.9, bf16[3,272,128]{2,1,0:T(8,128)(2,1)S(1)} %pad.22, bf16[3,272,256]{2,1,0:T(8,128)(2,1)S(1)} %get-tuple-element.72, bf16[3,272,3072]{2,1,0:T(8,128)(2,1)S(1)} %bitcast.94), kind=kOutput, calls=%fused_computation | convolution fusion | flops 8685563904 | bytes 18763776 | tf_op jit(solution)/shard_map/bsd,bse->de/dot_general | solution.py:1498
  434.1 14.6 %fusion.22 = (f32[1536]{0:T(1024)S(1)}, f32[3,256]{1,0:T(4,128)S(1)}, f32[3,256,1536]{2,1,0:T(8,128)}) fusion(bf16[3,256,1536]{2,1,0:T(8,128)(2,1)} %param.13, f32[3,256]{1,0:T(4,128)S(1)} %slice_bitcast_fusion.5, f32[3,16,1536]{2,1,0:T(8,128)S(1)} %slice_add_fusion, f32[3,240,1536]{2,1,0:T(8,128)} %slice.125, f32[1536]{0:T(1024)S(1)} %copy-done.16, ...), kind=kOutput, calls=%fused_computation.32 | convolution fusion | flops 7258372096 | bytes 25970688 | tf_op jit(solution)/shard_map/bse,de->bsd/dot_general | solution.py:1504
  449.3 59.3 %shard_map.227 = (f32[48,3456]{1,0:T(8,128)}, f32[168,128]{1,0:T(8,128)}) custom-call(bf16[1536,3456]{1,0:T(8,128)(2,1)} %bitcast_convert_fusion.refs_0_, f32[168,128]{1,0:T(8,128)} %pad_bitcast_fusion.refs_1_), custom_call_target="tpu_custom_call" | custom-call | tf_op jit(solution)/shard_map/pallas_call | solution.py:603
  518.0 6.4 %fusion.26 = bf16[3,256,1536]{2,1,0:T(8,128)(2,1)} fusion(bf16[3,256,1536]{2,1,0:T(8,128)(2,1)S(1)} %copy-done.7, bf16[3,256,1536]{2,1,0:T(8,128)(2,1)} %get-tuple-element.93.refs_0_, f32[3,256]{1,0:T(4,128)S(1)} %broadcast_multiply_fusion, f32[1536]{0:T(1024)S(1)} %copy-done.16, f32[3,256]{1,0:T(4,128)S(1)} %slice_bitcast_fusion.5, ...), kind=kLoop, calls=%fused_computation.36 | loop fusion | flops 12976128 | bytes 16527360 | tf_op jit(solution)/shard_map/convert_element_type | solution.py:1529
  (112 shorter events, 38.9 us)
Async XLA Ops:
  1.6 66.2 %collective-permute-start = (bf16[3,16,1536]{2,1,0:T(8,128)(2,1)S(1)}, bf16[3,16,1536]{2,1,0:T(8,128)(2,1)S(1)}, u32[]{:S(2)}, u32[]{:S(2)}) collective-permute-start(bf16[3,16,1536]{2,1,0:T(8,128)(2,1)S(1)} %slice.94), channel_id=1, source_target_pairs={{0,1},{1,2},{2,3},{3,4},{4,5},{5,6},{6,7},{8,9},{9,10},{10,11},{11... | collective-permute-start | bytes 442376 | tf_op jit(solution)/shard_map/ppermute | solution.py:35
  67.8 4.7 copy-start.16
  72.5 2.0 copy-start.1
  83.4 91.5 %copy-start.6 = (bf16[3,256,1536]{2,1,0:T(8,128)(2,1)S(1)}, bf16[3,256,1536]{2,1,0:T(8,128)(2,1)}, u32[]{:S(2)}) copy-start(bf16[3,256,1536]{2,1,0:T(8,128)(2,1)} %param.13) | copy-start | bytes 7077892
  208.2 12.5 %copy-start.15 = (f32[3,256,8]{2,1,0:T(8,128)S(1)}, f32[3,256,8]{2,1,0:T(8,128)}, u32[]{:S(2)}) copy-start(f32[3,256,8]{2,1,0:T(8,128)} %get-tuple-element.60) | copy-start | bytes 73732
  302.7 12.9 %copy-start.10 = (f32[6,3,256,16]{3,2,1,0:T(8,128)S(1)}, f32[6,3,256,16]{3,2,1,0:T(8,128)}, u32[]{:S(2)}) copy-start(f32[6,3,256,16]{3,2,1,0:T(8,128)} %get-tuple-element.73) | copy-start | bytes 884740
  382.7 8.1 %copy-start.3 = (f32[3,256,128]{2,1,0:T(8,128)S(1)}, f32[3,256,128]{2,1,0:T(8,128)}, u32[]{:S(2)}) copy-start(f32[3,256,128]{2,1,0:T(8,128)} %get-tuple-element.70.dq_ref) | copy-start | bytes 1179652
  382.7 8.1 %copy-start.4 = (f32[3,256,128]{2,1,0:T(8,128)S(1)}, f32[3,256,128]{2,1,0:T(8,128)}, u32[]{:S(2)}) copy-start(f32[3,256,128]{2,1,0:T(8,128)} %get-tuple-element.68.dk_ref) | copy-start | bytes 1179652
  382.7 8.1 %copy-start.5 = (f32[3,256,128]{2,1,0:T(8,128)S(1)}, f32[3,256,128]{2,1,0:T(8,128)}, u32[]{:S(2)}) copy-start(f32[3,256,128]{2,1,0:T(8,128)} %get-tuple-element.69.dk2_ref) | copy-start | bytes 1179652
  392.9 14.5 %copy-start.13 = (f32[3,256,48]{2,1,0:T(8,128)S(1)}, f32[3,256,48]{2,1,0:T(8,128)}, u32[]{:S(2)}) copy-start(f32[3,256,48]{2,1,0:T(8,128)} %copy.83) | copy-start | bytes 442372
  392.9 14.5 %copy-start.14 = (f32[3,256,48]{2,1,0:T(8,128)S(1)}, f32[3,256,48]{2,1,0:T(8,128)}, u32[]{:S(2)}) copy-start(f32[3,256,48]{2,1,0:T(8,128)} %copy.79) | copy-start | bytes 442372
  407.3 9.7 %slice-start = ((s8[5013504]{0:T(1024)(128)(4,1)}), s8[4194304]{0:T(1024)(128)(4,1)S(1)}, s32[]{:S(2)}) async-start(s8[5013504]{0:T(1024)(128)(4,1)} %bitcast.93), calls=%async_computation | async-start | bytes 8388608
  408.0 9.0 %slice-start.1 = ((s8[5013504]{0:T(1024)(128)(4,1)}), s8[819200]{0:T(1024)(128)(4,1)S(1)}, s32[]{:S(2)}) async-start(s8[5013504]{0:T(1024)(128)(4,1)} %bitcast.93), calls=%async_computation.1 | async-start | bytes 1638400
  411.6 3.9 copy-start.8
  411.6 5.4 %copy-start.9 = (bf16[3,272,1536]{2,1,0:T(8,128)(2,1)S(1)}, bf16[3,272,1536]{2,1,0:T(8,128)(2,1)}, u32[]{:S(2)}) copy-start(bf16[3,272,1536]{2,1,0:T(8,128)(2,1)} %multiply_convert_fusion.x_ref) | copy-start | bytes 7520260
  415.6 16.0 %copy-start.17 = (f32[4,3072]{1,0:T(4,128)S(1)}, f32[4,3072]{1,0:T(4,128)}, u32[]{:S(2)}) copy-start(f32[4,3072]{1,0:T(4,128)} %get-tuple-element.79) | copy-start | bytes 147460
  415.6 16.5 %copy-start.18 = (f32[1,3072]{1,0:T(1,128)S(1)}, f32[1,3072]{1,0:T(1,128)}, u32[]{:S(2)}) copy-start(f32[1,3072]{1,0:T(1,128)} %get-tuple-element.84) | copy-start | bytes 36868
  415.6 17.4 %copy-start.19 = (f32[1,3072]{1,0:T(1,128)S(1)}, f32[1,3072]{1,0:T(1,128)}, u32[]{:S(2)}) copy-start(f32[1,3072]{1,0:T(1,128)} %get-tuple-element.81) | copy-start | bytes 36868
  415.6 17.4 %copy-start.21 = (f32[48]{0:T(128)S(1)}, f32[48]{0:T(128)}, u32[]{:S(2)}) copy-start(f32[48]{0:T(128)} %param.22) | copy-start | bytes 580
  415.6 17.5 %collective-permute-start.1 = (bf16[3,16,1536]{2,1,0:T(8,128)(2,1)S(1)}, bf16[3,16,1536]{2,1,0:T(8,128)(2,1)S(1)}, u32[]{:S(2)}, u32[]{:S(2)}) collective-permute-start(bf16[3,16,1536]{2,1,0:T(8,128)(2,1)S(1)} %slice.151), channel_id=1, source_target_pairs={{1,0},{2,1},{3,2},{4,3},{5,4},{6,5},{7,6},{9,8},{10,9},{11,10},{12... | collective-permute-start | bytes 442376 | tf_op jit(solution)/shard_map/ppermute | solution.py:35
  434.0 14.6 %copy-start.20 = (f32[1,3072]{1,0:T(1,128)S(1)}, f32[1,3072]{1,0:T(1,128)}, u32[]{:S(2)}) copy-start(f32[1,3072]{1,0:T(1,128)} %get-tuple-element.83) | copy-start | bytes 36868
  449.3 68.6 %copy-start.7 = (bf16[3,256,1536]{2,1,0:T(8,128)(2,1)S(1)}, bf16[3,256,1536]{2,1,0:T(8,128)(2,1)}, u32[]{:S(2)}) copy-start(bf16[3,256,1536]{2,1,0:T(8,128)(2,1)} %param.13) | copy-start | bytes 7077892
  518.0 6.4 %copy-start.12 = (f32[48,3072]{1,0:T(8,128)S(1)}, f32[48,3072]{1,0:T(8,128)}, u32[]{:S(2)}) copy-start(f32[48,3072]{1,0:T(8,128)} %get-tuple-element.78) | copy-start | bytes 1769476
  518.0 7.6 %copy-start.11 = (f32[96,1536]{1,0:T(8,128)S(1)}, f32[96,1536]{1,0:T(8,128)}, u32[]{:S(2)}) copy-start(f32[96,1536]{1,0:T(8,128)} %get-tuple-element.125) | copy-start | bytes 1769476
  (2 other events, 1.4 us)
